TPU v7x, 32 devices: a whole 2x2x4 slice. The times are simulated.
32 devices in a mesh: groups: 2 (over x), ctx: 8 (over z, y), head: 2 (over core).
Axes of the slice: x: 2, y: 2, z: 4, core: 2. Of those that a mesh axis runs over, the one named last changes fastest.
Arguments:
- sem_tokens: int32 [2048, 4], P(('groups', 'ctx')), parts along dimension 0, may hold values from 0 to 255
- cand_request: int32 [2048, 1], P(('groups', 'ctx')), parts along dimension 0, may hold values from 0 to 7; in each aligned block of 128 rows (0 to 127, 128 to 255, ...) at most 24 rows name the same one
- hist_lengths: int32 [16], P('groups'), parts along dimension 0, may hold values from 512 to 2048, as said below
- hist_buckets: int32 [16384], P(('groups', 'ctx')), parts along dimension 0, may hold values from 0 to 127
- hist_keys: bfloat16 [16384, 1024], P(('groups', 'ctx'), 'head'), parts along dimension 0, may hold values from -6 to 6
- hist_values: bfloat16 [16384, 1024], P(('groups', 'ctx'), 'head'), parts along dimension 0, may hold values from -18 to 18
- code_table: bfloat16 [1024, 1024], replicated, may hold values from -3 to 3
- proj_in: bfloat16 [1024, 4, 1024], P(None, None, 'head'), may hold values from -0.1875 to 0.1875
- time_bias: float32 [128, 16], P(None, 'head'), may hold values from -6 to 6
- proj_out: bfloat16 [1024, 1024], P('head'), may hold values from -0.1875 to 0.1875
Outputs:
- verified: bfloat16 [2048, 1024], P(('groups', 'ctx'), 'head'), parts along dimension 0
There are 2 independent parts, one for each index of `groups`. A program takes and returns all parts, laid end to end along the dimension named above; an argument that names none is the same for every part. Nothing has to cross between parts.
Inputs may be any that keep to these rules, and one draw needn't show every extreme that they name: `hist_lengths`: every length is a multiple of 512; the lengths sum to 8192; the largest is exactly 2048. `cand_request`: among the candidates of one index of ctx, at most 24 belong to one request.
All inputs are finite; a program needn't handle non-finite values.
Results may differ from a plain program's by a relative error of at most 0.0047.
Values may be sent and summed in bfloat16 or wider, within the bound.
No kernel may reach another device: no remote copies, remote signals or barrier semaphores. Data moves between devices by JAX's collectives and lax.ppermute only.
A program may use at most 64 MiB of HBM per device.

v0:
```python
import jax
import jax.numpy as jnp
from jax import lax
from jax.sharding import PartitionSpec as P

MOST = 24


def slot_table(block_req, lower, upper, slot_count):
    wanted = jnp.logical_and(block_req >= lower, block_req <= upper)
    rank = jnp.cumsum(wanted.astype(jnp.int32), axis=-1) - 1
    slot_ids = jnp.arange(slot_count, dtype=jnp.int32)
    return jnp.logical_and(wanted[..., None, :], rank[..., None, :] == slot_ids[:, None])


def body(
    sem_tokens,
    cand_request,
    hist_lengths,
    hist_buckets,
    hist_keys,
    hist_values,
    code_table,
    proj_in,
    time_bias,
    proj_out,
):
    cand_rows = sem_tokens.shape[0]
    levels = sem_tokens.shape[1]
    code_count = code_table.shape[0] // levels
    model_width = code_table.shape[1]
    local_cols = proj_in.shape[2]
    heads_local = time_bias.shape[1]
    bucket_count = time_bias.shape[0]
    head_size = local_cols // heads_local
    hist_rows = hist_keys.shape[0]
    request_count = hist_lengths.shape[0]
    score_scale = head_size ** (-0.5)
    cand_flat = cand_request[:, 0]
    code_index = sem_tokens + code_count * jnp.arange(levels, dtype=jnp.int32)[None, :]
    table_ids = jnp.arange(levels * code_count, dtype=jnp.int32)
    one_hot = jnp.sum(
        (code_index[:, :, None] == table_ids[None, None, :]).astype(jnp.bfloat16), axis=1
    )
    embedded = jnp.dot(one_hot, code_table, preferred_element_type=jnp.float32)
    row_mean = jnp.mean(embedded, axis=-1, keepdims=True)
    row_var = jnp.mean((embedded - row_mean) ** 2, axis=-1, keepdims=True)
    normed = ((embedded - row_mean) / jnp.sqrt(row_var + 1e-05)).astype(jnp.bfloat16)
    activated = jax.nn.silu(
        jnp.dot(
            normed, proj_in.reshape(model_width, 4 * local_cols), preferred_element_type=jnp.float32
        )
    )
    activated = activated.reshape(cand_rows, 4, local_cols)
    gate_u = activated[:, 0]
    query = activated[:, 1].astype(jnp.bfloat16)
    self_key = activated[:, 2]
    self_value = activated[:, 3]
    seg_ends = jnp.cumsum(hist_lengths)
    positions = lax.axis_index("ctx") * hist_rows + jnp.arange(hist_rows, dtype=jnp.int32)
    key_seg = jnp.sum((positions[:, None] >= seg_ends[None, :]).astype(jnp.int32), axis=1)
    bucket_hot = (
        hist_buckets[:, None] == jnp.arange(bucket_count, dtype=jnp.int32)[None, :]
    ).astype(jnp.float32)
    key_bias = jnp.dot(bucket_hot, time_bias, precision=lax.Precision.HIGHEST)
    key_heads = hist_keys.reshape(hist_rows, heads_local, head_size)
    value_heads = hist_values.reshape(hist_rows, heads_local, head_size)

    def attend(block_query, block_req):
        rows_here = block_query.shape[0]
        scores = jnp.einsum(
            "qhe,khe->qhk",
            block_query.reshape(rows_here, heads_local, head_size),
            key_heads,
            preferred_element_type=jnp.float32,
        )
        scores = scores * score_scale + key_bias.T[None, :, :]
        masked = block_req[:, None] == key_seg[None, :]
        weights = jnp.where(masked[:, None, :], jax.nn.silu(scores), 0.0).astype(jnp.bfloat16)
        summed = jnp.einsum(
            "qhk,khe->qhe", weights, value_heads, preferred_element_type=jnp.float32
        )
        return summed.reshape(rows_here, local_cols)

    def attend_rows(part_query, part_req):
        row_count = part_query.shape[0]
        block_rows = 512 if row_count % 512 == 0 else row_count
        block_count = row_count // block_rows
        if block_count == 1:
            return attend(part_query, part_req)
        stacked = lax.map(
            lambda packed: attend(packed[0], packed[1]),
            (
                part_query.reshape(block_count, block_rows, local_cols),
                part_req.reshape(block_count, block_rows),
            ),
        )
        return stacked.reshape(row_count, local_cols)

    all_query, all_req = (
        lax.all_gather(query, "ctx", axis=0, tiled=True),
        lax.all_gather(cand_flat, "ctx", axis=0, tiled=True),
    )
    ctx_count = lax.axis_size("ctx")
    slot_count = 2 * MOST
    owner_req = all_req.reshape(ctx_count, cand_rows)
    pick = slot_table(owner_req, key_seg[0], key_seg[hist_rows - 1], slot_count)
    pick_hot = pick.astype(jnp.bfloat16)
    slot_query = jnp.einsum(
        "osc,ocf->osf",
        pick_hot,
        all_query.reshape(ctx_count, cand_rows, local_cols),
        preferred_element_type=jnp.float32,
    ).astype(jnp.bfloat16)
    slot_used = jnp.any(pick, axis=-1)
    slot_req = jnp.where(slot_used, jnp.sum(jnp.where(pick, owner_req[:, None, :], 0), axis=-1), -1)
    sent = attend_rows(
        slot_query.reshape(ctx_count * slot_count, local_cols),
        slot_req.reshape(ctx_count * slot_count),
    )
    received = lax.all_to_all(
        sent.reshape(ctx_count, slot_count, local_cols),
        "ctx",
        split_axis=0,
        concat_axis=0,
        tiled=True,
    )
    shard_starts = jnp.arange(ctx_count, dtype=jnp.int32) * hist_rows
    first_req = jnp.sum((shard_starts[:, None] >= seg_ends[None, :]).astype(jnp.int32), axis=1)
    last_req = jnp.sum(
        ((shard_starts + hist_rows - 1)[:, None] >= seg_ends[None, :]).astype(jnp.int32), axis=1
    )
    mine = jnp.broadcast_to(cand_flat[None, :], (ctx_count, cand_rows))
    tables = slot_table(mine, first_req[:, None], last_req[:, None], slot_count).astype(jnp.float32)
    history = jnp.einsum("dsc,dsf->cf", tables, received, precision=lax.Precision.HIGHEST)
    request_hot = cand_flat[:, None] == jnp.arange(request_count, dtype=jnp.int32)[None, :]
    req_lengths = jnp.sum(jnp.where(request_hot, hist_lengths[None, :], 0), axis=1).astype(
        jnp.float32
    )
    query_heads = query.astype(jnp.float32).reshape(cand_rows, heads_local, head_size)
    self_score = (
        jnp.sum(query_heads * self_key.reshape(cand_rows, heads_local, head_size), axis=-1)
        * score_scale
        + time_bias[0][None, :]
    )
    attended = (
        history.reshape(cand_rows, heads_local, head_size) / jnp.sqrt(req_lengths)[:, None, None]
    )
    attended = attended + jax.nn.silu(self_score)[:, :, None] * self_value.reshape(
        cand_rows, heads_local, head_size
    )
    head_mean = jnp.mean(attended, axis=-1, keepdims=True)
    head_var = jnp.mean((attended - head_mean) ** 2, axis=-1, keepdims=True)
    normalized = (attended - head_mean) / jnp.sqrt(head_var + 1e-05)
    mixed = (normalized.reshape(cand_rows, local_cols) * gate_u).astype(jnp.bfloat16)
    projected = jnp.dot(mixed, proj_out, preferred_element_type=jnp.float32)
    half_width = model_width // lax.axis_size("head")
    summed = lax.psum_scatter(projected, "head", scatter_dimension=1, tiled=True)
    residual = lax.dynamic_slice_in_dim(
        embedded, lax.axis_index("head") * half_width, half_width, 1
    )
    return (residual + summed).astype(jnp.bfloat16)


def solution(mesh):
    in_specs = (
        P(("groups", "ctx"), None),
        P(("groups", "ctx"), None),
        P("groups"),
        P(("groups", "ctx")),
        P(("groups", "ctx"), "head"),
        P(("groups", "ctx"), "head"),
        P(),
        P(None, None, "head"),
        P(None, "head"),
        P("head", None),
    )
    out_specs = P(("groups", "ctx"), "head")
    return jax.shard_map(body, mesh=mesh, in_specs=in_specs, out_specs=out_specs, check_vma=False)
```

profile of v0, /device:TPU:0, one launch (start us, length us, event | category | flops | bytes accessed | tf_op | source)
XLA Modules:
  0.0 123.1 jit_solution(9580051427585725987)
XLA Ops:
  6.5 3.7 %copy.52 = bf16[128,8,4,512]{3,1,2,0:T(8,128)(2,1)S(1)} copy(bf16[128,8,4,512]{3,2,1,0:T(4,128)(2,1)} %bitcast.72) | data formatting | bytes 8388608
  12.1 1.9 %divide_multiply_fusion = f32[128,2048]{1,0:T(8,128)} fusion(bf16[1024,2048]{1,0:T(8,128)(2,1)S(1)} %bitcast.73, f32[128,1024]{1,0:T(8,128)S(1)} %get-tuple-element.19, f32[128]{0:T(128)S(1)} %add_sqrt_fusion.1, f32[128]{0:T(128)S(1)} %broadcast_multiply_fusion.1), kind=kOutput, calls=%fused_computation.16 | convolution fusion | flops 538312704 | bytes 5768192 | tf_op jit(solution)/shard_map/dot_general | solution.py:50
  13.9 2.0 %reshape.298 = f32[128,4,512]{2,1,0:T(4,128)S(1)} reshape(f32[128,2048]{1,0:T(8,128)} %divide_multiply_fusion) | data formatting | bytes 2097152 | tf_op jit(solution)/shard_map/reshape | solution.py:54
  15.9 1.3 %fusion.44 = (f32[128,1,512]{2,1,0:T(1,128)S(1)}, f32[128,1,512]{2,1,0:T(1,128)}, f32[128,1,512]{2,1,0:T(1,128)}) fusion(f32[128,4,512]{2,1,0:T(4,128)S(1)} %reshape.298), kind=kLoop, calls=%fused_computation.79 | loop fusion | bytes 1572864 | tf_op jit(solution)/shard_map/slice | solution.py:57
  18.3 1.5 %copy.36 = bf16[1024,512]{0,1:T(8,128)(2,1)S(1)} copy(bf16[1024,512]{1,0:T(8,128)(2,1)} %param.15) | data formatting | bytes 2097152 | tf_op args[5]
  20.0 22.3 %all-gather = s32[1024,1]{0,1:T(1,128)S(1)} all-gather(s32[128,1]{0,1:T(1,128)S(1)} %copy-done.7), channel_id=2, replica_groups=mesh['groups'=2,'ctx'=8,'head'=2] {'ctx'}, dimensions={0}, use_global_device_ids=true | all-gather | bytes 4608 | tf_op jit(solution)/shard_map/all_gather | solution.py:102
  43.1 1.2 %fusion.43 = (s32[8,128]{1,0:T(8,128)S(1)}, pred[8,128]{1,0:T(8,128)(4,1)S(1)}) fusion(s32[8,128]{1,0:T(8,128)S(1)} %bitcast.83, s32[]{:T(128)} %bitcast.5, s32[]{:T(128)} %bitcast.4), kind=kLoop, calls=%fused_computation.78 | loop fusion | flops 4096 | bytes 9224 | tf_op jit(solution)/shard_map/convert_element_type | solution.py:11
  45.2 2.4 %copy.34 = bf16[1024,512]{0,1:T(8,128)(2,1)} copy(bf16[1024,512]{1,0:T(8,128)(2,1)} %param.14) | data formatting | bytes 2097152 | tf_op args[4]
  47.6 1.7 %convolution_bitcast_fusion.1 = f32[8,1024]{1,0:T(8,128)} fusion(f32[128,8]{0,1:T(8,128)S(1)} %copy-done.5, s32[1024]{0:T(1024)} %param.13), kind=kOutput, calls=%fused_computation.14 | convolution fusion | flops 12713984 | bytes 40960 | tf_op jit(solution)/shard_map/dot_general | solution.py:65
  49.3 1.0 broadcast_compare_fusion
  50.3 11.0 %all-gather.4.cloned.1.call-done = bf16[1024,1,512]{2,0,1:T(8,128)(2,1)} async-done(((bf16[128,1,512]{2,0,1:T(8,128)(2,1)}), bf16[1024,1,512]{2,0,1:T(8,128)(2,1)}) %all-gather.4.cloned.1.call-update) | async-done | bytes 1048592 | tf_op jit(solution)/shard_map/all_gather | solution.py:101
  61.4 1.5 %convolution_convert_fusion = bf16[8,48,512]{2,1,0:T(8,128)(2,1)S(1)} fusion(bf16[8,128,512]{2,1,0:T(8,128)(2,1)} %bitcast.76, s32[8,128]{1,0:T(8,128)S(1)} %broadcast_add_fusion, pred[8,128]{1,0:T(8,128)(4,1)S(1)} %get-tuple-element.10), kind=kOutput, calls=%fused_computation.12 | convolution fusion | flops 50626560 | bytes 1446912 | tf_op jit(solution)/shard_map/osc,ocf->osf/dot_general | solution.py:109
  62.9 1.3 %reshape_reshape.6 = bf16[384,8,64]{2,1,0:T(8,128)(2,1)} reshape(bf16[8,48,512]{2,1,0:T(8,128)(2,1)S(1)} %convolution_convert_fusion) | data formatting | bytes 786432 | tf_op jit(solution)/shard_map/reshape;reshape | solution.py:73
  64.1 7.6 %fusion.10 = f32[384,8,64]{0,2,1:T(8,128)} fusion(bf16[1024,8,64]{0,2,1:T(8,128)(2,1)S(1)} %bitcast.77, f32[8,1024]{1,0:T(8,128)} %convolution_bitcast_fusion.1, pred[384,1024]{1,0:T(8,128)(4,1)} %broadcast_compare_fusion, bf16[1024,8,64]{0,2,1:T(8,128)(2,1)} %bitcast.78, bf16[384,8,64]{2,1,0:T(8,128)(2,1)} %reshape_reshape.6), kind=kOutput, calls=%fused_computation.11 | convolution fusion | flops 830472192 | bytes 3702784 | tf_op jit(solution)/shard_map/qhk,khe->qhe/dot_general | solution.py:80
  71.8 2.8 %copy.37 = f32[384,8,64]{2,1,0:T(8,128)} copy(f32[384,8,64]{0,2,1:T(8,128)} %fusion.10) | data formatting | bytes 1572864 | tf_op jit(solution)/shard_map/qhk,khe->qhe/transpose | solution.py:80
  74.6 2.6 %reshape_reshape.7 = f32[8,48,512]{2,1,0:T(8,128)} reshape(f32[384,8,64]{2,1,0:T(8,128)} %copy.37) | data formatting | bytes 1572864 | tf_op jit(solution)/shard_map/reshape;reshape | solution.py:122
  77.2 3.5 %all-to-all-start = ((f32[8,48,512]{2,1,0:T(8,128)}), f32[8,48,512]{2,1,0:T(8,128)S(1)}, u32[]{:S(2)}, u32[]{:S(2)}) async-start(f32[8,48,512]{2,1,0:T(8,128)} %reshape_reshape.7), calls=%async_computation | async-start | bytes 1572864 | tf_op jit(solution)/shard_map/all_to_all | solution.py:121
  83.3 1.9 %copy.41 = f32[128,512]{1,0:T(8,128)} copy(f32[128,512]{0,1:T(8,128)} %bitcast.82) | data formatting | bytes 524288 | tf_op jit(solution)/shard_map/mul | solution.py:149
  85.3 14.9 %all-to-all-done = f32[8,48,512]{2,1,0:T(8,128)S(1)} async-done(((f32[8,48,512]{2,1,0:T(8,128)}), f32[8,48,512]{2,1,0:T(8,128)S(1)}, u32[]{:S(2)}, u32[]{:S(2)}) %all-to-all-start) | async-done | bytes 786464 | tf_op jit(solution)/shard_map/all_to_all | solution.py:121
  100.2 1.2 convolution_bitcast_fusion
  101.4 1.1 copy.42
  104.8 2.8 %fusion.31 = f32[128,1024]{1,0:T(8,128)} fusion(bf16[512,1024]{1,0:T(8,128)(2,1)} %param.19, f32[128,1,512]{2,1,0:T(1,128)} %get-tuple-element.15, f32[128,512]{1,0:T(8,128)S(1)} %copy.45, f32[128,512]{1,0:T(8,128)S(1)} %copy.44, f32[128,512]{1,0:T(8,128)} %copy.41, f32[128,1,512]{2,1,0:T(1,128)} %get-tuple-element.14, ...), kind=kOutput, calls=%fused_computation.45 | convolution fusion | flops 134676480 | bytes 3146240 | tf_op jit(solution)/shard_map/dot_general | solution.py:156
  107.6 7.0 %reduce-scatter.2.cloned.1.call-done = f32[128,512]{1,0:T(8,128)} async-done(((f32[128,1024]{1,0:T(8,128)}), f32[128,512]{1,0:T(8,128)}) %reduce-scatter.2.cloned.1.call-update) | async-done | bytes 262160 | tf_op jit(solution)/shard_map/reduce_scatter | solution.py:158
  114.6 1.6 %add_convert_fusion = bf16[128,512]{1,0:T(8,128)(2,1)} fusion(f32[128,512]{1,0:T(8,128)} %reduce-scatter.2.cloned.1.call-done, f32[128,1024]{1,0:T(8,128)S(1)} %copy-done.2, s32[]{:T(128)S(6)} %select_n.26), kind=kLoop, calls=%fused_computation.33 | loop fusion | flops 131072 | bytes 655364 | tf_op jit(solution)/shard_map/convert_element_type | solution.py:162
  (66 shorter events, 9.6 us)
Async XLA Ops:
  6.5 4.2 %copy-start = (bf16[1024,1024]{1,0:T(8,128)(2,1)S(1)}, bf16[1024,1024]{1,0:T(8,128)(2,1)}, u32[]{:S(2)}) copy-start(bf16[1024,1024]{1,0:T(8,128)(2,1)} %param.16) | copy-start | bytes 6291460
  6.5 54.8 %all-gather.4.cloned.1.call-start = ((), (), s32[]{:S(2)}) async-start(), calls=%async_computation.3 | async-start | bytes 1179648 | tf_op jit(solution)/shard_map/all_gather | solution.py:101
  6.5 3.8 %copy-start.6 = (s32[128,4]{0,1:T(4,128)S(1)}, s32[128,4]{0,1:T(4,128)}, u32[]{:S(2)}) copy-start(s32[128,4]{0,1:T(4,128)} %param.10) | copy-start | bytes 6148
  11.2 0.8 copy-start.1
  13.9 5.9 %copy-start.9 = (s32[8]{0:T(128)S(1)}, s32[8]{0:T(128)}, u32[]{:S(2)}) copy-start(s32[8]{0:T(128)} %param.12) | copy-start | bytes 100
  13.9 6.1 %copy-start.7 = (s32[128,1]{0,1:T(1,128)S(1)}, s32[128,1]{0,1:T(1,128)}, u32[]{:S(2)}) copy-start(s32[128,1]{0,1:T(1,128)} %param.11) | copy-start | bytes 1540
  15.9 31.7 %copy-start.5 = (f32[128,8]{0,1:T(8,128)S(1)}, f32[128,8]{0,1:T(8,128)}, u32[]{:S(2)}) copy-start(f32[128,8]{0,1:T(8,128)} %param.18) | copy-start | bytes 12292
  71.8 9.0 %copy-start.3 = (f32[128,1,512]{2,1,0:T(1,128)S(1)}, f32[128,1,512]{2,1,0:T(1,128)}, u32[]{:S(2)}) copy-start(f32[128,1,512]{2,1,0:T(1,128)} %get-tuple-element.14) | copy-start | bytes 786436
  71.8 9.9 %copy-start.4 = (f32[128,1,512]{2,0,1:T(8,128)S(1)}, f32[128,1,512]{2,0,1:T(8,128)}, u32[]{:S(2)}) copy-start(f32[128,1,512]{2,0,1:T(8,128)} %get-tuple-element.11) | copy-start | bytes 786436
  71.8 10.2 %copy-start.8 = (s32[128,1]{0,1:T(1,128)S(1)}, s32[128,1]{0,1:T(1,128)}, u32[]{:S(2)}) copy-start(s32[128,1]{0,1:T(1,128)} %param.11) | copy-start | bytes 1540
  71.8 13.4 %copy-start.10 = (s32[8]{0:T(128)S(1)}, s32[8]{0:T(128)}, u32[]{:S(2)}) copy-start(s32[8]{0:T(128)} %param.12) | copy-start | bytes 100
  77.2 23.0 %all-to-all-start = ((f32[8,48,512]{2,1,0:T(8,128)}), f32[8,48,512]{2,1,0:T(8,128)S(1)}, u32[]{:S(2)}, u32[]{:S(2)}) async-start(f32[8,48,512]{2,1,0:T(8,128)} %reshape_reshape.7), calls=%async_computation | async-start | bytes 1572864 | tf_op jit(solution)/shard_map/all_to_all | solution.py:121
  80.8 33.9 %reduce-scatter.2.cloned.1.call-start = ((), (), s32[]{:S(2)}) async-start(), calls=%async_computation.2 | async-start | bytes 786432 | tf_op jit(solution)/shard_map/reduce_scatter | solution.py:158
  83.3 31.3 %copy-start.2 = (f32[128,1024]{1,0:T(8,128)S(1)}, f32[128,1024]{1,0:T(8,128)}, u32[]{:S(2)}) copy-start(f32[128,1024]{1,0:T(8,128)} %copy-done.1) | copy-start | bytes 1572868
Sparse Core Ops, SparseCore 0:
  18.5 42.8 all-gather.3
  107.7 6.8 reduce-scatter.1
where the time goes:
time: 124 us; the launch traced here: 123 us
  waiting for transfers between devices  32.9 us (27%)
  local copies, waits for them, and re-layouts  24.3 us (20%)
  blocking collectives  22.3 us (18%)
  matrix products  17.2 us (14%)
  between operations  13.6 us (11%)
  other arithmetic  9.13 us (7%)
  starting transfers between devices  3.59 us (3%)
    all_gather x1, blocking collectives, body(): lax.all_gather(cand_flat, 'ctx', axis=0, tiled=True)  22.3 us
    all_to_all x1, waiting for transfers between devices, body(): lax.all_to_all(sent.reshape(ctx_count, slot_count, local_cols), 'ctx', sp...  14.9 us
    all_gather x1, waiting for transfers between devices, body(): lax.all_gather(query, 'ctx', axis=0, tiled=True)  11 us
    unnamed x25, local copies, waits for them, and re-layouts  8.25 us
    dot_general x1, matrix products, attend(): jnp.einsum('qhk,khe->qhe', weights, value_heads, preferred_element_type=j...  7.63 us
    reduce_scatter x1, waiting for transfers between devices, body(): lax.psum_scatter(projected, 'head', scatter_dimension=1, tiled=True)  7.01 us
    all_to_all x1, starting transfers between devices, body(): lax.all_to_all(sent.reshape(ctx_count, slot_count, local_cols), 'ctx', sp...  3.55 us
    transpose x1, local copies, waits for them, and re-layouts, attend(): jnp.einsum('qhk,khe->qhe', weights, value_heads, preferred_element_type=j...  2.83 us
  transfers between devices with their start and end apart: 3, of which 3 were waited for; matrix products, arithmetic and copies ran while one was open for 11% of the time, Pallas kernels for 0%

commit v1 on v0

v1 whole, which is shorter than its diff:
```python
import functools

import jax
import jax.numpy as jnp
from jax import lax
from jax.experimental import pallas as pl
from jax.experimental.pallas import tpu as pltpu
from jax.sharding import PartitionSpec as P

MOST = 24
UNIT = 512
ROWS = 8

BF16 = jnp.bfloat16
F32 = jnp.float32
NT = (((1,), (1,)), ((), ()))


def dot(a, b, dims=(((1,), (0,)), ((), ()))):
    return lax.dot_general(a, b, dims, preferred_element_type=F32)


def split_dot(x, b):
    high = x.astype(BF16)
    low = (x - high.astype(F32)).astype(BF16)
    return dot(high, b) + dot(low, b)


def silu(v):
    t = 0.5 * v
    return t + t * jnp.tanh(t)


def iota(shape, dim):
    return lax.broadcasted_iota(jnp.int32, shape, dim)


def upto(size):
    return (iota((size, size), 0) <= iota((size, size), 1)).astype(F32).astype(BF16)


def request_at(position, lens_ref):
    end = lens_ref[0]
    request = jnp.where(position >= end, 1, 0)
    for r in range(1, lens_ref.shape[0]):
        end = end + lens_ref[r]
        request = request + jnp.where(position >= end, 1, 0)
    return request


def embed(tokens, levels, table):
    codes = table.shape[0] // levels
    rows = tokens.shape[0]
    lane = iota((rows, codes), 1).astype(F32)
    hot = jnp.concatenate(
        [jnp.where(lane == tokens[:, l : l + 1], 1.0, 0.0).astype(BF16) for l in range(levels)],
        axis=1,
    )
    return dot(hot, table)


def normalize(embedded):
    width = embedded.shape[1]
    mean = jnp.sum(embedded, axis=1, keepdims=True) * (1.0 / width)
    centred = embedded - mean
    var = jnp.sum(centred * centred, axis=1, keepdims=True) * (1.0 / width)
    return (centred * lax.rsqrt(var + 1e-05)).astype(BF16)


def attend_kernel(
    levels, heads, me_ref, lens_ref, cand_ref, bucket_ref, bias_ref, key_ref, value_ref, table_ref, wq_ref, *rest
):
    owners, _, cand = cand_ref.shape
    outs, (slot_ref, result_ref) = rest[:owners], rest[owners:]
    hist, cols = key_ref.shape
    parts = hist // UNIT
    buckets = bias_ref.shape[1]
    part_rows = owners * MOST
    head_size = cols // heads
    first = me_ref[0] * hist
    order = upto(cand)
    slot = iota((MOST, cand), 0).astype(F32) + 1.0
    requests = cand_ref[:, levels, :]
    tokens = cand_ref[...].astype(F32).astype(BF16)
    for p in range(parts):
        wanted = requests == request_at(first + p * UNIT, lens_ref)
        hot = jnp.where(wanted, 1.0, 0.0)
        rank = jnp.where(wanted, dot(hot.astype(BF16), order), 0.0)
        for k in range(owners):
            pick = jnp.where(slot == rank[k : k + 1, :], 1.0, 0.0).astype(BF16)
            at = p * part_rows + k * MOST
            slot_ref[at : at + MOST, :] = dot(pick, tokens[k], NT)
    query = dot(normalize(embed(slot_ref[...], levels, table_ref[...])), wq_ref[...])
    query = silu(query).astype(BF16) * BF16(0.5 * head_size**-0.5)
    hot = jnp.where(iota((buckets, hist), 0) == bucket_ref[...], 1.0, 0.0).astype(BF16)
    bias = bias_ref[...] * 0.5
    high = bias.astype(BF16)
    low = (bias - high.astype(F32)).astype(BF16)
    bias = dot(high, hot) + dot(low, hot)
    pair = 2 * head_size
    lane = iota((part_rows, pair), 1)
    for p in range(parts):
        rows = slice(p * UNIT, (p + 1) * UNIT)
        for g in range(heads // 2):
            at = slice(g * pair, (g + 1) * pair)
            part = query[p * part_rows : (p + 1) * part_rows, at]
            zero = jnp.zeros_like(part)
            both = jnp.concatenate(
                [jnp.where(lane < head_size, part, zero), jnp.where(lane < head_size, zero, part)], axis=0
            )
            score = dot(both, key_ref[rows, at], NT)
            line = jnp.concatenate(
                [
                    jnp.broadcast_to(bias[2 * g + i : 2 * g + i + 1, rows], (part_rows, UNIT))
                    for i in range(2)
                ],
                axis=0,
            )
            t = score + line
            weight = (t + t * jnp.tanh(t)).astype(BF16)
            summed = dot(weight, value_ref[rows, at])
            kept = jnp.where(lane < head_size, summed[:part_rows], summed[part_rows:])
            for k in range(owners):
                result_ref[k, p * MOST : (p + 1) * MOST, at] = kept[k * MOST : (k + 1) * MOST]
    for k in range(owners):
        outs[k][...] = result_ref[k].astype(BF16)


def own_kernel(
    levels, heads, parts, me_ref, lens_ref, cand_ref, bias_ref, table_ref, win_ref, gate_ref, self_ref, assign_ref, scale_ref, embedded_ref
):
    _, cand = cand_ref.shape
    cols = win_ref.shape[2]
    head_size = cols // heads
    lens_count = lens_ref.shape[0]
    eye = (iota((cand, cand), 0) == iota((cand, cand), 1)).astype(F32).astype(BF16)
    facts = dot(eye, cand_ref[...].astype(F32).astype(BF16), NT)
    embedded = embed(facts, levels, table_ref[...])
    embedded_ref[...] = embedded
    normed = normalize(embedded)
    gate_ref[...] = silu(dot(normed, win_ref[0]))
    query = silu(dot(normed, win_ref[1])).astype(BF16).astype(F32)
    self_key = silu(dot(normed, win_ref[2]))
    self_value = silu(dot(normed, win_ref[3]))
    same = (iota((cols, cols), 0) // head_size == iota((cols, cols), 1) // head_size).astype(F32).astype(BF16)
    spread = (iota((heads, cols), 0) == iota((heads, cols), 1) // head_size).astype(F32)
    first_bias = jnp.sum(spread * bias_ref[:, 0:1], axis=0, keepdims=True)
    score = split_dot(query * self_key, same) * head_size**-0.5 + first_bias
    self_ref[...] = silu(score) * self_value
    request = facts[:, levels : levels + 1]
    other = cand_ref[levels : levels + 1, :].astype(F32)
    before = iota((cand, cand), 0) > iota((cand, cand), 1)
    rank = jnp.sum(jnp.where(jnp.logical_and(request == other, before), 1.0, 0.0), axis=1, keepdims=True)
    slots = assign_ref.shape[1]
    line = iota((1, slots), 1)
    block = line // MOST
    shard = jnp.bitwise_xor(block // parts, me_ref[0])
    slot_request = request_at((shard * parts + block % parts) * UNIT, lens_ref).astype(F32)
    slot_rank = (line % MOST).astype(F32)
    hit = jnp.logical_and(request == slot_request, rank == slot_rank)
    assign_ref[...] = jnp.where(hit, 1.0, 0.0).astype(BF16)
    length = jnp.zeros((cand, 1), F32)
    for r in range(lens_count):
        length = jnp.where(request == float(r), lens_ref[r].astype(F32), length)
    scale_ref[...] = jnp.broadcast_to(lax.rsqrt(length), scale_ref.shape)


def finish_kernel(heads, me_ref, gate_ref, self_ref, assign_ref, scale_ref, embedded_ref, wout_ref, *rest):
    received, (send_ref, keep_ref) = rest[:-2], rest[-2:]
    cols = gate_ref.shape[1]
    head_size = cols // heads
    history = dot(assign_ref[...], jnp.concatenate([r[...] for r in received], axis=0))
    attended = history * scale_ref[:, 0:1] + self_ref[...]
    same = (iota((cols, cols), 0) // head_size == iota((cols, cols), 1) // head_size).astype(F32).astype(BF16)
    centred = attended - split_dot(attended, same) * (1.0 / head_size)
    var = split_dot(centred * centred, same) * (1.0 / head_size)
    mixed = (centred * lax.rsqrt(var + 1e-05) * gate_ref[...]).astype(BF16)
    half = wout_ref.shape[1] // 2
    projected = dot(mixed, wout_ref[...])
    second = me_ref[1] == 1
    send_ref[...] = jnp.where(second, projected[:, :half], projected[:, half:]).astype(BF16)
    keep_ref[...] = jnp.where(
        second, projected[:, half:] + embedded_ref[:, half:], projected[:, :half] + embedded_ref[:, :half]
    )


def full(shape, dtype):
    return jax.ShapeDtypeStruct(shape, dtype)


def body(
    sem_tokens,
    cand_request,
    hist_lengths,
    hist_buckets,
    hist_keys,
    hist_values,
    code_table,
    proj_in,
    time_bias,
    proj_out,
):
    cand, levels = sem_tokens.shape
    hist, cols = hist_keys.shape
    heads = time_bias.shape[1]
    width = code_table.shape[1]
    owners = lax.axis_size("ctx")
    parts = hist // UNIT
    block = parts * MOST
    slots = owners * block
    me = jnp.stack([lax.axis_index("ctx"), lax.axis_index("head")]).astype(jnp.int32)
    payload = jnp.concatenate(
        [sem_tokens.T, cand_request.T, jnp.zeros((ROWS - levels - 1, cand), jnp.int32)], axis=0
    )

    def swap(x, mask):
        return lax.ppermute(x, "ctx", [(i, i ^ mask) for i in range(owners)])

    gathered = payload[None]
    bit = 1
    while bit < owners:
        gathered = jnp.concatenate([gathered, swap(gathered, bit)], axis=0)
        bit *= 2
    weights = jnp.transpose(proj_in, (1, 0, 2))
    bias = time_bias.T
    smem = pl.BlockSpec(memory_space=pltpu.SMEM)
    vmem = pl.BlockSpec(memory_space=pltpu.VMEM)
    sent = pl.pallas_call(
        functools.partial(attend_kernel, levels, heads),
        out_shape=[full((block, cols), BF16)] * owners,
        in_specs=[smem] * 2 + [vmem] * 7,
        out_specs=[vmem] * owners,
        scratch_shapes=[pltpu.VMEM((slots, ROWS), F32), pltpu.VMEM((owners, block, cols), F32)],
        compiler_params=pltpu.CompilerParams(vmem_limit_bytes=40 << 20),
        cost_estimate=pl.CostEstimate(flops=4_000_000_000, bytes_accessed=6 << 20, transcendentals=2_000_000),
        name="attend",
    )(me, hist_lengths, gathered, hist_buckets.reshape(1, hist), bias, hist_keys, hist_values, code_table, weights[1])
    received = [sent[0]] + [swap(sent[m], m) for m in range(1, owners)]
    own = pl.pallas_call(
        functools.partial(own_kernel, levels, heads, parts),
        out_shape=[
            full((cand, cols), F32),
            full((cand, cols), F32),
            full((cand, slots), BF16),
            full((cand, 128), F32),
            full((cand, width), F32),
        ],
        in_specs=[smem] * 2 + [vmem] * 4,
        out_specs=[vmem] * 5,
        compiler_params=pltpu.CompilerParams(vmem_limit_bytes=40 << 20),
        cost_estimate=pl.CostEstimate(flops=2_000_000_000, bytes_accessed=7 << 20, transcendentals=500_000),
        name="own",
    )(me, hist_lengths, payload, bias, code_table, weights)
    send, keep = pl.pallas_call(
        functools.partial(finish_kernel, heads),
        out_shape=[full((cand, width // 2), BF16), full((cand, width // 2), F32)],
        in_specs=[smem] + [vmem] * (6 + owners),
        out_specs=[vmem] * 2,
        compiler_params=pltpu.CompilerParams(vmem_limit_bytes=40 << 20),
        cost_estimate=pl.CostEstimate(flops=1_000_000_000, bytes_accessed=2 << 20, transcendentals=100_000),
        name="finish",
    )(me, *own, proj_out, *received)
    other = lax.ppermute(send, "head", [(0, 1), (1, 0)])
    return (keep + other.astype(F32)).astype(BF16)


def solution(mesh):
    in_specs = (
        P(("groups", "ctx"), None),
        P(("groups", "ctx"), None),
        P("groups"),
        P(("groups", "ctx")),
        P(("groups", "ctx"), "head"),
        P(("groups", "ctx"), "head"),
        P(),
        P(None, None, "head"),
        P(None, "head"),
        P("head", None),
    )
    out_specs = P(("groups", "ctx"), "head")
    return jax.shard_map(body, mesh=mesh, in_specs=in_specs, out_specs=out_specs, check_vma=False)
```

time: 124 us -> 43.5 us (0.35)
  waiting for transfers between devices: 32.9 us -> 6.71 us
  blocking collectives: 22.3 us -> 0 us
  matrix products: 17.2 us -> 0 us
  local copies, waits for them, and re-layouts: 24.3 us -> 7.56 us
  starting transfers between devices: 3.59 us -> 18.5 us
  between operations: 13.6 us -> 0.15 us
  Pallas kernels: 0 us -> 8.8 us
  other arithmetic: 9.13 us -> 1.53 us
    all_gather x1 -> x0, blocking collectives: 22.3 us -> none  [body(): lax.all_gather(cand_flat, 'ctx', axis=0, tiled=True)]
    ppermute x0 -> x11, starting transfers between devices: none -> 18.5 us  [the longest x10 18.5 us: swap(): return lax.ppermute(x, 'ctx', [(i, i ^ mask) for i in range(owners)])]
    dot_general x7 -> x0, matrix products: 17.2 us -> none  [the longest x1 7.63 us: attend(): jnp.einsum('qhk,khe->qhe', weights, value_heads, preferred_element_type=j...]
    all_to_all x1 -> x0, waiting for transfers between devices: 14.9 us -> none  [body(): lax.all_to_all(sent.reshape(ctx_count, slot_count, local_cols), 'ctx', sp...]
    all_gather x1 -> x0, waiting for transfers between devices: 11 us -> none  [body(): lax.all_gather(query, 'ctx', axis=0, tiled=True)]
    pallas_call x0 -> x3, Pallas kernels: none -> 8.8 us  [the longest x1 4.71 us: body(): pl.pallas_call(functools.partial(attend_kernel, levels, heads), out_shape...]
    reduce_scatter x1 -> x0, waiting for transfers between devices: 7.01 us -> none  [body(): lax.psum_scatter(projected, 'head', scatter_dimension=1, tiled=True)]
    ppermute x0 -> x11, waiting for transfers between devices: none -> 6.71 us  [the longest x10 5.37 us: swap(): return lax.ppermute(x, 'ctx', [(i, i ^ mask) for i in range(owners)])]
  transfers between devices with their start and end apart: 3 -> 11, of which waited for: 3 -> 4; matrix products, arithmetic and copies ran while one was open for 11% -> 7% of each run, Pallas kernels for 0% -> 6%
where the time goes in v1:
time: 43.5 us; the launch traced here: 43.3 us
  starting transfers between devices  18.5 us (43%)
  Pallas kernels  8.8 us (20%)
  local copies, waits for them, and re-layouts  7.56 us (17%)
  waiting for transfers between devices  6.71 us (15%)
  other arithmetic  1.53 us (4%)
    ppermute x10, starting transfers between devices, swap(): return lax.ppermute(x, 'ctx', [(i, i ^ mask) for i in range(owners)])  18.5 us
    unnamed x19, local copies, waits for them, and re-layouts  7.42 us
    ppermute x10, waiting for transfers between devices, swap(): return lax.ppermute(x, 'ctx', [(i, i ^ mask) for i in range(owners)])  5.37 us
    pallas_call x1, Pallas kernels, body(): pl.pallas_call(functools.partial(attend_kernel, levels, heads), out_shape...  4.71 us
    pallas_call x1, Pallas kernels, body(): pl.pallas_call(functools.partial(own_kernel, levels, heads, parts), out_s...  2.4 us
    pallas_call x1, Pallas kernels, body(): pl.pallas_call(functools.partial(finish_kernel, heads), out_shape=[full((...  1.69 us
    ppermute x1, waiting for transfers between devices, body(): other = lax.ppermute(send, 'head', [(0, 1), (1, 0)])  1.33 us
  transfers between devices with their start and end apart: 11, of which 4 were waited for; matrix products, arithmetic and copies ran while one was open for 7% of the time, Pallas kernels for 6%

profile of v1, /device:TPU:0, one launch (start us, length us, event | category | flops | bytes accessed | tf_op | source)
XLA Modules:
  0.0 43.3 jit_solution(16769499066804480420)
XLA Ops:
  0.0 0.1 pad.11.clone
  0.1 0.8 %fusion = (s32[1,8,128]{2,1,0:T(8,128)S(1)}, s32[8,128]{1,0:T(8,128)S(1)}) fusion(s32[8]{0:T(128)S(1)} %pad.11.clone, s32[1,128]{1,0:T(1,128)} %bitcast.19, s32[4,128]{1,0:T(4,128)} %bitcast.18), kind=kLoop, calls=%fused_computation.8 | loop fusion | flops 2048 | bytes 10784 | tf_op jit(solution)/shard_map/broadcast_in_dim | solution.py:219
  0.9 3.0 %collective-permute-start = (s32[1,8,128]{2,1,0:T(8,128)S(1)}, s32[1,8,128]{2,1,0:T(8,128)S(1)}, u32[]{:S(2)}, u32[]{:S(2)}) collective-permute-start(s32[1,8,128]{2,1,0:T(8,128)S(1)} %get-tuple-element.35), channel_id=1, source_target_pairs={{0,2},{2,0},{4,6},{6,4},{8,10},{10,8},{12,14},{14,12},{1,3},{3,1},... | collective-permute-start | bytes 12296 | tf_op jit(solution)/shard_map/ppermute | solution.py:217
  3.9 3.0 %copy.13 = bf16[1024,4,512]{2,0,1:T(8,128)(2,1)S(1)} copy(bf16[1024,4,512]{2,1,0:T(4,128)(2,1)} %param.17) | data formatting | bytes 8388608 | tf_op args[7]
  6.9 1.6 %collective-permute-start.1 = (s32[2,8,128]{2,1,0:T(8,128)S(1)}, s32[2,8,128]{2,1,0:T(8,128)S(1)}, u32[]{:S(2)}, u32[]{:S(2)}) collective-permute-start(s32[2,8,128]{2,1,0:T(8,128)S(1)} %pad_add_fusion.2), channel_id=1, source_target_pairs={{0,4},{2,6},{4,0},{6,2},{8,12},{10,14},{12,8},{14,10},{1,5},{3,7},... | collective-permute-start | bytes 24584 | tf_op jit(solution)/shard_map/ppermute | solution.py:217
  8.7 1.9 %copy-done = bf16[1024,4,512]{2,0,1:T(8,128)(2,1)} copy-done((bf16[1024,4,512]{2,0,1:T(8,128)(2,1)}, bf16[1024,4,512]{2,0,1:T(8,128)(2,1)S(1)}, u32[]{:S(2)}) %copy-start) | copy-done | bytes 4194328
  10.7 2.6 %collective-permute-start.2 = (s32[4,8,128]{2,1,0:T(8,128)S(1)}, s32[4,8,128]{2,1,0:T(8,128)S(1)}, u32[]{:S(2)}, u32[]{:S(2)}) collective-permute-start(s32[4,8,128]{2,1,0:T(8,128)S(1)} %pad_add_fusion.1), channel_id=1, source_target_pairs={{0,8},{2,10},{4,12},{6,14},{8,0},{10,2},{12,4},{14,6},{1,9},{3,11}... | collective-permute-start | bytes 49160 | tf_op jit(solution)/shard_map/ppermute | solution.py:217
  13.3 0.1 pad_add_fusion.3.me_ref
  13.3 2.0 %collective-permute-done.2 = s32[4,8,128]{2,1,0:T(8,128)S(1)} collective-permute-done((s32[4,8,128]{2,1,0:T(8,128)S(1)}, s32[4,8,128]{2,1,0:T(8,128)S(1)}, u32[]{:S(2)}, u32[]{:S(2)}) %collective-permute-start.2) | collective-permute-done | bytes 16416 | tf_op jit(solution)/shard_map/ppermute | solution.py:217
  15.3 1.2 %copy-done.3 = bf16[1024,512]{1,0:T(8,128)(2,1)S(1)} copy-done((bf16[1024,512]{1,0:T(8,128)(2,1)S(1)}, bf16[1024,512]{1,0:T(8,128)(2,1)}, u32[]{:S(2)}) %copy-start.3) | copy-done | bytes 1048600
  16.6 1.2 %copy-done.4 = bf16[1024,512]{1,0:T(8,128)(2,1)S(1)} copy-done((bf16[1024,512]{1,0:T(8,128)(2,1)S(1)}, bf16[1024,512]{1,0:T(8,128)(2,1)}, u32[]{:S(2)}) %copy-start.4) | copy-done | bytes 1048600
  17.8 4.7 %attend.1 = (bf16[48,512]{1,0:T(8,128)(2,1)S(1)}, bf16[48,512]{1,0:T(8,128)(2,1)S(1)}, bf16[48,512]{1,0:T(8,128)(2,1)S(1)}, bf16[48,512]{1,0:T(8,128)(2,1)S(1)},...) custom-call(s32[2]{0:T(128)S(1)} %pad_add_fusion.3.me_ref, ...), custom_call_target="tpu_custom_call" | custom-call | flops 4000000000 | bytes 6291456 | tf_op jit(solution)/shard_map/attend/pallas_call | solution.py:228
  22.5 0.6 %collective-permute-start.3 = (bf16[48,512]{1,0:T(8,128)(2,1)S(1)}, bf16[48,512]{1,0:T(8,128)(2,1)S(1)}, u32[]{:S(2)}, u32[]{:S(2)}) collective-permute-start(bf16[48,512]{1,0:T(8,128)(2,1)S(1)} %get-tuple-element.26), channel_id=1, source_target_pairs={{0,2},{2,0},{4,6},{6,4},{8,10},{10,8},{12,14},{14,12},{1,3},{3,1},... | collective-permute-start | bytes 147464 | tf_op jit(solution)/shard_map/ppermute | solution.py:217
  23.1 1.6 %collective-permute-start.4 = (bf16[48,512]{1,0:T(8,128)(2,1)S(1)}, bf16[48,512]{1,0:T(8,128)(2,1)S(1)}, u32[]{:S(2)}, u32[]{:S(2)}) collective-permute-start(bf16[48,512]{1,0:T(8,128)(2,1)S(1)} %get-tuple-element.27), channel_id=1, source_target_pairs={{0,4},{2,6},{4,0},{6,2},{8,12},{10,14},{12,8},{14,10},{1,5},{3,7},... | collective-permute-start | bytes 147464 | tf_op jit(solution)/shard_map/ppermute | solution.py:217
  24.8 1.3 %collective-permute-start.5 = (bf16[48,512]{1,0:T(8,128)(2,1)S(1)}, bf16[48,512]{1,0:T(8,128)(2,1)S(1)}, u32[]{:S(2)}, u32[]{:S(2)}) collective-permute-start(bf16[48,512]{1,0:T(8,128)(2,1)S(1)} %get-tuple-element.28), channel_id=1, source_target_pairs={{0,6},{2,4},{4,2},{6,0},{8,14},{10,12},{12,10},{14,8},{1,7},{3,5},... | collective-permute-start | bytes 147464 | tf_op jit(solution)/shard_map/ppermute | solution.py:217
  26.1 2.6 %collective-permute-start.6 = (bf16[48,512]{1,0:T(8,128)(2,1)S(1)}, bf16[48,512]{1,0:T(8,128)(2,1)S(1)}, u32[]{:S(2)}, u32[]{:S(2)}) collective-permute-start(bf16[48,512]{1,0:T(8,128)(2,1)S(1)} %get-tuple-element.29), channel_id=1, source_target_pairs={{0,8},{2,10},{4,12},{6,14},{8,0},{10,2},{12,4},{14,6},{1,9},{3,11}... | collective-permute-start | bytes 147464 | tf_op jit(solution)/shard_map/ppermute | solution.py:217
  28.7 0.3 collective-permute-start.7
  29.0 3.7 %collective-permute-start.8 = (bf16[48,512]{1,0:T(8,128)(2,1)S(1)}, bf16[48,512]{1,0:T(8,128)(2,1)S(1)}, u32[]{:S(2)}, u32[]{:S(2)}) collective-permute-start(bf16[48,512]{1,0:T(8,128)(2,1)S(1)} %get-tuple-element.31), channel_id=1, source_target_pairs={{0,12},{2,14},{4,8},{6,10},{8,4},{10,6},{12,0},{14,2},{1,13},{3,15... | collective-permute-start | bytes 147464 | tf_op jit(solution)/shard_map/ppermute | solution.py:217
  32.7 1.0 %collective-permute-start.9 = (bf16[48,512]{1,0:T(8,128)(2,1)S(1)}, bf16[48,512]{1,0:T(8,128)(2,1)S(1)}, u32[]{:S(2)}, u32[]{:S(2)}) collective-permute-start(bf16[48,512]{1,0:T(8,128)(2,1)S(1)} %get-tuple-element.32), channel_id=1, source_target_pairs={{0,14},{2,12},{4,10},{6,8},{8,6},{10,4},{12,2},{14,0},{1,15},{3,13... | collective-permute-start | bytes 147464 | tf_op jit(solution)/shard_map/ppermute | solution.py:217
  33.7 2.4 %own.1 = (f32[128,512]{1,0:T(8,128)S(1)}, f32[128,512]{1,0:T(8,128)S(1)}, bf16[128,384]{1,0:T(8,128)(2,1)S(1)}, f32[128,128]{1,0:T(8,128)S(1)}, f32[128,1024]{1,0:T(8,128)S(1)}) custom-call(s32[2]{0:T(128)S(1)} %pad_add_fusion.3.me_ref, s32[8]{0:T(128)S(1)} %copy-done.8, s32[8,128]{1,0:T(8,128)S(1)} %get-tuple-element.36.cand_ref, f32[8,128]{1,0:T(8,128)S(1)} %bitcast.17, ...), custom_call_target="tpu_custom_call" | custom-call | flops 2000000000 | bytes 7340032 | tf_op jit(solution)/shard_map/own/pallas_call | solution.py:239
  36.2 3.3 %collective-permute-done.9.rest_7_ = bf16[48,512]{1,0:T(8,128)(2,1)S(1)} collective-permute-done((bf16[48,512]{1,0:T(8,128)(2,1)S(1)}, bf16[48,512]{1,0:T(8,128)(2,1)S(1)}, u32[]{:S(2)}, u32[]{:S(2)}) %collective-permute-start.9) | collective-permute-done | bytes 49184 | tf_op jit(solution)/shard_map/ppermute | solution.py:217
  39.5 1.7 %finish.1 = (bf16[128,512]{1,0:T(8,128)(2,1)S(1)}, f32[128,512]{1,0:T(8,128)S(1)}) custom-call(s32[2]{0:T(128)S(1)} %pad_add_fusion.3.me_ref, f32[128,512]{1,0:T(8,128)S(1)} %get-tuple-element.20.gate_ref, f32[128,512]{1,0:T(8,128)S(1)} %get-tuple-element.21.self_ref, bf16[128,384]{1,0:T(8,128)(2,1)S(1)} %get-tuple-element.22.assign_ref, ...), custom_call_target="tpu_custom_call" | custom-call | flops 1000000000 | bytes 2097152 | tf_op jit(solution)/shard_map/finish/pallas_call | solution.py:254
  41.3 1.3 %collective-permute-done.10 = bf16[128,512]{1,0:T(8,128)(2,1)S(1)} collective-permute-done((bf16[128,512]{1,0:T(8,128)(2,1)S(1)}, bf16[128,512]{1,0:T(8,128)(2,1)S(1)}, u32[]{:S(2)}, u32[]{:S(2)}) %collective-permute-start.10) | collective-permute-done | bytes 131104 | tf_op jit(solution)/shard_map/ppermute | solution.py:263
  42.6 0.7 %add_convert_fusion = bf16[128,512]{1,0:T(8,128)(2,1)} fusion(f32[128,512]{1,0:T(8,128)S(1)} %get-tuple-element.33, bf16[128,512]{1,0:T(8,128)(2,1)S(1)} %collective-permute-done.10), kind=kLoop, calls=%fused_computation.2 | loop fusion | flops 196608 | bytes 524288 | tf_op jit(solution)/shard_map/convert_element_type | solution.py:264
  (29 shorter events, 0.3 us)
Async XLA Ops:
  0.8 14.5 %copy-start.2 = (bf16[1024,1024]{1,0:T(8,128)(2,1)S(1)}, bf16[1024,1024]{1,0:T(8,128)(2,1)}, u32[]{:S(2)}) copy-start(bf16[1024,1024]{1,0:T(8,128)(2,1)} %table_ref.3) | copy-start | bytes 6291460
  0.8 14.5 %copy-start.6 = (s32[1024]{0:T(1024)S(1)}, s32[1024]{0:T(1024)}, u32[]{:S(2)}) copy-start(s32[1024]{0:T(1024)} %param.13) | copy-start | bytes 12292
  0.9 14.5 %copy-start.7 = (f32[128,8]{0,1:T(8,128)S(1)}, f32[128,8]{0,1:T(8,128)}, u32[]{:S(2)}) copy-start(f32[128,8]{0,1:T(8,128)} %param.18) | copy-start | bytes 12292
  0.9 14.5 %copy-start.8 = (s32[8]{0:T(128)S(1)}, s32[8]{0:T(128)}, u32[]{:S(2)}) copy-start(s32[8]{0:T(128)} %lens_ref.3) | copy-start | bytes 100
  0.9 6.1 %collective-permute-start = (s32[1,8,128]{2,1,0:T(8,128)S(1)}, s32[1,8,128]{2,1,0:T(8,128)S(1)}, u32[]{:S(2)}, u32[]{:S(2)}) collective-permute-start(s32[1,8,128]{2,1,0:T(8,128)S(1)} %get-tuple-element.35), channel_id=1, source_target_pairs={{0,2},{2,0},{4,6},{6,4},{8,10},{10,8},{12,14},{14,12},{1,3},{3,1},... | collective-permute-start | bytes 12296 | tf_op jit(solution)/shard_map/ppermute | solution.py:217
  6.9 3.7 %collective-permute-start.1 = (s32[2,8,128]{2,1,0:T(8,128)S(1)}, s32[2,8,128]{2,1,0:T(8,128)S(1)}, u32[]{:S(2)}, u32[]{:S(2)}) collective-permute-start(s32[2,8,128]{2,1,0:T(8,128)S(1)} %pad_add_fusion.2), channel_id=1, source_target_pairs={{0,4},{2,6},{4,0},{6,2},{8,12},{10,14},{12,8},{14,10},{1,5},{3,7},... | collective-permute-start | bytes 24584 | tf_op jit(solution)/shard_map/ppermute | solution.py:217
  8.7 1.9 %copy-start = (bf16[1024,4,512]{2,0,1:T(8,128)(2,1)}, bf16[1024,4,512]{2,0,1:T(8,128)(2,1)S(1)}, u32[]{:S(2)}) copy-start(bf16[1024,4,512]{2,0,1:T(8,128)(2,1)S(1)} %copy.13) | copy-start | bytes 12582916
  10.7 4.6 %collective-permute-start.2 = (s32[4,8,128]{2,1,0:T(8,128)S(1)}, s32[4,8,128]{2,1,0:T(8,128)S(1)}, u32[]{:S(2)}, u32[]{:S(2)}) collective-permute-start(s32[4,8,128]{2,1,0:T(8,128)S(1)} %pad_add_fusion.1), channel_id=1, source_target_pairs={{0,8},{2,10},{4,12},{6,14},{8,0},{10,2},{12,4},{14,6},{1,9},{3,11}... | collective-permute-start | bytes 49160 | tf_op jit(solution)/shard_map/ppermute | solution.py:217
  15.3 1.2 %copy-start.3 = (bf16[1024,512]{1,0:T(8,128)(2,1)S(1)}, bf16[1024,512]{1,0:T(8,128)(2,1)}, u32[]{:S(2)}) copy-start(bf16[1024,512]{1,0:T(8,128)(2,1)} %key_ref.1) | copy-start | bytes 3145732
  16.6 1.2 %copy-start.4 = (bf16[1024,512]{1,0:T(8,128)(2,1)S(1)}, bf16[1024,512]{1,0:T(8,128)(2,1)}, u32[]{:S(2)}) copy-start(bf16[1024,512]{1,0:T(8,128)(2,1)} %value_ref.1) | copy-start | bytes 3145732
  17.8 15.9 %copy-start.1 = (bf16[1024,4,512]{2,0,1:T(8,128)(2,1)S(1)}, bf16[1024,4,512]{2,0,1:T(8,128)(2,1)}, u32[]{:S(2)}) copy-start(bf16[1024,4,512]{2,0,1:T(8,128)(2,1)} %copy-done) | copy-start | bytes 12582916
  22.5 17.0 %copy-start.5 = (bf16[512,1024]{1,0:T(8,128)(2,1)S(1)}, bf16[512,1024]{1,0:T(8,128)(2,1)}, u32[]{:S(2)}) copy-start(bf16[512,1024]{1,0:T(8,128)(2,1)} %wout_ref.1) | copy-start | bytes 3145732
  22.5 6.5 %collective-permute-start.3 = (bf16[48,512]{1,0:T(8,128)(2,1)S(1)}, bf16[48,512]{1,0:T(8,128)(2,1)S(1)}, u32[]{:S(2)}, u32[]{:S(2)}) collective-permute-start(bf16[48,512]{1,0:T(8,128)(2,1)S(1)} %get-tuple-element.26), channel_id=1, source_target_pairs={{0,2},{2,0},{4,6},{6,4},{8,10},{10,8},{12,14},{14,12},{1,3},{3,1},... | collective-permute-start | bytes 147464 | tf_op jit(solution)/shard_map/ppermute | solution.py:217
  23.1 9.6 %collective-permute-start.4 = (bf16[48,512]{1,0:T(8,128)(2,1)S(1)}, bf16[48,512]{1,0:T(8,128)(2,1)S(1)}, u32[]{:S(2)}, u32[]{:S(2)}) collective-permute-start(bf16[48,512]{1,0:T(8,128)(2,1)S(1)} %get-tuple-element.27), channel_id=1, source_target_pairs={{0,4},{2,6},{4,0},{6,2},{8,12},{10,14},{12,8},{14,10},{1,5},{3,7},... | collective-permute-start | bytes 147464 | tf_op jit(solution)/shard_map/ppermute | solution.py:217
  24.8 11.4 %collective-permute-start.5 = (bf16[48,512]{1,0:T(8,128)(2,1)S(1)}, bf16[48,512]{1,0:T(8,128)(2,1)S(1)}, u32[]{:S(2)}, u32[]{:S(2)}) collective-permute-start(bf16[48,512]{1,0:T(8,128)(2,1)S(1)} %get-tuple-element.28), channel_id=1, source_target_pairs={{0,6},{2,4},{4,2},{6,0},{8,14},{10,12},{12,10},{14,8},{1,7},{3,5},... | collective-permute-start | bytes 147464 | tf_op jit(solution)/shard_map/ppermute | solution.py:217
  26.1 10.1 %collective-permute-start.6 = (bf16[48,512]{1,0:T(8,128)(2,1)S(1)}, bf16[48,512]{1,0:T(8,128)(2,1)S(1)}, u32[]{:S(2)}, u32[]{:S(2)}) collective-permute-start(bf16[48,512]{1,0:T(8,128)(2,1)S(1)} %get-tuple-element.29), channel_id=1, source_target_pairs={{0,8},{2,10},{4,12},{6,14},{8,0},{10,2},{12,4},{14,6},{1,9},{3,11}... | collective-permute-start | bytes 147464 | tf_op jit(solution)/shard_map/ppermute | solution.py:217
  28.7 7.5 %collective-permute-start.7 = (bf16[48,512]{1,0:T(8,128)(2,1)S(1)}, bf16[48,512]{1,0:T(8,128)(2,1)S(1)}, u32[]{:S(2)}, u32[]{:S(2)}) collective-permute-start(bf16[48,512]{1,0:T(8,128)(2,1)S(1)} %get-tuple-element.30), channel_id=1, source_target_pairs={{0,10},{2,8},{4,14},{6,12},{8,2},{10,0},{12,6},{14,4},{1,11},{3,9}... | collective-permute-start | bytes 147464 | tf_op jit(solution)/shard_map/ppermute | solution.py:217
  29.0 7.2 %collective-permute-start.8 = (bf16[48,512]{1,0:T(8,128)(2,1)S(1)}, bf16[48,512]{1,0:T(8,128)(2,1)S(1)}, u32[]{:S(2)}, u32[]{:S(2)}) collective-permute-start(bf16[48,512]{1,0:T(8,128)(2,1)S(1)} %get-tuple-element.31), channel_id=1, source_target_pairs={{0,12},{2,14},{4,8},{6,10},{8,4},{10,6},{12,0},{14,2},{1,13},{3,15... | collective-permute-start | bytes 147464 | tf_op jit(solution)/shard_map/ppermute | solution.py:217
  32.7 6.8 %collective-permute-start.9 = (bf16[48,512]{1,0:T(8,128)(2,1)S(1)}, bf16[48,512]{1,0:T(8,128)(2,1)S(1)}, u32[]{:S(2)}, u32[]{:S(2)}) collective-permute-start(bf16[48,512]{1,0:T(8,128)(2,1)S(1)} %get-tuple-element.32), channel_id=1, source_target_pairs={{0,14},{2,12},{4,10},{6,8},{8,6},{10,4},{12,2},{14,0},{1,15},{3,13... | collective-permute-start | bytes 147464 | tf_op jit(solution)/shard_map/ppermute | solution.py:217
  41.2 1.4 %collective-permute-start.10 = (bf16[128,512]{1,0:T(8,128)(2,1)S(1)}, bf16[128,512]{1,0:T(8,128)(2,1)S(1)}, u32[]{:S(2)}, u32[]{:S(2)}) collective-permute-start(bf16[128,512]{1,0:T(8,128)(2,1)S(1)} %get-tuple-element.34), channel_id=1, source_target_pairs={{0,1},{1,0},{2,3},{3,2},{4,5},{5,4},{6,7},{7,6},{8,9},{9,8},{10,11... | collective-permute-start | bytes 393224 | tf_op jit(solution)/shard_map/ppermute | solution.py:263

commit v2 on v1

v2 whole, which is shorter than its diff:
```python
import functools

import jax
import jax.numpy as jnp
from jax import lax
from jax.experimental import pallas as pl
from jax.experimental.pallas import tpu as pltpu
from jax.sharding import PartitionSpec as P

MOST = 24
UNIT = 512
ROWS = 8
LANES = 128

BF16 = jnp.bfloat16
F32 = jnp.float32
NN = (((1,), (0,)), ((), ()))
NT = (((1,), (1,)), ((), ()))


def dot(a, b, dims=NN):
    return lax.dot_general(a, b, dims, preferred_element_type=F32)


def silu(v):
    t = 0.5 * v
    return t + t * jnp.tanh(t)


def iota(shape, dim):
    return lax.broadcasted_iota(jnp.int32, shape, dim)


def ones_where(mask):
    return jnp.where(mask, 1.0, 0.0).astype(BF16)


def head_sums(x, head_size):
    rows, cols = x.shape
    tall = jnp.concatenate([x[:, at : at + LANES] for at in range(0, cols, LANES)], axis=0)
    same = ones_where(iota((LANES, LANES), 0) // head_size == iota((LANES, LANES), 1) // head_size)
    high = tall.astype(BF16)
    low = (tall - high.astype(F32)).astype(BF16)
    sums = dot(high, same) + dot(low, same)
    return jnp.concatenate([sums[at : at + rows] for at in range(0, sums.shape[0], rows)], axis=1)


def request_at(position, lens_ref):
    end = lens_ref[0]
    request = jnp.where(position >= end, 1, 0)
    for r in range(1, lens_ref.shape[0]):
        end = end + lens_ref[r]
        request = request + jnp.where(position >= end, 1, 0)
    return request


def embed(tokens, levels, table):
    codes = table.shape[0] // levels
    lane = iota((tokens.shape[0], codes), 1).astype(F32)
    hot = jnp.concatenate([ones_where(lane == tokens[:, l : l + 1]) for l in range(levels)], axis=1)
    return dot(hot, table)


def normalize(embedded):
    width = embedded.shape[1]
    mean = jnp.sum(embedded, axis=1, keepdims=True) * (1.0 / width)
    centred = embedded - mean
    var = jnp.sum(centred * centred, axis=1, keepdims=True) * (1.0 / width)
    return (centred * lax.rsqrt(var + 1e-05)).astype(BF16)


def slot_queries(parts, levels, scale, me_ref, lens_ref, cand_ref, table_ref, wq_ref, slot_ref):
    owners, _, cand = cand_ref.shape
    first = me_ref[0] * parts * UNIT
    order = ones_where(iota((cand, cand), 0) <= iota((cand, cand), 1))
    slot = iota((MOST, cand), 0).astype(F32) + 1.0
    requests = jnp.concatenate([cand_ref[:, levels, :]] * parts, axis=0)
    line = iota(requests.shape, 0) // owners
    target = jnp.zeros(requests.shape, jnp.int32)
    for p in range(parts):
        target = jnp.where(line == p, request_at(first + p * UNIT, lens_ref), target)
    wanted = requests == target
    rank = jnp.where(wanted, dot(ones_where(wanted), order), 0.0)
    for k in range(owners):
        pick = jnp.concatenate(
            [ones_where(slot == rank[p * owners + k : p * owners + k + 1, :]) for p in range(parts)], axis=0
        )
        facts = dot(pick, cand_ref[k].astype(F32).astype(BF16), NT)
        for p in range(parts):
            at = (p * owners + k) * MOST
            slot_ref[at : at + MOST, :] = facts[p * MOST : (p + 1) * MOST]
    query = dot(normalize(embed(slot_ref[...], levels, table_ref[...])), wq_ref[...])
    return silu(query).astype(BF16) * BF16(scale)


def payload_kernel(cand_ref, out_ref):
    out_ref[...] = cand_ref[...]


def prepare_kernel(
    levels, heads, parts, me_ref, lens_ref, cand_ref, bucket_ref, bias_ref, table_ref,
    normed_ref, residual_ref, assign_ref, scale_ref, line_ref, next_ref,
):
    _, cand = cand_ref.shape
    eye = ones_where(iota((cand, cand), 0) == iota((cand, cand), 1))
    facts = dot(eye, cand_ref[...].astype(F32).astype(BF16), NT)
    embedded = embed(facts, levels, table_ref[...])
    half = embedded.shape[1] // 2
    residual_ref[...] = jnp.where(me_ref[1] == 1, embedded[:, half:], embedded[:, :half])
    normed_ref[...] = normalize(embedded)
    buckets = bias_ref.shape[1]
    hot = ones_where(iota((buckets, bucket_ref.shape[1]), 0) == bucket_ref[...])
    bias = bias_ref[...] * 0.5
    high = bias.astype(BF16)
    low = (bias - high.astype(F32)).astype(BF16)
    line_ref[...] = dot(high, hot) + dot(low, hot)
    request = facts[:, levels : levels + 1]
    other = cand_ref[levels : levels + 1, :].astype(F32)
    before = iota((cand, cand), 0) > iota((cand, cand), 1)
    rank = jnp.sum(jnp.where(jnp.logical_and(request == other, before), 1.0, 0.0), axis=1, keepdims=True)
    line = iota((1, assign_ref.shape[1]), 1)
    block = line // MOST
    owners = assign_ref.shape[1] // (parts * MOST)
    shard = jnp.bitwise_xor(owners - 1 - block // parts, me_ref[0])
    slot_request = request_at((shard * parts + block % parts) * UNIT, lens_ref).astype(F32)
    hit = jnp.logical_and(request == slot_request, rank == (line % MOST).astype(F32))
    assign_ref[...] = ones_where(hit)
    length = jnp.zeros((cand, 1), F32)
    for r in range(lens_ref.shape[0]):
        length = jnp.where(request == float(r), lens_ref[r].astype(F32), length)
    scale_ref[...] = jnp.broadcast_to(lax.rsqrt(length), scale_ref.shape)
    next_ref[...] = cand_ref[...]


def own_kernel(heads, cand_ref, bias_ref, normed_ref, win_ref, gate_ref, self_ref, wq_ref, next_ref):
    cols = win_ref.shape[2]
    head_size = cols // heads
    weights = jnp.swapaxes(win_ref[...], 0, 1)
    normed = normed_ref[...]
    wq_ref[...] = weights[1]
    gate_ref[...] = silu(dot(normed, weights[0]))
    query = silu(dot(normed, weights[1])).astype(BF16).astype(F32)
    self_key = silu(dot(normed, weights[2]))
    spread = jnp.where(iota((heads, cols), 0) == iota((heads, cols), 1) // head_size, 1.0, 0.0)
    first_bias = jnp.sum(spread * bias_ref[:, 0:1], axis=0, keepdims=True)
    score = head_sums(query * self_key, head_size) * head_size**-0.5 + first_bias
    self_ref[...] = silu(score) * silu(dot(normed, weights[3]))
    next_ref[...] = cand_ref[...]


def near_kernel(parts, levels, scale, me_ref, lens_ref, cand_ref, table_ref, wq_ref, query_ref, slot_ref):
    query_ref[...] = slot_queries(parts, levels, scale, me_ref, lens_ref, cand_ref, table_ref, wq_ref, slot_ref)


def attend_kernel(
    parts, levels, heads, stack, scale, me_ref, lens_ref, cand_ref, near_ref, line_ref, key_ref, value_ref, table_ref, wq_ref, *rest
):
    far_owners = cand_ref.shape[0]
    owners = 2 * far_owners
    outs, (slot_ref, result_ref) = rest[:owners], rest[owners:]
    far = slot_queries(parts, levels, scale, me_ref, lens_ref, cand_ref, table_ref, wq_ref, slot_ref)
    cols = key_ref.shape[1]
    head_size = cols // heads
    half = far_owners * MOST
    part_rows = owners * MOST
    wide = stack * head_size
    lane = iota((part_rows, wide), 1) // head_size
    for p in range(parts):
        rows = slice(p * UNIT, (p + 1) * UNIT)
        for g in range(heads // stack):
            at = slice(g * wide, (g + 1) * wide)
            part = jnp.concatenate(
                [near_ref[p * half : (p + 1) * half, at], far[p * half : (p + 1) * half, at]], axis=0
            )
            zero = jnp.zeros_like(part)
            stacked = jnp.concatenate([jnp.where(lane == i, part, zero) for i in range(stack)], axis=0)
            score = dot(stacked, key_ref[rows, at], NT)
            line = jnp.concatenate(
                [
                    jnp.broadcast_to(line_ref[stack * g + i : stack * g + i + 1, rows], (part_rows, UNIT))
                    for i in range(stack)
                ],
                axis=0,
            )
            t = score + line
            weight = (t + t * jnp.tanh(t)).astype(BF16)
            summed = dot(weight, value_ref[rows, at])
            kept = summed[:part_rows]
            for i in range(1, stack):
                kept = jnp.where(lane == i, summed[i * part_rows : (i + 1) * part_rows], kept)
            for k in range(owners):
                result_ref[k, p * MOST : (p + 1) * MOST, at] = kept[k * MOST : (k + 1) * MOST]
    for k in range(owners):
        outs[k][...] = result_ref[k].astype(BF16)


def finish_kernel(heads, me_ref, gate_ref, self_ref, assign_ref, scale_ref, residual_ref, wout_ref, *rest):
    received, (send_ref, keep_ref) = rest[:-2], rest[-2:]
    head_size = gate_ref.shape[1] // heads
    history = dot(assign_ref[...], jnp.concatenate([r[...] for r in received], axis=0))
    attended = history * scale_ref[:, 0:1] + self_ref[...]
    centred = attended - head_sums(attended, head_size) * (1.0 / head_size)
    var = head_sums(centred * centred, head_size) * (1.0 / head_size)
    mixed = (centred * lax.rsqrt(var + 1e-05) * gate_ref[...]).astype(BF16)
    half = wout_ref.shape[1] // 2
    projected = dot(mixed, wout_ref[...])
    second = me_ref[1] == 1
    send_ref[...] = jnp.where(second, projected[:, :half], projected[:, half:]).astype(BF16)
    keep_ref[...] = jnp.where(second, projected[:, half:], projected[:, :half]) + residual_ref[...]


def full(shape, dtype):
    return jax.ShapeDtypeStruct(shape, dtype)


def body(
    sem_tokens,
    cand_request,
    hist_lengths,
    hist_buckets,
    hist_keys,
    hist_values,
    code_table,
    proj_in,
    time_bias,
    proj_out,
):
    cand, levels = sem_tokens.shape
    hist, cols = hist_keys.shape
    heads = time_bias.shape[1]
    width = code_table.shape[1]
    owners = lax.axis_size("ctx")
    parts = hist // UNIT
    block = parts * MOST
    slots = owners * block
    stack = 4
    scale = 0.5 * (cols // heads) ** -0.5
    me = jnp.stack([lax.axis_index("ctx"), lax.axis_index("head")]).astype(jnp.int32)
    bias = time_bias.T
    smem = pl.BlockSpec(memory_space=pltpu.SMEM)
    vmem = pl.BlockSpec(memory_space=pltpu.VMEM)

    def swap(x, mask):
        return lax.ppermute(x, "ctx", [(i, i ^ mask) for i in range(owners)])

    def call(kernel, name, flops, out_shape, in_specs, scratch=(), cost=1 << 20):
        return pl.pallas_call(
            kernel,
            out_shape=out_shape,
            in_specs=in_specs,
            out_specs=jax.tree.map(lambda _: vmem, out_shape),
            scratch_shapes=scratch,
            compiler_params=pltpu.CompilerParams(vmem_limit_bytes=(8 + owners) << 20),
            cost_estimate=pl.CostEstimate(flops=flops, bytes_accessed=cost, transcendentals=0),
            name=name,
        )

    payload = jnp.concatenate(
        [sem_tokens.T, cand_request.T, jnp.zeros((ROWS - levels - 1, cand), jnp.int32)], axis=0
    )
    payload = call(
        payload_kernel, "payload", 9_000_000_000, full((ROWS, cand), jnp.int32), [vmem], cost=32 << 20
    )(payload)
    normed, residual, assign, lengths, line, payload_next = call(
        functools.partial(prepare_kernel, levels, heads, parts),
        "prepare",
        8_000_000_000,
        [
            full((cand, width), BF16),
            full((cand, width // 2), F32),
            full((cand, slots), BF16),
            full((cand, LANES), F32),
            full((heads, hist), F32),
            full((ROWS, cand), jnp.int32),
        ],
        [smem] * 2 + [vmem] * 4,
    )(me, hist_lengths, payload, hist_buckets.reshape(1, hist), bias, code_table)
    first = jnp.stack([payload_next, swap(payload, 1)])
    gate, self_term, wq, first_next = call(
        functools.partial(own_kernel, heads),
        "own",
        1_000_000_000,
        [full((cand, cols), F32)] * 2 + [full((width, cols), BF16), full((2, ROWS, cand), jnp.int32)],
        [vmem] * 4,
    )(first, bias, normed, proj_in)
    gathered = [first, jnp.concatenate([first_next, swap(first, 2)], axis=0)]
    bit = 4
    while bit < owners:
        gathered.append(jnp.concatenate([gathered[-1], swap(gathered[-1], bit)], axis=0))
        bit *= 2
    near_cand, far_cand = gathered[-2], gathered[-1][owners // 2 :]
    near = call(
        functools.partial(near_kernel, parts, levels, scale),
        "near",
        1_000_000_000,
        full((slots // 2, cols), BF16),
        [smem] * 2 + [vmem] * 3,
        [pltpu.VMEM((slots // 2, ROWS), F32)],
    )(me, hist_lengths, near_cand, code_table, wq)
    sent = call(
        functools.partial(attend_kernel, parts, levels, heads, stack, scale),
        "attend",
        3_000_000_000,
        [full((block, cols), BF16)] * owners,
        [smem] * 2 + [vmem] * 7,
        [
            pltpu.VMEM((slots // 2, ROWS), F32),
            pltpu.VMEM((owners, block, cols), F32),
        ],
    )(me, hist_lengths, far_cand, near, line, hist_keys, hist_values, code_table, wq)
    received = [swap(sent[m], m) for m in range(owners - 1, 0, -1)] + [sent[0]]
    send, keep = call(
        functools.partial(finish_kernel, heads),
        "finish",
        1_000_000_000,
        [full((cand, width // 2), BF16), full((cand, width // 2), F32)],
        [smem] + [vmem] * (6 + owners),
    )(me, gate, self_term, assign, lengths, residual, proj_out, *received)
    other = lax.ppermute(send, "head", [(0, 1), (1, 0)])
    return (keep + other.astype(F32)).astype(BF16)


def solution(mesh):
    in_specs = (
        P(("groups", "ctx"), None),
        P(("groups", "ctx"), None),
        P("groups"),
        P(("groups", "ctx")),
        P(("groups", "ctx"), "head"),
        P(("groups", "ctx"), "head"),
        P(),
        P(None, None, "head"),
        P(None, "head"),
        P("head", None),
    )
    out_specs = P(("groups", "ctx"), "head")
    return jax.shard_map(body, mesh=mesh, in_specs=in_specs, out_specs=out_specs, check_vma=False)
```

time: 43.5 us -> 36.8 us (0.85)
  local copies, waits for them, and re-layouts: 7.56 us -> 0.12 us
  waiting for transfers between devices: 6.71 us -> 5.03 us
  Pallas kernels: 8.8 us -> 10.4 us
  starting transfers between devices: 18.5 us -> 19.3 us
    unnamed x19 -> x17, local copies, waits for them, and re-layouts: 7.42 us -> 0.04 us
    ppermute x10, waiting for transfers between devices: 5.37 us -> 3.69 us  [swap(): return lax.ppermute(x, 'ctx', [(i, i ^ mask) for i in range(owners)])]
    pallas_call x3 -> x6, Pallas kernels: 8.8 us -> 10.4 us  [the longest x1 3.81 us: body(): call(functools.partial(attend_kernel, parts, levels, heads, stack, scale)...]
    ppermute x10, starting transfers between devices: 18.5 us -> 19.3 us  [swap(): return lax.ppermute(x, 'ctx', [(i, i ^ mask) for i in range(owners)])]
    broadcast_in_dim x1 -> x0, other arithmetic: 0.77 us -> none  [body(): gathered = payload[None]]
    concatenate x3 -> x1, other arithmetic: 0.01 us -> 0.77 us  [body(): jnp.concatenate([sem_tokens.T, cand_request.T, jnp.zeros((ROWS - levels -...]
  transfers between devices with their start and end apart: 11 -> 11, of which waited for: 4 -> 7; matrix products, arithmetic and copies ran while one was open for 7% -> 0% of each run, Pallas kernels for 6% -> 14%
where the time goes in v2:
time: 36.8 us; the launch traced here: 36.6 us
  starting transfers between devices  19.3 us (52%)
  Pallas kernels  10.4 us (28%)
  waiting for transfers between devices  5.03 us (14%)
  other arithmetic  1.53 us (4%)
    ppermute x10, starting transfers between devices, swap(): return lax.ppermute(x, 'ctx', [(i, i ^ mask) for i in range(owners)])  19.3 us
    pallas_call x1, Pallas kernels, body(): call(functools.partial(attend_kernel, parts, levels, heads, stack, scale)...  3.81 us
    ppermute x10, waiting for transfers between devices, swap(): return lax.ppermute(x, 'ctx', [(i, i ^ mask) for i in range(owners)])  3.69 us
    pallas_call x1, Pallas kernels, body(): call(functools.partial(near_kernel, parts, levels, scale), 'near', 100000...  1.98 us
    pallas_call x1, Pallas kernels, body(): call(functools.partial(own_kernel, heads), 'own', 1000000000, [full((cand...  1.76 us
    pallas_call x1, Pallas kernels, body(): call(functools.partial(finish_kernel, heads), 'finish', 1000000000, [full...  1.46 us
    pallas_call x1, Pallas kernels, body(): call(functools.partial(prepare_kernel, levels, heads, parts), 'prepare',...  1.39 us
    ppermute x1, waiting for transfers between devices, body(): other = lax.ppermute(send, 'head', [(0, 1), (1, 0)])  1.33 us
  transfers between devices with their start and end apart: 11, of which 7 were waited for; matrix products, arithmetic and copies ran while one was open for 0% of the time, Pallas kernels for 14%

profile of v2, /device:TPU:0, one launch (start us, length us, event | category | flops | bytes accessed | tf_op | source)
XLA Modules:
  0.0 36.6 jit_solution(4849262378110120364)
XLA Ops:
  0.0 0.1 pad.4.clone
  0.1 0.8 %add_add_fusion.cand_ref = s32[8,128]{1,0:T(8,128)S(1)} fusion(s32[1,128]{1,0:T(1,128)} %bitcast.14, s32[4,128]{1,0:T(4,128)} %bitcast.13, s32[8]{0:T(128)S(1)} %pad.4.clone), kind=kLoop, calls=%fused_computation.4 | loop fusion | flops 2048 | bytes 6688 | tf_op jit(solution)/shard_map/concatenate | solution.py:258
  0.9 3.0 %collective-permute-start = (s32[8,128]{1,0:T(8,128)S(1)}, s32[8,128]{1,0:T(8,128)S(1)}, u32[]{:S(2)}, u32[]{:S(2)}) collective-permute-start(s32[8,128]{1,0:T(8,128)S(1)} %payload.1.cand_ref), channel_id=1, source_target_pairs={{0,2},{2,0},{4,6},{6,4},{8,10},{10,8},{12,14},{14,12},{1,3},{3,1},... | collective-permute-start | bytes 12296 | tf_op jit(solution)/shard_map/ppermute | solution.py:244
  4.0 1.4 %prepare.1 = (bf16[128,1024]{1,0:T(8,128)(2,1)S(1)}, f32[128,512]{1,0:T(8,128)S(1)}, bf16[128,384]{1,0:T(8,128)(2,1)S(1)}, f32[128,128]{1,0:T(8,128)S(1)}, f32[8,1024]{1,0:T(8,128)S(1)}, /*index=5*/s32[8,128]{1,0:T(8,128)S(1)}) custom-call(s32[2]{0:T(128)S(1)} %pad_add_fusion.1.me_ref, s32[8]{0:T(128)S(1)} %copy-done.7, s32[8,128]{1,0:T(8,128)S(1)} %payload.1.cand_ref, ...), custom_call_target="tpu_custom_call" | custom-call | flops 8000000000 | bytes 1048576 | tf_op jit(solution)/shard_map/prepare/pallas_call | solution.py:264
  5.5 2.1 %collective-permute-start.1 = (s32[2,8,128]{2,1,0:T(8,128)S(1)}, s32[2,8,128]{2,1,0:T(8,128)S(1)}, u32[]{:S(2)}, u32[]{:S(2)}) collective-permute-start(s32[2,8,128]{2,1,0:T(8,128)S(1)} %pad_add_fusion.cand_ref), channel_id=1, source_target_pairs={{0,4},{2,6},{4,0},{6,2},{8,12},{10,14},{12,8},{14,10},{1,5},{3,7},... | collective-permute-start | bytes 24584 | tf_op jit(solution)/shard_map/ppermute | solution.py:244
  7.6 1.8 %own.1 = (f32[128,512]{1,0:T(8,128)S(1)}, f32[128,512]{1,0:T(8,128)S(1)}, bf16[1024,512]{1,0:T(8,128)(2,1)S(1)}, s32[2,8,128]{2,1,0:T(8,128)S(1)}) custom-call(s32[2,8,128]{2,1,0:T(8,128)S(1)} %pad_add_fusion.cand_ref, f32[8,128]{1,0:T(8,128)S(1)} %bitcast.9, bf16[128,1024]{1,0:T(8,128)(2,1)S(1)} %get-tuple-element.26.normed_ref, ...), custom_call_target="tpu_custom_call" | custom-call | flops 1000000000 | bytes 1048576 | tf_op jit(solution)/shard_map/own/pallas_call | solution.py:279
  9.4 2.9 %collective-permute-start.2 = (s32[4,8,128]{2,1,0:T(8,128)S(1)}, s32[4,8,128]{2,1,0:T(8,128)S(1)}, u32[]{:S(2)}, u32[]{:S(2)}) collective-permute-start(s32[4,8,128]{2,1,0:T(8,128)S(1)} %constant_dynamic-update-slice_fusion.cand_ref), channel_id=1, source_target_pairs={{0,8},{2,10},{4,12},{6,14},{8,0},{10,2},{12,4},{14,6},{1,9},{3,11}... | collective-permute-start | bytes 49160 | tf_op jit(solution)/shard_map/ppermute | solution.py:244
  12.2 2.0 %near.1.near_ref = bf16[192,512]{1,0:T(8,128)(2,1)S(1)} custom-call(s32[2]{0:T(128)S(1)} %pad_add_fusion.1.me_ref, s32[8]{0:T(128)S(1)} %copy-done.7, s32[4,8,128]{2,1,0:T(8,128)S(1)} %constant_dynamic-update-slice_fusion.cand_ref, bf16[1024,1024]{1,0:T(8,128)(2,1)S(1)} %copy-done.2, bf16[1024,512]{1,0:T(8,128)(2,1)S(1)} %get-tuple-element.33.wq_ref), custom_call_target="tpu_custom_call" | custom-call | flops 1000000000 | bytes 1048576 | tf_op jit(solution)/shard_map/near/pallas_call | solution.py:292
  14.3 3.8 %attend.1 = (bf16[48,512]{1,0:T(8,128)(2,1)S(1)}, bf16[48,512]{1,0:T(8,128)(2,1)S(1)}, bf16[48,512]{1,0:T(8,128)(2,1)S(1)}, bf16[48,512]{1,0:T(8,128)(2,1)S(1)},...) custom-call(s32[2]{0:T(128)S(1)} %pad_add_fusion.1.me_ref, ...), custom_call_target="tpu_custom_call" | custom-call | flops 3000000000 | bytes 1048576 | tf_op jit(solution)/shard_map/attend/pallas_call | solution.py:300
  18.1 4.7 %collective-permute-start.3 = (bf16[48,512]{1,0:T(8,128)(2,1)S(1)}, bf16[48,512]{1,0:T(8,128)(2,1)S(1)}, u32[]{:S(2)}, u32[]{:S(2)}) collective-permute-start(bf16[48,512]{1,0:T(8,128)(2,1)S(1)} %get-tuple-element.35), channel_id=1, source_target_pairs={{0,14},{2,12},{4,10},{6,8},{8,6},{10,4},{12,2},{14,0},{1,15},{3,13... | collective-permute-start | bytes 147464 | tf_op jit(solution)/shard_map/ppermute | solution.py:244
  22.8 0.2 collective-permute-start.4
  23.0 0.7 %collective-permute-start.5 = (bf16[48,512]{1,0:T(8,128)(2,1)S(1)}, bf16[48,512]{1,0:T(8,128)(2,1)S(1)}, u32[]{:S(2)}, u32[]{:S(2)}) collective-permute-start(bf16[48,512]{1,0:T(8,128)(2,1)S(1)} %get-tuple-element.37), channel_id=1, source_target_pairs={{0,10},{2,8},{4,14},{6,12},{8,2},{10,0},{12,6},{14,4},{1,11},{3,9}... | collective-permute-start | bytes 147464 | tf_op jit(solution)/shard_map/ppermute | solution.py:244
  23.7 2.1 %collective-permute-start.6 = (bf16[48,512]{1,0:T(8,128)(2,1)S(1)}, bf16[48,512]{1,0:T(8,128)(2,1)S(1)}, u32[]{:S(2)}, u32[]{:S(2)}) collective-permute-start(bf16[48,512]{1,0:T(8,128)(2,1)S(1)} %get-tuple-element.38), channel_id=1, source_target_pairs={{0,8},{2,10},{4,12},{6,14},{8,0},{10,2},{12,4},{14,6},{1,9},{3,11}... | collective-permute-start | bytes 147464 | tf_op jit(solution)/shard_map/ppermute | solution.py:244
  25.8 2.3 %collective-permute-start.7 = (bf16[48,512]{1,0:T(8,128)(2,1)S(1)}, bf16[48,512]{1,0:T(8,128)(2,1)S(1)}, u32[]{:S(2)}, u32[]{:S(2)}) collective-permute-start(bf16[48,512]{1,0:T(8,128)(2,1)S(1)} %get-tuple-element.39), channel_id=1, source_target_pairs={{0,6},{2,4},{4,2},{6,0},{8,14},{10,12},{12,10},{14,8},{1,7},{3,5},... | collective-permute-start | bytes 147464 | tf_op jit(solution)/shard_map/ppermute | solution.py:244
  28.1 0.7 %collective-permute-start.8 = (bf16[48,512]{1,0:T(8,128)(2,1)S(1)}, bf16[48,512]{1,0:T(8,128)(2,1)S(1)}, u32[]{:S(2)}, u32[]{:S(2)}) collective-permute-start(bf16[48,512]{1,0:T(8,128)(2,1)S(1)} %get-tuple-element.40), channel_id=1, source_target_pairs={{0,4},{2,6},{4,0},{6,2},{8,12},{10,14},{12,8},{14,10},{1,5},{3,7},... | collective-permute-start | bytes 147464 | tf_op jit(solution)/shard_map/ppermute | solution.py:244
  28.8 0.1 collective-permute-done.4.rest_1_
  28.9 0.6 %collective-permute-start.9 = (bf16[48,512]{1,0:T(8,128)(2,1)S(1)}, bf16[48,512]{1,0:T(8,128)(2,1)S(1)}, u32[]{:S(2)}, u32[]{:S(2)}) collective-permute-start(bf16[48,512]{1,0:T(8,128)(2,1)S(1)} %get-tuple-element.41), channel_id=1, source_target_pairs={{0,2},{2,0},{4,6},{6,4},{8,10},{10,8},{12,14},{14,12},{1,3},{3,1},... | collective-permute-start | bytes 147464 | tf_op jit(solution)/shard_map/ppermute | solution.py:244
  29.5 0.6 %collective-permute-done.6.rest_3_ = bf16[48,512]{1,0:T(8,128)(2,1)S(1)} collective-permute-done((bf16[48,512]{1,0:T(8,128)(2,1)S(1)}, bf16[48,512]{1,0:T(8,128)(2,1)S(1)}, u32[]{:S(2)}, u32[]{:S(2)}) %collective-permute-start.6) | collective-permute-done | bytes 49184 | tf_op jit(solution)/shard_map/ppermute | solution.py:244
  30.1 0.7 %collective-permute-done.7.rest_4_ = bf16[48,512]{1,0:T(8,128)(2,1)S(1)} collective-permute-done((bf16[48,512]{1,0:T(8,128)(2,1)S(1)}, bf16[48,512]{1,0:T(8,128)(2,1)S(1)}, u32[]{:S(2)}, u32[]{:S(2)}) %collective-permute-start.7) | collective-permute-done | bytes 49184 | tf_op jit(solution)/shard_map/ppermute | solution.py:244
  30.8 1.4 %collective-permute-done.8.rest_5_ = bf16[48,512]{1,0:T(8,128)(2,1)S(1)} collective-permute-done((bf16[48,512]{1,0:T(8,128)(2,1)S(1)}, bf16[48,512]{1,0:T(8,128)(2,1)S(1)}, u32[]{:S(2)}, u32[]{:S(2)}) %collective-permute-start.8) | collective-permute-done | bytes 49184 | tf_op jit(solution)/shard_map/ppermute | solution.py:244
  32.2 0.8 %collective-permute-done.9.rest_6_ = bf16[48,512]{1,0:T(8,128)(2,1)S(1)} collective-permute-done((bf16[48,512]{1,0:T(8,128)(2,1)S(1)}, bf16[48,512]{1,0:T(8,128)(2,1)S(1)}, u32[]{:S(2)}, u32[]{:S(2)}) %collective-permute-start.9) | collective-permute-done | bytes 49184 | tf_op jit(solution)/shard_map/ppermute | solution.py:244
  33.0 1.5 %finish.1 = (bf16[128,512]{1,0:T(8,128)(2,1)S(1)}, f32[128,512]{1,0:T(8,128)S(1)}) custom-call(s32[2]{0:T(128)S(1)} %pad_add_fusion.1.me_ref, f32[128,512]{1,0:T(8,128)S(1)} %get-tuple-element.27.gate_ref, f32[128,512]{1,0:T(8,128)S(1)} %get-tuple-element.28.self_ref, bf16[128,384]{1,0:T(8,128)(2,1)S(1)} %get-tuple-element.29.assign_ref, ...), custom_call_target="tpu_custom_call" | custom-call | flops 1000000000 | bytes 1048576 | tf_op jit(solution)/shard_map/finish/pallas_call | solution.py:312
  34.6 1.3 %collective-permute-done.10 = bf16[128,512]{1,0:T(8,128)(2,1)S(1)} collective-permute-done((bf16[128,512]{1,0:T(8,128)(2,1)S(1)}, bf16[128,512]{1,0:T(8,128)(2,1)S(1)}, u32[]{:S(2)}, u32[]{:S(2)}) %collective-permute-start.10) | collective-permute-done | bytes 131104 | tf_op jit(solution)/shard_map/ppermute | solution.py:319
  35.9 0.7 %add_convert_fusion = bf16[128,512]{1,0:T(8,128)(2,1)} fusion(f32[128,512]{1,0:T(8,128)S(1)} %get-tuple-element.43, bf16[128,512]{1,0:T(8,128)(2,1)S(1)} %collective-permute-done.10), kind=kLoop, calls=%fused_computation | loop fusion | flops 196608 | bytes 524288 | tf_op jit(solution)/shard_map/convert_element_type | solution.py:320
  (28 shorter events, 0.3 us)
Async XLA Ops:
  0.8 3.1 %copy-start.1 = (f32[128,8]{0,1:T(8,128)S(1)}, f32[128,8]{0,1:T(8,128)}, u32[]{:S(2)}) copy-start(f32[128,8]{0,1:T(8,128)} %param.18) | copy-start | bytes 12292
  0.8 3.1 %copy-start.2 = (bf16[1024,1024]{1,0:T(8,128)(2,1)S(1)}, bf16[1024,1024]{1,0:T(8,128)(2,1)}, u32[]{:S(2)}) copy-start(bf16[1024,1024]{1,0:T(8,128)(2,1)} %table_ref.5) | copy-start | bytes 6291460
  0.9 3.1 %copy-start.6 = (s32[1024]{0:T(1024)S(1)}, s32[1024]{0:T(1024)}, u32[]{:S(2)}) copy-start(s32[1024]{0:T(1024)} %param.13) | copy-start | bytes 12292
  0.9 3.1 %copy-start.7 = (s32[8]{0:T(128)S(1)}, s32[8]{0:T(128)}, u32[]{:S(2)}) copy-start(s32[8]{0:T(128)} %lens_ref.5) | copy-start | bytes 100
  0.9 4.6 %collective-permute-start = (s32[8,128]{1,0:T(8,128)S(1)}, s32[8,128]{1,0:T(8,128)S(1)}, u32[]{:S(2)}, u32[]{:S(2)}) collective-permute-start(s32[8,128]{1,0:T(8,128)S(1)} %payload.1.cand_ref), channel_id=1, source_target_pairs={{0,2},{2,0},{4,6},{6,4},{8,10},{10,8},{12,14},{14,12},{1,3},{3,1},... | collective-permute-start | bytes 12296 | tf_op jit(solution)/shard_map/ppermute | solution.py:244
  4.0 3.6 %copy-start = (bf16[1024,4,512]{2,1,0:T(4,128)(2,1)S(1)}, bf16[1024,4,512]{2,1,0:T(4,128)(2,1)}, u32[]{:S(2)}) copy-start(bf16[1024,4,512]{2,1,0:T(4,128)(2,1)} %win_ref.1) | copy-start | bytes 12582916
  5.4 8.8 %copy-start.3 = (bf16[1024,512]{1,0:T(8,128)(2,1)S(1)}, bf16[1024,512]{1,0:T(8,128)(2,1)}, u32[]{:S(2)}) copy-start(bf16[1024,512]{1,0:T(8,128)(2,1)} %key_ref.1) | copy-start | bytes 3145732
  5.4 8.8 %copy-start.4 = (bf16[1024,512]{1,0:T(8,128)(2,1)S(1)}, bf16[1024,512]{1,0:T(8,128)(2,1)}, u32[]{:S(2)}) copy-start(bf16[1024,512]{1,0:T(8,128)(2,1)} %value_ref.1) | copy-start | bytes 3145732
  5.5 3.9 %collective-permute-start.1 = (s32[2,8,128]{2,1,0:T(8,128)S(1)}, s32[2,8,128]{2,1,0:T(8,128)S(1)}, u32[]{:S(2)}, u32[]{:S(2)}) collective-permute-start(s32[2,8,128]{2,1,0:T(8,128)S(1)} %pad_add_fusion.cand_ref), channel_id=1, source_target_pairs={{0,4},{2,6},{4,0},{6,2},{8,12},{10,14},{12,8},{14,10},{1,5},{3,7},... | collective-permute-start | bytes 24584 | tf_op jit(solution)/shard_map/ppermute | solution.py:244
  9.4 4.9 %collective-permute-start.2 = (s32[4,8,128]{2,1,0:T(8,128)S(1)}, s32[4,8,128]{2,1,0:T(8,128)S(1)}, u32[]{:S(2)}, u32[]{:S(2)}) collective-permute-start(s32[4,8,128]{2,1,0:T(8,128)S(1)} %constant_dynamic-update-slice_fusion.cand_ref), channel_id=1, source_target_pairs={{0,8},{2,10},{4,12},{6,14},{8,0},{10,2},{12,4},{14,6},{1,9},{3,11}... | collective-permute-start | bytes 49160 | tf_op jit(solution)/shard_map/ppermute | solution.py:244
  14.3 18.8 %copy-start.5 = (bf16[512,1024]{1,0:T(8,128)(2,1)S(1)}, bf16[512,1024]{1,0:T(8,128)(2,1)}, u32[]{:S(2)}) copy-start(bf16[512,1024]{1,0:T(8,128)(2,1)} %wout_ref.1) | copy-start | bytes 3145732
  18.1 10.0 %collective-permute-start.3 = (bf16[48,512]{1,0:T(8,128)(2,1)S(1)}, bf16[48,512]{1,0:T(8,128)(2,1)S(1)}, u32[]{:S(2)}, u32[]{:S(2)}) collective-permute-start(bf16[48,512]{1,0:T(8,128)(2,1)S(1)} %get-tuple-element.35), channel_id=1, source_target_pairs={{0,14},{2,12},{4,10},{6,8},{8,6},{10,4},{12,2},{14,0},{1,15},{3,13... | collective-permute-start | bytes 147464 | tf_op jit(solution)/shard_map/ppermute | solution.py:244
  22.8 6.1 %collective-permute-start.4 = (bf16[48,512]{1,0:T(8,128)(2,1)S(1)}, bf16[48,512]{1,0:T(8,128)(2,1)S(1)}, u32[]{:S(2)}, u32[]{:S(2)}) collective-permute-start(bf16[48,512]{1,0:T(8,128)(2,1)S(1)} %get-tuple-element.36), channel_id=1, source_target_pairs={{0,12},{2,14},{4,8},{6,10},{8,4},{10,6},{12,0},{14,2},{1,13},{3,15... | collective-permute-start | bytes 147464 | tf_op jit(solution)/shard_map/ppermute | solution.py:244
  23.0 6.6 %collective-permute-start.5 = (bf16[48,512]{1,0:T(8,128)(2,1)S(1)}, bf16[48,512]{1,0:T(8,128)(2,1)S(1)}, u32[]{:S(2)}, u32[]{:S(2)}) collective-permute-start(bf16[48,512]{1,0:T(8,128)(2,1)S(1)} %get-tuple-element.37), channel_id=1, source_target_pairs={{0,10},{2,8},{4,14},{6,12},{8,2},{10,0},{12,6},{14,4},{1,11},{3,9}... | collective-permute-start | bytes 147464 | tf_op jit(solution)/shard_map/ppermute | solution.py:244
  23.7 6.4 %collective-permute-start.6 = (bf16[48,512]{1,0:T(8,128)(2,1)S(1)}, bf16[48,512]{1,0:T(8,128)(2,1)S(1)}, u32[]{:S(2)}, u32[]{:S(2)}) collective-permute-start(bf16[48,512]{1,0:T(8,128)(2,1)S(1)} %get-tuple-element.38), channel_id=1, source_target_pairs={{0,8},{2,10},{4,12},{6,14},{8,0},{10,2},{12,4},{14,6},{1,9},{3,11}... | collective-permute-start | bytes 147464 | tf_op jit(solution)/shard_map/ppermute | solution.py:244
  25.8 5.0 %collective-permute-start.7 = (bf16[48,512]{1,0:T(8,128)(2,1)S(1)}, bf16[48,512]{1,0:T(8,128)(2,1)S(1)}, u32[]{:S(2)}, u32[]{:S(2)}) collective-permute-start(bf16[48,512]{1,0:T(8,128)(2,1)S(1)} %get-tuple-element.39), channel_id=1, source_target_pairs={{0,6},{2,4},{4,2},{6,0},{8,14},{10,12},{12,10},{14,8},{1,7},{3,5},... | collective-permute-start | bytes 147464 | tf_op jit(solution)/shard_map/ppermute | solution.py:244
  28.1 4.1 %collective-permute-start.8 = (bf16[48,512]{1,0:T(8,128)(2,1)S(1)}, bf16[48,512]{1,0:T(8,128)(2,1)S(1)}, u32[]{:S(2)}, u32[]{:S(2)}) collective-permute-start(bf16[48,512]{1,0:T(8,128)(2,1)S(1)} %get-tuple-element.40), channel_id=1, source_target_pairs={{0,4},{2,6},{4,0},{6,2},{8,12},{10,14},{12,8},{14,10},{1,5},{3,7},... | collective-permute-start | bytes 147464 | tf_op jit(solution)/shard_map/ppermute | solution.py:244
  28.9 4.1 %collective-permute-start.9 = (bf16[48,512]{1,0:T(8,128)(2,1)S(1)}, bf16[48,512]{1,0:T(8,128)(2,1)S(1)}, u32[]{:S(2)}, u32[]{:S(2)}) collective-permute-start(bf16[48,512]{1,0:T(8,128)(2,1)S(1)} %get-tuple-element.41), channel_id=1, source_target_pairs={{0,2},{2,0},{4,6},{6,4},{8,10},{10,8},{12,14},{14,12},{1,3},{3,1},... | collective-permute-start | bytes 147464 | tf_op jit(solution)/shard_map/ppermute | solution.py:244
  34.5 1.4 %collective-permute-start.10 = (bf16[128,512]{1,0:T(8,128)(2,1)S(1)}, bf16[128,512]{1,0:T(8,128)(2,1)S(1)}, u32[]{:S(2)}, u32[]{:S(2)}) collective-permute-start(bf16[128,512]{1,0:T(8,128)(2,1)S(1)} %get-tuple-element.44), channel_id=1, source_target_pairs={{0,1},{1,0},{2,3},{3,2},{4,5},{5,4},{6,7},{7,6},{8,9},{9,8},{10,11... | collective-permute-start | bytes 393224 | tf_op jit(solution)/shard_map/ppermute | solution.py:319

commit v3 on v2

--- a/solution.py
+++ b/solution.py
@@ -132,12 +132,11 @@
     next_ref[...] = cand_ref[...]
 
 
-def own_kernel(heads, cand_ref, bias_ref, normed_ref, win_ref, gate_ref, self_ref, wq_ref, next_ref):
+def own_kernel(heads, sent_ref, bias_ref, normed_ref, win_ref, gate_ref, self_ref):
     cols = win_ref.shape[2]
     head_size = cols // heads
     weights = jnp.swapaxes(win_ref[...], 0, 1)
     normed = normed_ref[...]
-    wq_ref[...] = weights[1]
     gate_ref[...] = silu(dot(normed, weights[0]))
     query = silu(dot(normed, weights[1])).astype(BF16).astype(F32)
     self_key = silu(dot(normed, weights[2]))
@@ -145,10 +144,10 @@
     first_bias = jnp.sum(spread * bias_ref[:, 0:1], axis=0, keepdims=True)
     score = head_sums(query * self_key, head_size) * head_size**-0.5 + first_bias
     self_ref[...] = silu(score) * silu(dot(normed, weights[3]))
-    next_ref[...] = cand_ref[...]
-
-
-def near_kernel(parts, levels, scale, me_ref, lens_ref, cand_ref, table_ref, wq_ref, query_ref, slot_ref):
+
+
+def near_kernel(parts, levels, scale, me_ref, lens_ref, cand_ref, table_ref, win_ref, query_ref, wq_ref, slot_ref):
+    wq_ref[...] = jnp.swapaxes(win_ref[...], 0, 1)[1]
     query_ref[...] = slot_queries(parts, levels, scale, me_ref, lens_ref, cand_ref, table_ref, wq_ref, slot_ref)
 
 
@@ -275,28 +274,20 @@
         ],
         [smem] * 2 + [vmem] * 4,
     )(me, hist_lengths, payload, hist_buckets.reshape(1, hist), bias, code_table)
-    first = jnp.stack([payload_next, swap(payload, 1)])
-    gate, self_term, wq, first_next = call(
-        functools.partial(own_kernel, heads),
-        "own",
-        1_000_000_000,
-        [full((cand, cols), F32)] * 2 + [full((width, cols), BF16), full((2, ROWS, cand), jnp.int32)],
-        [vmem] * 4,
-    )(first, bias, normed, proj_in)
-    gathered = [first, jnp.concatenate([first_next, swap(first, 2)], axis=0)]
+    gathered = [jnp.stack([payload_next] + [swap(payload, m) for m in (3, 2, 1)][::-1])]
     bit = 4
     while bit < owners:
         gathered.append(jnp.concatenate([gathered[-1], swap(gathered[-1], bit)], axis=0))
         bit *= 2
     near_cand, far_cand = gathered[-2], gathered[-1][owners // 2 :]
-    near = call(
+    near, wq = call(
         functools.partial(near_kernel, parts, levels, scale),
         "near",
         1_000_000_000,
-        full((slots // 2, cols), BF16),
+        [full((slots // 2, cols), BF16), full((width, cols), BF16)],
         [smem] * 2 + [vmem] * 3,
         [pltpu.VMEM((slots // 2, ROWS), F32)],
-    )(me, hist_lengths, near_cand, code_table, wq)
+    )(me, hist_lengths, near_cand, code_table, proj_in)
     sent = call(
         functools.partial(attend_kernel, parts, levels, heads, stack, scale),
         "attend",
@@ -308,6 +299,13 @@
             pltpu.VMEM((owners, block, cols), F32),
         ],
     )(me, hist_lengths, far_cand, near, line, hist_keys, hist_values, code_table, wq)
+    gate, self_term = call(
+        functools.partial(own_kernel, heads),
+        "own",
+        1_000_000_000,
+        [full((cand, cols), F32)] * 2,
+        [vmem] * 4,
+    )(sent[0], bias, normed, proj_in)
     received = [swap(sent[m], m) for m in range(owners - 1, 0, -1)] + [sent[0]]
     send, keep = call(
         functools.partial(finish_kernel, heads),

time: 36.8 us -> 35.1 us (0.954)
  waiting for transfers between devices: 5.03 us -> 3.99 us
  starting transfers between devices: 19.3 us -> 18.5 us
    ppermute x10 -> x11, waiting for transfers between devices: 3.69 us -> 2.66 us  [swap(): return lax.ppermute(x, 'ctx', [(i, i ^ mask) for i in range(owners)])]
    ppermute x10 -> x11, starting transfers between devices: 19.3 us -> 18.5 us  [swap(): return lax.ppermute(x, 'ctx', [(i, i ^ mask) for i in range(owners)])]
  transfers between devices with their start and end apart: 11 -> 12, of which waited for: 7 -> 4; matrix products, arithmetic and copies ran while one was open for 0% -> 0% of each run, Pallas kernels for 14% -> 16%
where the time goes in v3:
time: 35.1 us; the launch traced here: 35 us
  starting transfers between devices  18.5 us (53%)
  Pallas kernels  10.6 us (30%)
  waiting for transfers between devices  3.99 us (11%)
  other arithmetic  1.53 us (4%)
    ppermute x11, starting transfers between devices, swap(): return lax.ppermute(x, 'ctx', [(i, i ^ mask) for i in range(owners)])  18.5 us
    pallas_call x1, Pallas kernels, body(): call(functools.partial(attend_kernel, parts, levels, heads, stack, scale)...  3.71 us
    ppermute x11, waiting for transfers between devices, swap(): return lax.ppermute(x, 'ctx', [(i, i ^ mask) for i in range(owners)])  2.66 us
    pallas_call x1, Pallas kernels, body(): call(functools.partial(near_kernel, parts, levels, scale), 'near', 100000...  2.27 us
    pallas_call x1, Pallas kernels, body(): call(functools.partial(own_kernel, heads), 'own', 1000000000, [full((cand...  1.77 us
    pallas_call x1, Pallas kernels, body(): call(functools.partial(finish_kernel, heads), 'finish', 1000000000, [full...  1.47 us
    pallas_call x1, Pallas kernels, body(): call(functools.partial(prepare_kernel, levels, heads, parts), 'prepare',...  1.38 us
    ppermute x1, waiting for transfers between devices, body(): other = lax.ppermute(send, 'head', [(0, 1), (1, 0)])  1.33 us
  transfers between devices with their start and end apart: 12, of which 4 were waited for; matrix products, arithmetic and copies ran while one was open for 0% of the time, Pallas kernels for 16%

profile of v3, /device:TPU:0, one launch (start us, length us, event | category | flops | bytes accessed | tf_op | source)
XLA Modules:
  0.0 35.0 jit_solution(12775074859390004223)
XLA Ops:
  0.0 0.1 pad.6.clone
  0.1 0.8 %add_add_fusion.cand_ref = s32[8,128]{1,0:T(8,128)S(1)} fusion(s32[1,128]{1,0:T(1,128)} %bitcast.18, s32[4,128]{1,0:T(4,128)} %bitcast.17, s32[8]{0:T(128)S(1)} %pad.6.clone), kind=kLoop, calls=%fused_computation.2 | loop fusion | flops 2048 | bytes 6688 | tf_op jit(solution)/shard_map/concatenate | solution.py:257
  0.9 4.0 %collective-permute-start.2 = (s32[8,128]{1,0:T(8,128)S(1)}, s32[8,128]{1,0:T(8,128)S(1)}, u32[]{:S(2)}, u32[]{:S(2)}) collective-permute-start(s32[8,128]{1,0:T(8,128)S(1)} %payload.1.cand_ref), channel_id=1, source_target_pairs={{0,6},{2,4},{4,2},{6,0},{8,14},{10,12},{12,10},{14,8},{1,7},{3,5},... | collective-permute-start | bytes 12296 | tf_op jit(solution)/shard_map/ppermute | solution.py:243
  4.9 0.4 %collective-permute-start.1 = (s32[8,128]{1,0:T(8,128)S(1)}, s32[8,128]{1,0:T(8,128)S(1)}, u32[]{:S(2)}, u32[]{:S(2)}) collective-permute-start(s32[8,128]{1,0:T(8,128)S(1)} %payload.1.cand_ref), channel_id=1, source_target_pairs={{0,4},{2,6},{4,0},{6,2},{8,12},{10,14},{12,8},{14,10},{1,5},{3,7},... | collective-permute-start | bytes 12296 | tf_op jit(solution)/shard_map/ppermute | solution.py:243
  5.4 0.2 collective-permute-start
  5.6 0.1 pad_add_fusion.1.me_ref
  5.7 1.4 %prepare.1 = (bf16[128,1024]{1,0:T(8,128)(2,1)S(1)}, f32[128,512]{1,0:T(8,128)S(1)}, bf16[128,384]{1,0:T(8,128)(2,1)S(1)}, f32[128,128]{1,0:T(8,128)S(1)}, f32[8,1024]{1,0:T(8,128)S(1)}, /*index=5*/s32[8,128]{1,0:T(8,128)S(1)}) custom-call(s32[2]{0:T(128)S(1)} %pad_add_fusion.1.me_ref, s32[8]{0:T(128)S(1)} %copy-done.3, s32[8,128]{1,0:T(8,128)S(1)} %payload.1.cand_ref, ...), custom_call_target="tpu_custom_call" | custom-call | flops 8000000000 | bytes 1048576 | tf_op jit(solution)/shard_map/prepare/pallas_call | solution.py:263
  7.1 1.4 %collective-permute-done.1 = s32[8,128]{1,0:T(8,128)S(1)} collective-permute-done((s32[8,128]{1,0:T(8,128)S(1)}, s32[8,128]{1,0:T(8,128)S(1)}, u32[]{:S(2)}, u32[]{:S(2)}) %collective-permute-start.1) | collective-permute-done | bytes 4128 | tf_op jit(solution)/shard_map/ppermute | solution.py:243
  8.5 0.4 %collective-permute-done = s32[8,128]{1,0:T(8,128)S(1)} collective-permute-done((s32[8,128]{1,0:T(8,128)S(1)}, s32[8,128]{1,0:T(8,128)S(1)}, u32[]{:S(2)}, u32[]{:S(2)}) %collective-permute-start) | collective-permute-done | bytes 4128 | tf_op jit(solution)/shard_map/ppermute | solution.py:243
  9.0 2.6 %collective-permute-start.3 = (s32[4,8,128]{2,1,0:T(8,128)S(1)}, s32[4,8,128]{2,1,0:T(8,128)S(1)}, u32[]{:S(2)}, u32[]{:S(2)}) collective-permute-start(s32[4,8,128]{2,1,0:T(8,128)S(1)} %pad_add_fusion.cand_ref), channel_id=1, source_target_pairs={{0,8},{2,10},{4,12},{6,14},{8,0},{10,2},{12,4},{14,6},{1,9},{3,11}... | collective-permute-start | bytes 49160 | tf_op jit(solution)/shard_map/ppermute | solution.py:243
  11.6 2.3 %near.1 = (bf16[192,512]{1,0:T(8,128)(2,1)S(1)}, bf16[1024,512]{1,0:T(8,128)(2,1)S(1)}) custom-call(s32[2]{0:T(128)S(1)} %pad_add_fusion.1.me_ref, s32[8]{0:T(128)S(1)} %copy-done.3, s32[4,8,128]{2,1,0:T(8,128)S(1)} %pad_add_fusion.cand_ref, bf16[1024,1024]{1,0:T(8,128)(2,1)S(1)} %copy-done.1, bf16[1024,4,512]{2,1,0:T(4,128)(2,1)S(1)} %copy-done), custom_call_target="tpu_custom_call" | custom-call | flops 1000000000 | bytes 1048576 | tf_op jit(solution)/shard_map/near/pallas_call | solution.py:283
  13.9 3.7 %attend.1 = (bf16[48,512]{1,0:T(8,128)(2,1)S(1)}, bf16[48,512]{1,0:T(8,128)(2,1)S(1)}, bf16[48,512]{1,0:T(8,128)(2,1)S(1)}, bf16[48,512]{1,0:T(8,128)(2,1)S(1)},...) custom-call(s32[2]{0:T(128)S(1)} %pad_add_fusion.1.me_ref, ...), custom_call_target="tpu_custom_call" | custom-call | flops 3000000000 | bytes 1048576 | tf_op jit(solution)/shard_map/attend/pallas_call | solution.py:291
  17.6 3.4 %collective-permute-start.4 = (bf16[48,512]{1,0:T(8,128)(2,1)S(1)}, bf16[48,512]{1,0:T(8,128)(2,1)S(1)}, u32[]{:S(2)}, u32[]{:S(2)}) collective-permute-start(bf16[48,512]{1,0:T(8,128)(2,1)S(1)} %get-tuple-element.36), channel_id=1, source_target_pairs={{0,14},{2,12},{4,10},{6,8},{8,6},{10,4},{12,2},{14,0},{1,15},{3,13... | collective-permute-start | bytes 147464 | tf_op jit(solution)/shard_map/ppermute | solution.py:243
  21.0 0.4 %collective-permute-start.5 = (bf16[48,512]{1,0:T(8,128)(2,1)S(1)}, bf16[48,512]{1,0:T(8,128)(2,1)S(1)}, u32[]{:S(2)}, u32[]{:S(2)}) collective-permute-start(bf16[48,512]{1,0:T(8,128)(2,1)S(1)} %get-tuple-element.37), channel_id=1, source_target_pairs={{0,12},{2,14},{4,8},{6,10},{8,4},{10,6},{12,0},{14,2},{1,13},{3,15... | collective-permute-start | bytes 147464 | tf_op jit(solution)/shard_map/ppermute | solution.py:243
  21.4 1.5 %collective-permute-start.6 = (bf16[48,512]{1,0:T(8,128)(2,1)S(1)}, bf16[48,512]{1,0:T(8,128)(2,1)S(1)}, u32[]{:S(2)}, u32[]{:S(2)}) collective-permute-start(bf16[48,512]{1,0:T(8,128)(2,1)S(1)} %get-tuple-element.38), channel_id=1, source_target_pairs={{0,10},{2,8},{4,14},{6,12},{8,2},{10,0},{12,6},{14,4},{1,11},{3,9}... | collective-permute-start | bytes 147464 | tf_op jit(solution)/shard_map/ppermute | solution.py:243
  22.9 2.4 %collective-permute-start.7 = (bf16[48,512]{1,0:T(8,128)(2,1)S(1)}, bf16[48,512]{1,0:T(8,128)(2,1)S(1)}, u32[]{:S(2)}, u32[]{:S(2)}) collective-permute-start(bf16[48,512]{1,0:T(8,128)(2,1)S(1)} %get-tuple-element.39), channel_id=1, source_target_pairs={{0,8},{2,10},{4,12},{6,14},{8,0},{10,2},{12,4},{14,6},{1,9},{3,11}... | collective-permute-start | bytes 147464 | tf_op jit(solution)/shard_map/ppermute | solution.py:243
  25.3 1.0 %collective-permute-start.8 = (bf16[48,512]{1,0:T(8,128)(2,1)S(1)}, bf16[48,512]{1,0:T(8,128)(2,1)S(1)}, u32[]{:S(2)}, u32[]{:S(2)}) collective-permute-start(bf16[48,512]{1,0:T(8,128)(2,1)S(1)} %get-tuple-element.40), channel_id=1, source_target_pairs={{0,6},{2,4},{4,2},{6,0},{8,14},{10,12},{12,10},{14,8},{1,7},{3,5},... | collective-permute-start | bytes 147464 | tf_op jit(solution)/shard_map/ppermute | solution.py:243
  26.4 0.9 %collective-permute-start.9 = (bf16[48,512]{1,0:T(8,128)(2,1)S(1)}, bf16[48,512]{1,0:T(8,128)(2,1)S(1)}, u32[]{:S(2)}, u32[]{:S(2)}) collective-permute-start(bf16[48,512]{1,0:T(8,128)(2,1)S(1)} %get-tuple-element.41), channel_id=1, source_target_pairs={{0,4},{2,6},{4,0},{6,2},{8,12},{10,14},{12,8},{14,10},{1,5},{3,7},... | collective-permute-start | bytes 147464 | tf_op jit(solution)/shard_map/ppermute | solution.py:243
  27.3 1.5 %collective-permute-start.10 = (bf16[48,512]{1,0:T(8,128)(2,1)S(1)}, bf16[48,512]{1,0:T(8,128)(2,1)S(1)}, u32[]{:S(2)}, u32[]{:S(2)}) collective-permute-start(bf16[48,512]{1,0:T(8,128)(2,1)S(1)} %get-tuple-element.42), channel_id=1, source_target_pairs={{0,2},{2,0},{4,6},{6,4},{8,10},{10,8},{12,14},{14,12},{1,3},{3,1},... | collective-permute-start | bytes 147464 | tf_op jit(solution)/shard_map/ppermute | solution.py:243
  28.8 1.8 %own.1 = (f32[128,512]{1,0:T(8,128)S(1)}, f32[128,512]{1,0:T(8,128)S(1)}) custom-call(bf16[48,512]{1,0:T(8,128)(2,1)S(1)} %get-tuple-element.29.sent_ref.rest_7_, f32[8,128]{1,0:T(8,128)S(1)} %bitcast.11, bf16[128,1024]{1,0:T(8,128)(2,1)S(1)} %get-tuple-element.30.normed_ref, bf16[1024,4,512]{2,1,0:T(4,128)(2,1)S(1)} %copy-done), custom_call_target="tpu_custom_call" | custom-call | flops 1000000000 | bytes 1048576 | tf_op jit(solution)/shard_map/own/pallas_call | solution.py:302
  30.6 0.8 %collective-permute-done.10.rest_6_ = bf16[48,512]{1,0:T(8,128)(2,1)S(1)} collective-permute-done((bf16[48,512]{1,0:T(8,128)(2,1)S(1)}, bf16[48,512]{1,0:T(8,128)(2,1)S(1)}, u32[]{:S(2)}, u32[]{:S(2)}) %collective-permute-start.10) | collective-permute-done | bytes 49184 | tf_op jit(solution)/shard_map/ppermute | solution.py:243
  31.4 1.5 %finish.1 = (bf16[128,512]{1,0:T(8,128)(2,1)S(1)}, f32[128,512]{1,0:T(8,128)S(1)}) custom-call(s32[2]{0:T(128)S(1)} %pad_add_fusion.1.me_ref, f32[128,512]{1,0:T(8,128)S(1)} %get-tuple-element.31.gate_ref, f32[128,512]{1,0:T(8,128)S(1)} %get-tuple-element.32.self_ref, bf16[128,384]{1,0:T(8,128)(2,1)S(1)} %get-tuple-element.33.assign_ref, ...), custom_call_target="tpu_custom_call" | custom-call | flops 1000000000 | bytes 1048576 | tf_op jit(solution)/shard_map/finish/pallas_call | solution.py:310
  33.0 1.3 %collective-permute-done.11 = bf16[128,512]{1,0:T(8,128)(2,1)S(1)} collective-permute-done((bf16[128,512]{1,0:T(8,128)(2,1)S(1)}, bf16[128,512]{1,0:T(8,128)(2,1)S(1)}, u32[]{:S(2)}, u32[]{:S(2)}) %collective-permute-start.11) | collective-permute-done | bytes 131104 | tf_op jit(solution)/shard_map/ppermute | solution.py:317
  34.3 0.7 %add_convert_fusion = bf16[128,512]{1,0:T(8,128)(2,1)} fusion(f32[128,512]{1,0:T(8,128)S(1)} %get-tuple-element.43, bf16[128,512]{1,0:T(8,128)(2,1)S(1)} %collective-permute-done.11), kind=kLoop, calls=%fused_computation | loop fusion | flops 196608 | bytes 524288 | tf_op jit(solution)/shard_map/convert_element_type | solution.py:318
  (28 shorter events, 0.1 us)
Async XLA Ops:
  0.8 4.8 %copy-start.1 = (bf16[1024,1024]{1,0:T(8,128)(2,1)S(1)}, bf16[1024,1024]{1,0:T(8,128)(2,1)}, u32[]{:S(2)}) copy-start(bf16[1024,1024]{1,0:T(8,128)(2,1)} %table_ref.5) | copy-start | bytes 6291460
  0.8 4.8 %copy-start.2 = (f32[128,8]{0,1:T(8,128)S(1)}, f32[128,8]{0,1:T(8,128)}, u32[]{:S(2)}) copy-start(f32[128,8]{0,1:T(8,128)} %param.18) | copy-start | bytes 12292
  0.9 4.8 %copy-start.3 = (s32[8]{0:T(128)S(1)}, s32[8]{0:T(128)}, u32[]{:S(2)}) copy-start(s32[8]{0:T(128)} %lens_ref.5) | copy-start | bytes 100
  0.9 4.8 %copy-start.7 = (s32[1024]{0:T(1024)S(1)}, s32[1024]{0:T(1024)}, u32[]{:S(2)}) copy-start(s32[1024]{0:T(1024)} %param.13) | copy-start | bytes 12292
  0.9 6.2 %collective-permute-start.2 = (s32[8,128]{1,0:T(8,128)S(1)}, s32[8,128]{1,0:T(8,128)S(1)}, u32[]{:S(2)}, u32[]{:S(2)}) collective-permute-start(s32[8,128]{1,0:T(8,128)S(1)} %payload.1.cand_ref), channel_id=1, source_target_pairs={{0,6},{2,4},{4,2},{6,0},{8,14},{10,12},{12,10},{14,8},{1,7},{3,5},... | collective-permute-start | bytes 12296 | tf_op jit(solution)/shard_map/ppermute | solution.py:243
  4.9 3.6 %collective-permute-start.1 = (s32[8,128]{1,0:T(8,128)S(1)}, s32[8,128]{1,0:T(8,128)S(1)}, u32[]{:S(2)}, u32[]{:S(2)}) collective-permute-start(s32[8,128]{1,0:T(8,128)S(1)} %payload.1.cand_ref), channel_id=1, source_target_pairs={{0,4},{2,6},{4,0},{6,2},{8,12},{10,14},{12,8},{14,10},{1,5},{3,7},... | collective-permute-start | bytes 12296 | tf_op jit(solution)/shard_map/ppermute | solution.py:243
  5.4 3.6 %collective-permute-start = (s32[8,128]{1,0:T(8,128)S(1)}, s32[8,128]{1,0:T(8,128)S(1)}, u32[]{:S(2)}, u32[]{:S(2)}) collective-permute-start(s32[8,128]{1,0:T(8,128)S(1)} %payload.1.cand_ref), channel_id=1, source_target_pairs={{0,2},{2,0},{4,6},{6,4},{8,10},{10,8},{12,14},{14,12},{1,3},{3,1},... | collective-permute-start | bytes 12296 | tf_op jit(solution)/shard_map/ppermute | solution.py:243
  5.6 5.9 %copy-start = (bf16[1024,4,512]{2,1,0:T(4,128)(2,1)S(1)}, bf16[1024,4,512]{2,1,0:T(4,128)(2,1)}, u32[]{:S(2)}) copy-start(bf16[1024,4,512]{2,1,0:T(4,128)(2,1)} %win_ref.3) | copy-start | bytes 12582916
  7.1 6.8 %copy-start.4 = (bf16[1024,512]{1,0:T(8,128)(2,1)S(1)}, bf16[1024,512]{1,0:T(8,128)(2,1)}, u32[]{:S(2)}) copy-start(bf16[1024,512]{1,0:T(8,128)(2,1)} %key_ref.1) | copy-start | bytes 3145732
  7.1 6.8 %copy-start.5 = (bf16[1024,512]{1,0:T(8,128)(2,1)S(1)}, bf16[1024,512]{1,0:T(8,128)(2,1)}, u32[]{:S(2)}) copy-start(bf16[1024,512]{1,0:T(8,128)(2,1)} %value_ref.1) | copy-start | bytes 3145732
  9.0 4.9 %collective-permute-start.3 = (s32[4,8,128]{2,1,0:T(8,128)S(1)}, s32[4,8,128]{2,1,0:T(8,128)S(1)}, u32[]{:S(2)}, u32[]{:S(2)}) collective-permute-start(s32[4,8,128]{2,1,0:T(8,128)S(1)} %pad_add_fusion.cand_ref), channel_id=1, source_target_pairs={{0,8},{2,10},{4,12},{6,14},{8,0},{10,2},{12,4},{14,6},{1,9},{3,11}... | collective-permute-start | bytes 49160 | tf_op jit(solution)/shard_map/ppermute | solution.py:243
  17.6 13.8 %copy-start.6 = (bf16[512,1024]{1,0:T(8,128)(2,1)S(1)}, bf16[512,1024]{1,0:T(8,128)(2,1)}, u32[]{:S(2)}) copy-start(bf16[512,1024]{1,0:T(8,128)(2,1)} %wout_ref.1) | copy-start | bytes 3145732
  17.6 8.8 %collective-permute-start.4 = (bf16[48,512]{1,0:T(8,128)(2,1)S(1)}, bf16[48,512]{1,0:T(8,128)(2,1)S(1)}, u32[]{:S(2)}, u32[]{:S(2)}) collective-permute-start(bf16[48,512]{1,0:T(8,128)(2,1)S(1)} %get-tuple-element.36), channel_id=1, source_target_pairs={{0,14},{2,12},{4,10},{6,8},{8,6},{10,4},{12,2},{14,0},{1,15},{3,13... | collective-permute-start | bytes 147464 | tf_op jit(solution)/shard_map/ppermute | solution.py:243
  21.0 6.3 %collective-permute-start.5 = (bf16[48,512]{1,0:T(8,128)(2,1)S(1)}, bf16[48,512]{1,0:T(8,128)(2,1)S(1)}, u32[]{:S(2)}, u32[]{:S(2)}) collective-permute-start(bf16[48,512]{1,0:T(8,128)(2,1)S(1)} %get-tuple-element.37), channel_id=1, source_target_pairs={{0,12},{2,14},{4,8},{6,10},{8,4},{10,6},{12,0},{14,2},{1,13},{3,15... | collective-permute-start | bytes 147464 | tf_op jit(solution)/shard_map/ppermute | solution.py:243
  21.4 9.2 %collective-permute-start.6 = (bf16[48,512]{1,0:T(8,128)(2,1)S(1)}, bf16[48,512]{1,0:T(8,128)(2,1)S(1)}, u32[]{:S(2)}, u32[]{:S(2)}) collective-permute-start(bf16[48,512]{1,0:T(8,128)(2,1)S(1)} %get-tuple-element.38), channel_id=1, source_target_pairs={{0,10},{2,8},{4,14},{6,12},{8,2},{10,0},{12,6},{14,4},{1,11},{3,9}... | collective-permute-start | bytes 147464 | tf_op jit(solution)/shard_map/ppermute | solution.py:243
  22.9 7.7 %collective-permute-start.7 = (bf16[48,512]{1,0:T(8,128)(2,1)S(1)}, bf16[48,512]{1,0:T(8,128)(2,1)S(1)}, u32[]{:S(2)}, u32[]{:S(2)}) collective-permute-start(bf16[48,512]{1,0:T(8,128)(2,1)S(1)} %get-tuple-element.39), channel_id=1, source_target_pairs={{0,8},{2,10},{4,12},{6,14},{8,0},{10,2},{12,4},{14,6},{1,9},{3,11}... | collective-permute-start | bytes 147464 | tf_op jit(solution)/shard_map/ppermute | solution.py:243
  25.3 5.3 %collective-permute-start.8 = (bf16[48,512]{1,0:T(8,128)(2,1)S(1)}, bf16[48,512]{1,0:T(8,128)(2,1)S(1)}, u32[]{:S(2)}, u32[]{:S(2)}) collective-permute-start(bf16[48,512]{1,0:T(8,128)(2,1)S(1)} %get-tuple-element.40), channel_id=1, source_target_pairs={{0,6},{2,4},{4,2},{6,0},{8,14},{10,12},{12,10},{14,8},{1,7},{3,5},... | collective-permute-start | bytes 147464 | tf_op jit(solution)/shard_map/ppermute | solution.py:243
  26.4 4.3 %collective-permute-start.9 = (bf16[48,512]{1,0:T(8,128)(2,1)S(1)}, bf16[48,512]{1,0:T(8,128)(2,1)S(1)}, u32[]{:S(2)}, u32[]{:S(2)}) collective-permute-start(bf16[48,512]{1,0:T(8,128)(2,1)S(1)} %get-tuple-element.41), channel_id=1, source_target_pairs={{0,4},{2,6},{4,0},{6,2},{8,12},{10,14},{12,8},{14,10},{1,5},{3,7},... | collective-permute-start | bytes 147464 | tf_op jit(solution)/shard_map/ppermute | solution.py:243
  27.3 4.1 %collective-permute-start.10 = (bf16[48,512]{1,0:T(8,128)(2,1)S(1)}, bf16[48,512]{1,0:T(8,128)(2,1)S(1)}, u32[]{:S(2)}, u32[]{:S(2)}) collective-permute-start(bf16[48,512]{1,0:T(8,128)(2,1)S(1)} %get-tuple-element.42), channel_id=1, source_target_pairs={{0,2},{2,0},{4,6},{6,4},{8,10},{10,8},{12,14},{14,12},{1,3},{3,1},... | collective-permute-start | bytes 147464 | tf_op jit(solution)/shard_map/ppermute | solution.py:243
  32.9 1.4 %collective-permute-start.11 = (bf16[128,512]{1,0:T(8,128)(2,1)S(1)}, bf16[128,512]{1,0:T(8,128)(2,1)S(1)}, u32[]{:S(2)}, u32[]{:S(2)}) collective-permute-start(bf16[128,512]{1,0:T(8,128)(2,1)S(1)} %get-tuple-element.44), channel_id=1, source_target_pairs={{0,1},{1,0},{2,3},{3,2},{4,5},{5,4},{6,7},{7,6},{8,9},{9,8},{10,11... | collective-permute-start | bytes 393224 | tf_op jit(solution)/shard_map/ppermute | solution.py:317

commit v4 on v3

--- a/solution.py
+++ b/solution.py
@@ -132,7 +132,9 @@
     next_ref[...] = cand_ref[...]
 
 
-def own_kernel(heads, sent_ref, bias_ref, normed_ref, win_ref, gate_ref, self_ref):
+def own_kernel(
+    heads, me_ref, sent_ref, bias_ref, normed_ref, win_ref, wout_ref, gate_ref, self_ref, mine_ref, other_ref
+):
     cols = win_ref.shape[2]
     head_size = cols // heads
     weights = jnp.swapaxes(win_ref[...], 0, 1)
@@ -144,23 +146,16 @@
     first_bias = jnp.sum(spread * bias_ref[:, 0:1], axis=0, keepdims=True)
     score = head_sums(query * self_key, head_size) * head_size**-0.5 + first_bias
     self_ref[...] = silu(score) * silu(dot(normed, weights[3]))
-
-
-def near_kernel(parts, levels, scale, me_ref, lens_ref, cand_ref, table_ref, win_ref, query_ref, wq_ref, slot_ref):
-    wq_ref[...] = jnp.swapaxes(win_ref[...], 0, 1)[1]
-    query_ref[...] = slot_queries(parts, levels, scale, me_ref, lens_ref, cand_ref, table_ref, wq_ref, slot_ref)
-
-
-def attend_kernel(
-    parts, levels, heads, stack, scale, me_ref, lens_ref, cand_ref, near_ref, line_ref, key_ref, value_ref, table_ref, wq_ref, *rest
-):
-    far_owners = cand_ref.shape[0]
-    owners = 2 * far_owners
-    outs, (slot_ref, result_ref) = rest[:owners], rest[owners:]
-    far = slot_queries(parts, levels, scale, me_ref, lens_ref, cand_ref, table_ref, wq_ref, slot_ref)
+    half = wout_ref.shape[1] // 2
+    low, high = wout_ref[:, :half], wout_ref[:, half:]
+    second = me_ref[1] == 1
+    mine_ref[...] = jnp.where(second, high, low)
+    other_ref[...] = jnp.where(second, low, high)
+
+
+def attend(parts, heads, stack, owners, query, line_ref, key_ref, value_ref, store):
     cols = key_ref.shape[1]
     head_size = cols // heads
-    half = far_owners * MOST
     part_rows = owners * MOST
     wide = stack * head_size
     lane = iota((part_rows, wide), 1) // head_size
@@ -168,9 +163,7 @@
         rows = slice(p * UNIT, (p + 1) * UNIT)
         for g in range(heads // stack):
             at = slice(g * wide, (g + 1) * wide)
-            part = jnp.concatenate(
-                [near_ref[p * half : (p + 1) * half, at], far[p * half : (p + 1) * half, at]], axis=0
-            )
+            part = query[p * part_rows : (p + 1) * part_rows, at]
             zero = jnp.zeros_like(part)
             stacked = jnp.concatenate([jnp.where(lane == i, part, zero) for i in range(stack)], axis=0)
             score = dot(stacked, key_ref[rows, at], NT)
@@ -188,24 +181,64 @@
             for i in range(1, stack):
                 kept = jnp.where(lane == i, summed[i * part_rows : (i + 1) * part_rows], kept)
             for k in range(owners):
-                result_ref[k, p * MOST : (p + 1) * MOST, at] = kept[k * MOST : (k + 1) * MOST]
+                store(k, p, at, kept[k * MOST : (k + 1) * MOST])
+
+
+def near_kernel(
+    parts, levels, heads, stack, scale,
+    me_ref, lens_ref, cand_ref, table_ref, win_ref, line_ref, key_ref, value_ref, *rest
+):
+    owners = cand_ref.shape[0]
+    outs, (wq_ref, slot_ref, result_ref) = rest[:owners], rest[owners:]
+    wq_ref[...] = jnp.swapaxes(win_ref[...], 0, 1)[1]
+    sums_of(
+        parts, levels, heads, stack, scale,
+        me_ref, lens_ref, cand_ref, table_ref, wq_ref, line_ref, key_ref, value_ref, outs, slot_ref, result_ref,
+    )
+
+
+def far_kernel(
+    parts, levels, heads, stack, scale,
+    me_ref, lens_ref, cand_ref, table_ref, wq_ref, line_ref, key_ref, value_ref, *rest
+):
+    owners = cand_ref.shape[0]
+    outs, (slot_ref, result_ref) = rest[:owners], rest[owners:]
+    sums_of(
+        parts, levels, heads, stack, scale,
+        me_ref, lens_ref, cand_ref, table_ref, wq_ref, line_ref, key_ref, value_ref, outs, slot_ref, result_ref,
+    )
+
+
+def sums_of(
+    parts, levels, heads, stack, scale,
+    me_ref, lens_ref, cand_ref, table_ref, wq_ref, line_ref, key_ref, value_ref, outs, slot_ref, result_ref,
+):
+    owners = cand_ref.shape[0]
+    query = slot_queries(parts, levels, scale, me_ref, lens_ref, cand_ref, table_ref, wq_ref, slot_ref)
+
+    def store(k, p, at, value):
+        result_ref[k, p * MOST : (p + 1) * MOST, at] = value
+
+    attend(parts, heads, stack, owners, query, line_ref, key_ref, value_ref, store)
     for k in range(owners):
         outs[k][...] = result_ref[k].astype(BF16)
 
 
-def finish_kernel(heads, me_ref, gate_ref, self_ref, assign_ref, scale_ref, residual_ref, wout_ref, *rest):
-    received, (send_ref, keep_ref) = rest[:-2], rest[-2:]
+def mix_kernel(heads, turns, gate_ref, self_ref, assign_ref, scale_ref, wout_ref, *rest):
+    received, (mixed_ref, send_ref) = rest[:-2], rest[-2:]
+    received = [received[turns.index(m)] for m in range(len(turns), 0, -1)] + [received[-1]]
     head_size = gate_ref.shape[1] // heads
     history = dot(assign_ref[...], jnp.concatenate([r[...] for r in received], axis=0))
     attended = history * scale_ref[:, 0:1] + self_ref[...]
     centred = attended - head_sums(attended, head_size) * (1.0 / head_size)
     var = head_sums(centred * centred, head_size) * (1.0 / head_size)
     mixed = (centred * lax.rsqrt(var + 1e-05) * gate_ref[...]).astype(BF16)
-    half = wout_ref.shape[1] // 2
-    projected = dot(mixed, wout_ref[...])
-    second = me_ref[1] == 1
-    send_ref[...] = jnp.where(second, projected[:, :half], projected[:, half:]).astype(BF16)
-    keep_ref[...] = jnp.where(second, projected[:, half:], projected[:, :half]) + residual_ref[...]
+    mixed_ref[...] = mixed
+    send_ref[...] = dot(mixed, wout_ref[...]).astype(BF16)
+
+
+def keep_kernel(mixed_ref, residual_ref, wout_ref, keep_ref):
+    keep_ref[...] = residual_ref[...] + dot(mixed_ref[...], wout_ref[...])
 
 
 def full(shape, dtype):
@@ -280,41 +313,45 @@
         gathered.append(jnp.concatenate([gathered[-1], swap(gathered[-1], bit)], axis=0))
         bit *= 2
     near_cand, far_cand = gathered[-2], gathered[-1][owners // 2 :]
-    near, wq = call(
-        functools.partial(near_kernel, parts, levels, scale),
+    half = owners // 2
+    scratch = [pltpu.VMEM((slots // 2, ROWS), F32), pltpu.VMEM((half, block, cols), F32)]
+    *near, wq = call(
+        functools.partial(near_kernel, parts, levels, heads, stack, scale),
         "near",
         1_000_000_000,
-        [full((slots // 2, cols), BF16), full((width, cols), BF16)],
-        [smem] * 2 + [vmem] * 3,
-        [pltpu.VMEM((slots // 2, ROWS), F32)],
-    )(me, hist_lengths, near_cand, code_table, proj_in)
-    sent = call(
-        functools.partial(attend_kernel, parts, levels, heads, stack, scale),
-        "attend",
+        [full((block, cols), BF16)] * half + [full((width, cols), BF16)],
+        [smem] * 2 + [vmem] * 6,
+        scratch,
+    )(me, hist_lengths, near_cand, code_table, proj_in, line, hist_keys, hist_values)
+    far = call(
+        functools.partial(far_kernel, parts, levels, heads, stack, scale),
+        "far",
         3_000_000_000,
-        [full((block, cols), BF16)] * owners,
-        [smem] * 2 + [vmem] * 7,
-        [
-            pltpu.VMEM((slots // 2, ROWS), F32),
-            pltpu.VMEM((owners, block, cols), F32),
-        ],
-    )(me, hist_lengths, far_cand, near, line, hist_keys, hist_values, code_table, wq)
-    gate, self_term = call(
+        [full((block, cols), BF16)] * half,
+        [smem] * 2 + [vmem] * 6,
+        scratch,
+    )(me, hist_lengths, far_cand, code_table, wq, line, hist_keys, hist_values)
+    sent = list(lax.optimization_barrier(tuple(near) + tuple(far)))
+    gate, self_term, wout_mine, wout_other = call(
         functools.partial(own_kernel, heads),
         "own",
         1_000_000_000,
-        [full((cand, cols), F32)] * 2,
-        [vmem] * 4,
-    )(sent[0], bias, normed, proj_in)
-    received = [swap(sent[m], m) for m in range(owners - 1, 0, -1)] + [sent[0]]
-    send, keep = call(
-        functools.partial(finish_kernel, heads),
-        "finish",
+        [full((cand, cols), F32)] * 2 + [full((cols, width // 2), BF16)] * 2,
+        [smem] + [vmem] * 5,
+    )(me, sent[0], bias, normed, proj_in, proj_out)
+    turns = [4, 7, 6, 5, 3, 2, 1] if owners == 8 else list(range(owners - 1, 0, -1))
+    received = [swap(sent[m], m) for m in turns] + [sent[0]]
+    mixed, send = call(
+        functools.partial(mix_kernel, heads, turns),
+        "mix",
         1_000_000_000,
-        [full((cand, width // 2), BF16), full((cand, width // 2), F32)],
-        [smem] + [vmem] * (6 + owners),
-    )(me, gate, self_term, assign, lengths, residual, proj_out, *received)
+        [full((cand, cols), BF16), full((cand, width // 2), BF16)],
+        [vmem] * (5 + owners),
+    )(gate, self_term, assign, lengths, wout_other, *received)
     other = lax.ppermute(send, "head", [(0, 1), (1, 0)])
+    keep = call(keep_kernel, "keep", 1_000_000, full((cand, width // 2), F32), [vmem] * 3)(
+        mixed, residual, wout_mine
+    )
     return (keep + other.astype(F32)).astype(BF16)
 
 

time: 35.1 us -> 34.3 us (0.977)
  waiting for transfers between devices: 3.99 us -> 3.11 us
  Pallas kernels: 10.6 us -> 11 us
    pallas_call x1, Pallas kernels: 1.77 us -> 2.42 us  [body(): call(functools.partial(own_kernel, heads), 'own', 1000000000, [full((cand...]
    ppermute x11, waiting for transfers between devices: 2.66 us -> 2.01 us  [swap(): return lax.ppermute(x, 'ctx', [(i, i ^ mask) for i in range(owners)])]
    ppermute x11, starting transfers between devices: 18.5 us -> 18.1 us  [swap(): return lax.ppermute(x, 'ctx', [(i, i ^ mask) for i in range(owners)])]
    pallas_call x3 -> x4, Pallas kernels: 7.45 us -> 7.23 us  [the longest x1 3.24 us: body(): call(functools.partial(near_kernel, parts, levels, heads, stack, scale),...]
  transfers between devices with their start and end apart: 12 -> 12, of which waited for: 4 -> 4; matrix products, arithmetic and copies ran while one was open for 0% -> 0% of each run, Pallas kernels for 16% -> 21%
where the time goes in v4:
time: 34.3 us; the launch traced here: 34.1 us
  starting transfers between devices  18.2 us (53%)
  Pallas kernels  11 us (32%)
  waiting for transfers between devices  3.11 us (9%)
  other arithmetic  1.53 us (4%)
    ppermute x11, starting transfers between devices, swap(): return lax.ppermute(x, 'ctx', [(i, i ^ mask) for i in range(owners)])  18.1 us
    pallas_call x1, Pallas kernels, body(): call(functools.partial(near_kernel, parts, levels, heads, stack, scale),...  3.24 us
    pallas_call x1, Pallas kernels, body(): call(functools.partial(far_kernel, parts, levels, heads, stack, scale), '...  2.92 us
    pallas_call x1, Pallas kernels, body(): call(functools.partial(own_kernel, heads), 'own', 1000000000, [full((cand...  2.42 us
    ppermute x11, waiting for transfers between devices, swap(): return lax.ppermute(x, 'ctx', [(i, i ^ mask) for i in range(owners)])  2.01 us
    pallas_call x1, Pallas kernels, body(): call(functools.partial(prepare_kernel, levels, heads, parts), 'prepare',...  1.38 us
    ppermute x1, waiting for transfers between devices, body(): other = lax.ppermute(send, 'head', [(0, 1), (1, 0)])  1.1 us
    pallas_call x1, Pallas kernels, body(): call(functools.partial(mix_kernel, heads, turns), 'mix', 1000000000, [ful...  0.83 us
  transfers between devices with their start and end apart: 12, of which 4 were waited for; matrix products, arithmetic and copies ran while one was open for 0% of the time, Pallas kernels for 21%

profile of v4, /device:TPU:0, one launch (start us, length us, event | category | flops | bytes accessed | tf_op | source)
XLA Modules:
  0.0 34.1 jit_solution(7039194116007183125)
XLA Ops:
  0.0 0.1 pad.6.clone
  0.1 0.8 %add_add_fusion.cand_ref = s32[8,128]{1,0:T(8,128)S(1)} fusion(s32[1,128]{1,0:T(1,128)} %bitcast.18, s32[4,128]{1,0:T(4,128)} %bitcast.17, s32[8]{0:T(128)S(1)} %pad.6.clone), kind=kLoop, calls=%fused_computation.2 | loop fusion | flops 2048 | bytes 6688 | tf_op jit(solution)/shard_map/concatenate | solution.py:290
  0.9 4.0 %collective-permute-start.2 = (s32[8,128]{1,0:T(8,128)S(1)}, s32[8,128]{1,0:T(8,128)S(1)}, u32[]{:S(2)}, u32[]{:S(2)}) collective-permute-start(s32[8,128]{1,0:T(8,128)S(1)} %payload.1.cand_ref), channel_id=1, source_target_pairs={{0,6},{2,4},{4,2},{6,0},{8,14},{10,12},{12,10},{14,8},{1,7},{3,5},... | collective-permute-start | bytes 12296 | tf_op jit(solution)/shard_map/ppermute | solution.py:276
  4.9 0.4 %collective-permute-start.1 = (s32[8,128]{1,0:T(8,128)S(1)}, s32[8,128]{1,0:T(8,128)S(1)}, u32[]{:S(2)}, u32[]{:S(2)}) collective-permute-start(s32[8,128]{1,0:T(8,128)S(1)} %payload.1.cand_ref), channel_id=1, source_target_pairs={{0,4},{2,6},{4,0},{6,2},{8,12},{10,14},{12,8},{14,10},{1,5},{3,7},... | collective-permute-start | bytes 12296 | tf_op jit(solution)/shard_map/ppermute | solution.py:276
  5.4 0.2 collective-permute-start
  5.6 0.1 pad_add_fusion.1.me_ref
  5.7 1.4 %prepare.1 = (bf16[128,1024]{1,0:T(8,128)(2,1)S(1)}, f32[128,512]{1,0:T(8,128)S(1)}, bf16[128,384]{1,0:T(8,128)(2,1)S(1)}, f32[128,128]{1,0:T(8,128)S(1)}, f32[8,1024]{1,0:T(8,128)S(1)}, /*index=5*/s32[8,128]{1,0:T(8,128)S(1)}) custom-call(s32[2]{0:T(128)S(1)} %pad_add_fusion.1.me_ref, s32[8]{0:T(128)S(1)} %copy-done.6, s32[8,128]{1,0:T(8,128)S(1)} %payload.1.cand_ref, ...), custom_call_target="tpu_custom_call" | custom-call | flops 8000000000 | bytes 1048576 | tf_op jit(solution)/shard_map/prepare/pallas_call | solution.py:296
  7.1 1.4 %collective-permute-done.1 = s32[8,128]{1,0:T(8,128)S(1)} collective-permute-done((s32[8,128]{1,0:T(8,128)S(1)}, s32[8,128]{1,0:T(8,128)S(1)}, u32[]{:S(2)}, u32[]{:S(2)}) %collective-permute-start.1) | collective-permute-done | bytes 4128 | tf_op jit(solution)/shard_map/ppermute | solution.py:276
  8.5 0.4 %collective-permute-done = s32[8,128]{1,0:T(8,128)S(1)} collective-permute-done((s32[8,128]{1,0:T(8,128)S(1)}, s32[8,128]{1,0:T(8,128)S(1)}, u32[]{:S(2)}, u32[]{:S(2)}) %collective-permute-start) | collective-permute-done | bytes 4128 | tf_op jit(solution)/shard_map/ppermute | solution.py:276
  9.0 2.6 %collective-permute-start.3 = (s32[4,8,128]{2,1,0:T(8,128)S(1)}, s32[4,8,128]{2,1,0:T(8,128)S(1)}, u32[]{:S(2)}, u32[]{:S(2)}) collective-permute-start(s32[4,8,128]{2,1,0:T(8,128)S(1)} %pad_add_fusion.cand_ref), channel_id=1, source_target_pairs={{0,8},{2,10},{4,12},{6,14},{8,0},{10,2},{12,4},{14,6},{1,9},{3,11}... | collective-permute-start | bytes 49160 | tf_op jit(solution)/shard_map/ppermute | solution.py:276
  11.6 3.2 %near.1 = (bf16[48,512]{1,0:T(8,128)(2,1)S(1)}, bf16[48,512]{1,0:T(8,128)(2,1)S(1)}, bf16[48,512]{1,0:T(8,128)(2,1)S(1)}, bf16[48,512]{1,0:T(8,128)(2,1)S(1)}, bf16[1024,512]{1,0:T(8,128)(2,1)S(1)}) custom-call(s32[2]{0:T(128)S(1)} %pad_add_fusion.1.me_ref, s32[8]{0:T(128)S(1)} %copy-done.6, s32[4,8,128]{2,1,0:T(8,128)S(1)} %pad_add_fusion.cand_ref, ...), custom_call_target="tpu_custom_call" | custom-call | flops 1000000000 | bytes 1048576 | tf_op jit(solution)/shard_map/near/pallas_call | solution.py:318
  14.8 2.9 %far.1 = (bf16[48,512]{1,0:T(8,128)(2,1)S(1)}, bf16[48,512]{1,0:T(8,128)(2,1)S(1)}, bf16[48,512]{1,0:T(8,128)(2,1)S(1)}, bf16[48,512]{1,0:T(8,128)(2,1)S(1)}) custom-call(s32[2]{0:T(128)S(1)} %pad_add_fusion.1.me_ref, s32[8]{0:T(128)S(1)} %copy-done.6, s32[4,8,128]{2,1,0:T(8,128)S(1)} %collective-permute-done.3.cand_ref, bf16[1024,1024]{1,0:T(8,128)(2,1)S(1)} %copy-done.1, ...), custom_call_target="tpu_custom_call" | custom-call | flops 3000000000 | bytes 1048576 | tf_op jit(solution)/shard_map/far/pallas_call | solution.py:326
  17.8 1.4 %collective-permute-start.4 = (bf16[48,512]{1,0:T(8,128)(2,1)S(1)}, bf16[48,512]{1,0:T(8,128)(2,1)S(1)}, u32[]{:S(2)}, u32[]{:S(2)}) collective-permute-start(bf16[48,512]{1,0:T(8,128)(2,1)S(1)} %get-tuple-element.52), channel_id=1, source_target_pairs={{0,8},{2,10},{4,12},{6,14},{8,0},{10,2},{12,4},{14,6},{1,9},{3,11}... | collective-permute-start | bytes 147464 | tf_op jit(solution)/shard_map/ppermute | solution.py:276
  19.2 2.5 %collective-permute-start.5 = (bf16[48,512]{1,0:T(8,128)(2,1)S(1)}, bf16[48,512]{1,0:T(8,128)(2,1)S(1)}, u32[]{:S(2)}, u32[]{:S(2)}) collective-permute-start(bf16[48,512]{1,0:T(8,128)(2,1)S(1)} %get-tuple-element.53), channel_id=1, source_target_pairs={{0,14},{2,12},{4,10},{6,8},{8,6},{10,4},{12,2},{14,0},{1,15},{3,13... | collective-permute-start | bytes 147464 | tf_op jit(solution)/shard_map/ppermute | solution.py:276
  21.7 1.3 %collective-permute-start.6 = (bf16[48,512]{1,0:T(8,128)(2,1)S(1)}, bf16[48,512]{1,0:T(8,128)(2,1)S(1)}, u32[]{:S(2)}, u32[]{:S(2)}) collective-permute-start(bf16[48,512]{1,0:T(8,128)(2,1)S(1)} %get-tuple-element.54), channel_id=1, source_target_pairs={{0,12},{2,14},{4,8},{6,10},{8,4},{10,6},{12,0},{14,2},{1,13},{3,15... | collective-permute-start | bytes 147464 | tf_op jit(solution)/shard_map/ppermute | solution.py:276
  23.0 0.7 %collective-permute-start.7 = (bf16[48,512]{1,0:T(8,128)(2,1)S(1)}, bf16[48,512]{1,0:T(8,128)(2,1)S(1)}, u32[]{:S(2)}, u32[]{:S(2)}) collective-permute-start(bf16[48,512]{1,0:T(8,128)(2,1)S(1)} %get-tuple-element.55), channel_id=1, source_target_pairs={{0,10},{2,8},{4,14},{6,12},{8,2},{10,0},{12,6},{14,4},{1,11},{3,9}... | collective-permute-start | bytes 147464 | tf_op jit(solution)/shard_map/ppermute | solution.py:276
  23.7 3.3 %collective-permute-start.8 = (bf16[48,512]{1,0:T(8,128)(2,1)S(1)}, bf16[48,512]{1,0:T(8,128)(2,1)S(1)}, u32[]{:S(2)}, u32[]{:S(2)}) collective-permute-start(bf16[48,512]{1,0:T(8,128)(2,1)S(1)} %get-tuple-element.56), channel_id=1, source_target_pairs={{0,6},{2,4},{4,2},{6,0},{8,14},{10,12},{12,10},{14,8},{1,7},{3,5},... | collective-permute-start | bytes 147464 | tf_op jit(solution)/shard_map/ppermute | solution.py:276
  27.1 1.5 %collective-permute-start.10 = (bf16[48,512]{1,0:T(8,128)(2,1)S(1)}, bf16[48,512]{1,0:T(8,128)(2,1)S(1)}, u32[]{:S(2)}, u32[]{:S(2)}) collective-permute-start(bf16[48,512]{1,0:T(8,128)(2,1)S(1)} %get-tuple-element.58), channel_id=1, source_target_pairs={{0,2},{2,0},{4,6},{6,4},{8,10},{10,8},{12,14},{14,12},{1,3},{3,1},... | collective-permute-start | bytes 147464 | tf_op jit(solution)/shard_map/ppermute | solution.py:276
  28.6 2.4 %own.1 = (f32[128,512]{1,0:T(8,128)S(1)}, f32[128,512]{1,0:T(8,128)S(1)}, bf16[512,512]{1,0:T(8,128)(2,1)S(1)}, bf16[512,512]{1,0:T(8,128)(2,1)S(1)}) custom-call(s32[2]{0:T(128)S(1)} %pad_add_fusion.1.me_ref, bf16[48,512]{1,0:T(8,128)(2,1)S(1)} %get-tuple-element.45.sent_ref.rest_7_, f32[8,128]{1,0:T(8,128)S(1)} %bitcast.11, ...), custom_call_target="tpu_custom_call" | custom-call | flops 1000000000 | bytes 1048576 | tf_op jit(solution)/shard_map/own/pallas_call | solution.py:335
  31.1 0.1 collective-permute-done.10.rest_6_
  31.2 0.8 %mix.1 = (bf16[128,512]{1,0:T(8,128)(2,1)S(1)}, bf16[128,512]{1,0:T(8,128)(2,1)S(1)}) custom-call(f32[128,512]{1,0:T(8,128)S(1)} %get-tuple-element.47.gate_ref, f32[128,512]{1,0:T(8,128)S(1)} %get-tuple-element.48.self_ref, bf16[128,384]{1,0:T(8,128)(2,1)S(1)} %get-tuple-element.49.assign_ref, f32[128,128]{1,0:T(8,128)S(1)} %get-tuple-element.50.scale_ref, ...), custom_call_target="tpu_custom_call" | custom-call | flops 1000000000 | bytes 1048576 | tf_op jit(solution)/shard_map/mix/pallas_call | solution.py:344
  32.1 0.2 keep.1
  32.3 1.1 %collective-permute-done.11 = bf16[128,512]{1,0:T(8,128)(2,1)S(1)} collective-permute-done((bf16[128,512]{1,0:T(8,128)(2,1)S(1)}, bf16[128,512]{1,0:T(8,128)(2,1)S(1)}, u32[]{:S(2)}, u32[]{:S(2)}) %collective-permute-start.11) | collective-permute-done | bytes 131104 | tf_op jit(solution)/shard_map/ppermute | solution.py:351
  33.4 0.7 %add_convert_fusion = bf16[128,512]{1,0:T(8,128)(2,1)} fusion(f32[128,512]{1,0:T(8,128)S(1)} %keep.1, bf16[128,512]{1,0:T(8,128)(2,1)S(1)} %collective-permute-done.11), kind=kLoop, calls=%fused_computation | loop fusion | flops 196608 | bytes 524288 | tf_op jit(solution)/shard_map/convert_element_type | solution.py:355
  (29 shorter events, 0.2 us)
Async XLA Ops:
  0.8 4.8 %copy-start.1 = (bf16[1024,1024]{1,0:T(8,128)(2,1)S(1)}, bf16[1024,1024]{1,0:T(8,128)(2,1)}, u32[]{:S(2)}) copy-start(bf16[1024,1024]{1,0:T(8,128)(2,1)} %table_ref.5) | copy-start | bytes 6291460
  0.8 4.8 %copy-start.5 = (f32[128,8]{0,1:T(8,128)S(1)}, f32[128,8]{0,1:T(8,128)}, u32[]{:S(2)}) copy-start(f32[128,8]{0,1:T(8,128)} %param.18) | copy-start | bytes 12292
  0.9 4.8 %copy-start.6 = (s32[8]{0:T(128)S(1)}, s32[8]{0:T(128)}, u32[]{:S(2)}) copy-start(s32[8]{0:T(128)} %lens_ref.5) | copy-start | bytes 100
  0.9 4.8 %copy-start.7 = (s32[1024]{0:T(1024)S(1)}, s32[1024]{0:T(1024)}, u32[]{:S(2)}) copy-start(s32[1024]{0:T(1024)} %param.13) | copy-start | bytes 12292
  0.9 6.2 %collective-permute-start.2 = (s32[8,128]{1,0:T(8,128)S(1)}, s32[8,128]{1,0:T(8,128)S(1)}, u32[]{:S(2)}, u32[]{:S(2)}) collective-permute-start(s32[8,128]{1,0:T(8,128)S(1)} %payload.1.cand_ref), channel_id=1, source_target_pairs={{0,6},{2,4},{4,2},{6,0},{8,14},{10,12},{12,10},{14,8},{1,7},{3,5},... | collective-permute-start | bytes 12296 | tf_op jit(solution)/shard_map/ppermute | solution.py:276
  4.9 3.6 %collective-permute-start.1 = (s32[8,128]{1,0:T(8,128)S(1)}, s32[8,128]{1,0:T(8,128)S(1)}, u32[]{:S(2)}, u32[]{:S(2)}) collective-permute-start(s32[8,128]{1,0:T(8,128)S(1)} %payload.1.cand_ref), channel_id=1, source_target_pairs={{0,4},{2,6},{4,0},{6,2},{8,12},{10,14},{12,8},{14,10},{1,5},{3,7},... | collective-permute-start | bytes 12296 | tf_op jit(solution)/shard_map/ppermute | solution.py:276
  5.4 3.6 %collective-permute-start = (s32[8,128]{1,0:T(8,128)S(1)}, s32[8,128]{1,0:T(8,128)S(1)}, u32[]{:S(2)}, u32[]{:S(2)}) collective-permute-start(s32[8,128]{1,0:T(8,128)S(1)} %payload.1.cand_ref), channel_id=1, source_target_pairs={{0,2},{2,0},{4,6},{6,4},{8,10},{10,8},{12,14},{14,12},{1,3},{3,1},... | collective-permute-start | bytes 12296 | tf_op jit(solution)/shard_map/ppermute | solution.py:276
  5.6 5.9 %copy-start = (bf16[1024,4,512]{2,1,0:T(4,128)(2,1)S(1)}, bf16[1024,4,512]{2,1,0:T(4,128)(2,1)}, u32[]{:S(2)}) copy-start(bf16[1024,4,512]{2,1,0:T(4,128)(2,1)} %win_ref.3) | copy-start | bytes 12582916
  5.7 5.9 %copy-start.2 = (bf16[1024,512]{1,0:T(8,128)(2,1)S(1)}, bf16[1024,512]{1,0:T(8,128)(2,1)}, u32[]{:S(2)}) copy-start(bf16[1024,512]{1,0:T(8,128)(2,1)} %key_ref.3) | copy-start | bytes 3145732
  5.7 5.9 %copy-start.3 = (bf16[1024,512]{1,0:T(8,128)(2,1)S(1)}, bf16[1024,512]{1,0:T(8,128)(2,1)}, u32[]{:S(2)}) copy-start(bf16[1024,512]{1,0:T(8,128)(2,1)} %value_ref.3) | copy-start | bytes 3145732
  9.0 5.8 %collective-permute-start.3 = (s32[4,8,128]{2,1,0:T(8,128)S(1)}, s32[4,8,128]{2,1,0:T(8,128)S(1)}, u32[]{:S(2)}, u32[]{:S(2)}) collective-permute-start(s32[4,8,128]{2,1,0:T(8,128)S(1)} %pad_add_fusion.cand_ref), channel_id=1, source_target_pairs={{0,8},{2,10},{4,12},{6,14},{8,0},{10,2},{12,4},{14,6},{1,9},{3,11}... | collective-permute-start | bytes 49160 | tf_op jit(solution)/shard_map/ppermute | solution.py:276
  14.8 13.8 %copy-start.4 = (bf16[512,1024]{1,0:T(8,128)(2,1)S(1)}, bf16[512,1024]{1,0:T(8,128)(2,1)}, u32[]{:S(2)}) copy-start(bf16[512,1024]{1,0:T(8,128)(2,1)} %wout_ref.1) | copy-start | bytes 3145732
  17.8 9.2 %collective-permute-start.4 = (bf16[48,512]{1,0:T(8,128)(2,1)S(1)}, bf16[48,512]{1,0:T(8,128)(2,1)S(1)}, u32[]{:S(2)}, u32[]{:S(2)}) collective-permute-start(bf16[48,512]{1,0:T(8,128)(2,1)S(1)} %get-tuple-element.52), channel_id=1, source_target_pairs={{0,8},{2,10},{4,12},{6,14},{8,0},{10,2},{12,4},{14,6},{1,9},{3,11}... | collective-permute-start | bytes 147464 | tf_op jit(solution)/shard_map/ppermute | solution.py:276
  19.2 7.9 %collective-permute-start.5 = (bf16[48,512]{1,0:T(8,128)(2,1)S(1)}, bf16[48,512]{1,0:T(8,128)(2,1)S(1)}, u32[]{:S(2)}, u32[]{:S(2)}) collective-permute-start(bf16[48,512]{1,0:T(8,128)(2,1)S(1)} %get-tuple-element.53), channel_id=1, source_target_pairs={{0,14},{2,12},{4,10},{6,8},{8,6},{10,4},{12,2},{14,0},{1,15},{3,13... | collective-permute-start | bytes 147464 | tf_op jit(solution)/shard_map/ppermute | solution.py:276
  21.7 9.3 %collective-permute-start.6 = (bf16[48,512]{1,0:T(8,128)(2,1)S(1)}, bf16[48,512]{1,0:T(8,128)(2,1)S(1)}, u32[]{:S(2)}, u32[]{:S(2)}) collective-permute-start(bf16[48,512]{1,0:T(8,128)(2,1)S(1)} %get-tuple-element.54), channel_id=1, source_target_pairs={{0,12},{2,14},{4,8},{6,10},{8,4},{10,6},{12,0},{14,2},{1,13},{3,15... | collective-permute-start | bytes 147464 | tf_op jit(solution)/shard_map/ppermute | solution.py:276
  23.0 8.1 %collective-permute-start.7 = (bf16[48,512]{1,0:T(8,128)(2,1)S(1)}, bf16[48,512]{1,0:T(8,128)(2,1)S(1)}, u32[]{:S(2)}, u32[]{:S(2)}) collective-permute-start(bf16[48,512]{1,0:T(8,128)(2,1)S(1)} %get-tuple-element.55), channel_id=1, source_target_pairs={{0,10},{2,8},{4,14},{6,12},{8,2},{10,0},{12,6},{14,4},{1,11},{3,9}... | collective-permute-start | bytes 147464 | tf_op jit(solution)/shard_map/ppermute | solution.py:276
  23.7 7.4 %collective-permute-start.8 = (bf16[48,512]{1,0:T(8,128)(2,1)S(1)}, bf16[48,512]{1,0:T(8,128)(2,1)S(1)}, u32[]{:S(2)}, u32[]{:S(2)}) collective-permute-start(bf16[48,512]{1,0:T(8,128)(2,1)S(1)} %get-tuple-element.56), channel_id=1, source_target_pairs={{0,6},{2,4},{4,2},{6,0},{8,14},{10,12},{12,10},{14,8},{1,7},{3,5},... | collective-permute-start | bytes 147464 | tf_op jit(solution)/shard_map/ppermute | solution.py:276
  27.0 4.1 %collective-permute-start.9 = (bf16[48,512]{1,0:T(8,128)(2,1)S(1)}, bf16[48,512]{1,0:T(8,128)(2,1)S(1)}, u32[]{:S(2)}, u32[]{:S(2)}) collective-permute-start(bf16[48,512]{1,0:T(8,128)(2,1)S(1)} %get-tuple-element.57), channel_id=1, source_target_pairs={{0,4},{2,6},{4,0},{6,2},{8,12},{10,14},{12,8},{14,10},{1,5},{3,7},... | collective-permute-start | bytes 147464 | tf_op jit(solution)/shard_map/ppermute | solution.py:276
  27.1 4.1 %collective-permute-start.10 = (bf16[48,512]{1,0:T(8,128)(2,1)S(1)}, bf16[48,512]{1,0:T(8,128)(2,1)S(1)}, u32[]{:S(2)}, u32[]{:S(2)}) collective-permute-start(bf16[48,512]{1,0:T(8,128)(2,1)S(1)} %get-tuple-element.58), channel_id=1, source_target_pairs={{0,2},{2,0},{4,6},{6,4},{8,10},{10,8},{12,14},{14,12},{1,3},{3,1},... | collective-permute-start | bytes 147464 | tf_op jit(solution)/shard_map/ppermute | solution.py:276
  32.0 1.4 %collective-permute-start.11 = (bf16[128,512]{1,0:T(8,128)(2,1)S(1)}, bf16[128,512]{1,0:T(8,128)(2,1)S(1)}, u32[]{:S(2)}, u32[]{:S(2)}) collective-permute-start(bf16[128,512]{1,0:T(8,128)(2,1)S(1)} %get-tuple-element.62), channel_id=1, source_target_pairs={{0,1},{1,0},{2,3},{3,2},{4,5},{5,4},{6,7},{7,6},{8,9},{9,8},{10,11... | collective-permute-start | bytes 393224 | tf_op jit(solution)/shard_map/ppermute | solution.py:351

commit v5 on v4

--- a/solution.py
+++ b/solution.py
@@ -331,7 +331,11 @@
         [smem] * 2 + [vmem] * 6,
         scratch,
     )(me, hist_lengths, far_cand, code_table, wq, line, hist_keys, hist_values)
-    sent = list(lax.optimization_barrier(tuple(near) + tuple(far)))
+    early = []
+    late = [m for m in range(owners) if m not in early]
+    sums = list(near) + list(far)
+    tied = lax.optimization_barrier(tuple(sums[m] for m in late))
+    sent = [tied[late.index(m)] if m in late else sums[m] for m in range(owners)]
     gate, self_term, wout_mine, wout_other = call(
         functools.partial(own_kernel, heads),
         "own",
@@ -339,7 +343,7 @@
         [full((cand, cols), F32)] * 2 + [full((cols, width // 2), BF16)] * 2,
         [smem] + [vmem] * 5,
     )(me, sent[0], bias, normed, proj_in, proj_out)
-    turns = [4, 7, 6, 5, 3, 2, 1] if owners == 8 else list(range(owners - 1, 0, -1))
+    turns = [4, 7, 5, 6, 3, 2, 1] if owners == 8 else list(range(owners - 1, 0, -1))
     received = [swap(sent[m], m) for m in turns] + [sent[0]]
     mixed, send = call(
         functools.partial(mix_kernel, heads, turns),

time: 34.3 us -> 33.8 us (0.985)
  starting transfers between devices: 18.2 us -> 17.7 us
    ppermute x11, starting transfers between devices: 18.1 us -> 17.6 us  [swap(): return lax.ppermute(x, 'ctx', [(i, i ^ mask) for i in range(owners)])]
  transfers between devices with their start and end apart: 12 -> 12, of which waited for: 4 -> 4; matrix products, arithmetic and copies ran while one was open for 0% -> 0% of each run, Pallas kernels for 21% -> 22%
where the time goes in v5:
time: 33.8 us; the launch traced here: 33.6 us
  starting transfers between devices  17.7 us (52%)
  Pallas kernels  11 us (33%)
  waiting for transfers between devices  3.1 us (9%)
  other arithmetic  1.53 us (5%)
    ppermute x11, starting transfers between devices, swap(): return lax.ppermute(x, 'ctx', [(i, i ^ mask) for i in range(owners)])  17.6 us
    pallas_call x1, Pallas kernels, body(): call(functools.partial(near_kernel, parts, levels, heads, stack, scale),...  3.24 us
    pallas_call x1, Pallas kernels, body(): call(functools.partial(far_kernel, parts, levels, heads, stack, scale), '...  2.92 us
    pallas_call x1, Pallas kernels, body(): call(functools.partial(own_kernel, heads), 'own', 1000000000, [full((cand...  2.42 us
    ppermute x11, waiting for transfers between devices, swap(): return lax.ppermute(x, 'ctx', [(i, i ^ mask) for i in range(owners)])  2 us
    pallas_call x1, Pallas kernels, body(): call(functools.partial(prepare_kernel, levels, heads, parts), 'prepare',...  1.38 us
    ppermute x1, waiting for transfers between devices, body(): other = lax.ppermute(send, 'head', [(0, 1), (1, 0)])  1.1 us
    pallas_call x1, Pallas kernels, body(): call(functools.partial(mix_kernel, heads, turns), 'mix', 1000000000, [ful...  0.84 us
  transfers between devices with their start and end apart: 12, of which 4 were waited for; matrix products, arithmetic and copies ran while one was open for 0% of the time, Pallas kernels for 22%

profile of v5, /device:TPU:0, one launch (start us, length us, event | category | flops | bytes accessed | tf_op | source)
XLA Modules:
  0.0 33.6 jit_solution(5611731183182856770)
XLA Ops:
  0.0 0.1 pad.6.clone
  0.1 0.8 %add_add_fusion.cand_ref = s32[8,128]{1,0:T(8,128)S(1)} fusion(s32[1,128]{1,0:T(1,128)} %bitcast.18, s32[4,128]{1,0:T(4,128)} %bitcast.17, s32[8]{0:T(128)S(1)} %pad.6.clone), kind=kLoop, calls=%fused_computation.2 | loop fusion | flops 2048 | bytes 6688 | tf_op jit(solution)/shard_map/concatenate | solution.py:290
  0.9 4.0 %collective-permute-start.2 = (s32[8,128]{1,0:T(8,128)S(1)}, s32[8,128]{1,0:T(8,128)S(1)}, u32[]{:S(2)}, u32[]{:S(2)}) collective-permute-start(s32[8,128]{1,0:T(8,128)S(1)} %payload.1.cand_ref), channel_id=1, source_target_pairs={{0,6},{2,4},{4,2},{6,0},{8,14},{10,12},{12,10},{14,8},{1,7},{3,5},... | collective-permute-start | bytes 12296 | tf_op jit(solution)/shard_map/ppermute | solution.py:276
  4.9 0.4 %collective-permute-start.1 = (s32[8,128]{1,0:T(8,128)S(1)}, s32[8,128]{1,0:T(8,128)S(1)}, u32[]{:S(2)}, u32[]{:S(2)}) collective-permute-start(s32[8,128]{1,0:T(8,128)S(1)} %payload.1.cand_ref), channel_id=1, source_target_pairs={{0,4},{2,6},{4,0},{6,2},{8,12},{10,14},{12,8},{14,10},{1,5},{3,7},... | collective-permute-start | bytes 12296 | tf_op jit(solution)/shard_map/ppermute | solution.py:276
  5.4 0.2 collective-permute-start
  5.7 1.4 %prepare.1 = (bf16[128,1024]{1,0:T(8,128)(2,1)S(1)}, f32[128,512]{1,0:T(8,128)S(1)}, bf16[128,384]{1,0:T(8,128)(2,1)S(1)}, f32[128,128]{1,0:T(8,128)S(1)}, f32[8,1024]{1,0:T(8,128)S(1)}, /*index=5*/s32[8,128]{1,0:T(8,128)S(1)}) custom-call(s32[2]{0:T(128)S(1)} %pad_add_fusion.1.me_ref, s32[8]{0:T(128)S(1)} %copy-done.6, s32[8,128]{1,0:T(8,128)S(1)} %payload.1.cand_ref, ...), custom_call_target="tpu_custom_call" | custom-call | flops 8000000000 | bytes 1048576 | tf_op jit(solution)/shard_map/prepare/pallas_call | solution.py:296
  7.1 1.4 %collective-permute-done.1 = s32[8,128]{1,0:T(8,128)S(1)} collective-permute-done((s32[8,128]{1,0:T(8,128)S(1)}, s32[8,128]{1,0:T(8,128)S(1)}, u32[]{:S(2)}, u32[]{:S(2)}) %collective-permute-start.1) | collective-permute-done | bytes 4128 | tf_op jit(solution)/shard_map/ppermute | solution.py:276
  8.5 0.4 %collective-permute-done = s32[8,128]{1,0:T(8,128)S(1)} collective-permute-done((s32[8,128]{1,0:T(8,128)S(1)}, s32[8,128]{1,0:T(8,128)S(1)}, u32[]{:S(2)}, u32[]{:S(2)}) %collective-permute-start) | collective-permute-done | bytes 4128 | tf_op jit(solution)/shard_map/ppermute | solution.py:276
  9.0 2.6 %collective-permute-start.3 = (s32[4,8,128]{2,1,0:T(8,128)S(1)}, s32[4,8,128]{2,1,0:T(8,128)S(1)}, u32[]{:S(2)}, u32[]{:S(2)}) collective-permute-start(s32[4,8,128]{2,1,0:T(8,128)S(1)} %pad_add_fusion.cand_ref), channel_id=1, source_target_pairs={{0,8},{2,10},{4,12},{6,14},{8,0},{10,2},{12,4},{14,6},{1,9},{3,11}... | collective-permute-start | bytes 49160 | tf_op jit(solution)/shard_map/ppermute | solution.py:276
  11.6 3.2 %near.1 = (bf16[48,512]{1,0:T(8,128)(2,1)S(1)}, bf16[48,512]{1,0:T(8,128)(2,1)S(1)}, bf16[48,512]{1,0:T(8,128)(2,1)S(1)}, bf16[48,512]{1,0:T(8,128)(2,1)S(1)}, bf16[1024,512]{1,0:T(8,128)(2,1)S(1)}) custom-call(s32[2]{0:T(128)S(1)} %pad_add_fusion.1.me_ref, s32[8]{0:T(128)S(1)} %copy-done.6, s32[4,8,128]{2,1,0:T(8,128)S(1)} %pad_add_fusion.cand_ref, ...), custom_call_target="tpu_custom_call" | custom-call | flops 1000000000 | bytes 1048576 | tf_op jit(solution)/shard_map/near/pallas_call | solution.py:318
  14.8 2.9 %far.1 = (bf16[48,512]{1,0:T(8,128)(2,1)S(1)}, bf16[48,512]{1,0:T(8,128)(2,1)S(1)}, bf16[48,512]{1,0:T(8,128)(2,1)S(1)}, bf16[48,512]{1,0:T(8,128)(2,1)S(1)}) custom-call(s32[2]{0:T(128)S(1)} %pad_add_fusion.1.me_ref, s32[8]{0:T(128)S(1)} %copy-done.6, s32[4,8,128]{2,1,0:T(8,128)S(1)} %collective-permute-done.3.cand_ref, bf16[1024,1024]{1,0:T(8,128)(2,1)S(1)} %copy-done.1, ...), custom_call_target="tpu_custom_call" | custom-call | flops 3000000000 | bytes 1048576 | tf_op jit(solution)/shard_map/far/pallas_call | solution.py:326
  17.8 1.4 %collective-permute-start.4 = (bf16[48,512]{1,0:T(8,128)(2,1)S(1)}, bf16[48,512]{1,0:T(8,128)(2,1)S(1)}, u32[]{:S(2)}, u32[]{:S(2)}) collective-permute-start(bf16[48,512]{1,0:T(8,128)(2,1)S(1)} %get-tuple-element.52), channel_id=1, source_target_pairs={{0,8},{2,10},{4,12},{6,14},{8,0},{10,2},{12,4},{14,6},{1,9},{3,11}... | collective-permute-start | bytes 147464 | tf_op jit(solution)/shard_map/ppermute | solution.py:276
  19.2 2.5 %collective-permute-start.5 = (bf16[48,512]{1,0:T(8,128)(2,1)S(1)}, bf16[48,512]{1,0:T(8,128)(2,1)S(1)}, u32[]{:S(2)}, u32[]{:S(2)}) collective-permute-start(bf16[48,512]{1,0:T(8,128)(2,1)S(1)} %get-tuple-element.53), channel_id=1, source_target_pairs={{0,14},{2,12},{4,10},{6,8},{8,6},{10,4},{12,2},{14,0},{1,15},{3,13... | collective-permute-start | bytes 147464 | tf_op jit(solution)/shard_map/ppermute | solution.py:276
  21.7 1.5 %collective-permute-start.6 = (bf16[48,512]{1,0:T(8,128)(2,1)S(1)}, bf16[48,512]{1,0:T(8,128)(2,1)S(1)}, u32[]{:S(2)}, u32[]{:S(2)}) collective-permute-start(bf16[48,512]{1,0:T(8,128)(2,1)S(1)} %get-tuple-element.54), channel_id=1, source_target_pairs={{0,10},{2,8},{4,14},{6,12},{8,2},{10,0},{12,6},{14,4},{1,11},{3,9}... | collective-permute-start | bytes 147464 | tf_op jit(solution)/shard_map/ppermute | solution.py:276
  23.2 1.4 %collective-permute-start.7 = (bf16[48,512]{1,0:T(8,128)(2,1)S(1)}, bf16[48,512]{1,0:T(8,128)(2,1)S(1)}, u32[]{:S(2)}, u32[]{:S(2)}) collective-permute-start(bf16[48,512]{1,0:T(8,128)(2,1)S(1)} %get-tuple-element.55), channel_id=1, source_target_pairs={{0,12},{2,14},{4,8},{6,10},{8,4},{10,6},{12,0},{14,2},{1,13},{3,15... | collective-permute-start | bytes 147464 | tf_op jit(solution)/shard_map/ppermute | solution.py:276
  24.6 1.5 %collective-permute-start.8 = (bf16[48,512]{1,0:T(8,128)(2,1)S(1)}, bf16[48,512]{1,0:T(8,128)(2,1)S(1)}, u32[]{:S(2)}, u32[]{:S(2)}) collective-permute-start(bf16[48,512]{1,0:T(8,128)(2,1)S(1)} %get-tuple-element.56), channel_id=1, source_target_pairs={{0,6},{2,4},{4,2},{6,0},{8,14},{10,12},{12,10},{14,8},{1,7},{3,5},... | collective-permute-start | bytes 147464 | tf_op jit(solution)/shard_map/ppermute | solution.py:276
  26.1 0.5 %collective-permute-start.9 = (bf16[48,512]{1,0:T(8,128)(2,1)S(1)}, bf16[48,512]{1,0:T(8,128)(2,1)S(1)}, u32[]{:S(2)}, u32[]{:S(2)}) collective-permute-start(bf16[48,512]{1,0:T(8,128)(2,1)S(1)} %get-tuple-element.57), channel_id=1, source_target_pairs={{0,4},{2,6},{4,0},{6,2},{8,12},{10,14},{12,8},{14,10},{1,5},{3,7},... | collective-permute-start | bytes 147464 | tf_op jit(solution)/shard_map/ppermute | solution.py:276
  26.6 1.5 %collective-permute-start.10 = (bf16[48,512]{1,0:T(8,128)(2,1)S(1)}, bf16[48,512]{1,0:T(8,128)(2,1)S(1)}, u32[]{:S(2)}, u32[]{:S(2)}) collective-permute-start(bf16[48,512]{1,0:T(8,128)(2,1)S(1)} %get-tuple-element.58), channel_id=1, source_target_pairs={{0,2},{2,0},{4,6},{6,4},{8,10},{10,8},{12,14},{14,12},{1,3},{3,1},... | collective-permute-start | bytes 147464 | tf_op jit(solution)/shard_map/ppermute | solution.py:276
  28.1 2.4 %own.1 = (f32[128,512]{1,0:T(8,128)S(1)}, f32[128,512]{1,0:T(8,128)S(1)}, bf16[512,512]{1,0:T(8,128)(2,1)S(1)}, bf16[512,512]{1,0:T(8,128)(2,1)S(1)}) custom-call(s32[2]{0:T(128)S(1)} %pad_add_fusion.1.me_ref, bf16[48,512]{1,0:T(8,128)(2,1)S(1)} %get-tuple-element.45.sent_ref.rest_7_, f32[8,128]{1,0:T(8,128)S(1)} %bitcast.11, ...), custom_call_target="tpu_custom_call" | custom-call | flops 1000000000 | bytes 1048576 | tf_op jit(solution)/shard_map/own/pallas_call | solution.py:339
  30.6 0.1 collective-permute-done.10.rest_6_
  30.7 0.8 %mix.1 = (bf16[128,512]{1,0:T(8,128)(2,1)S(1)}, bf16[128,512]{1,0:T(8,128)(2,1)S(1)}) custom-call(f32[128,512]{1,0:T(8,128)S(1)} %get-tuple-element.47.gate_ref, f32[128,512]{1,0:T(8,128)S(1)} %get-tuple-element.48.self_ref, bf16[128,384]{1,0:T(8,128)(2,1)S(1)} %get-tuple-element.49.assign_ref, f32[128,128]{1,0:T(8,128)S(1)} %get-tuple-element.50.scale_ref, ...), custom_call_target="tpu_custom_call" | custom-call | flops 1000000000 | bytes 1048576 | tf_op jit(solution)/shard_map/mix/pallas_call | solution.py:348
  31.6 0.2 keep.1
  31.8 1.1 %collective-permute-done.11 = bf16[128,512]{1,0:T(8,128)(2,1)S(1)} collective-permute-done((bf16[128,512]{1,0:T(8,128)(2,1)S(1)}, bf16[128,512]{1,0:T(8,128)(2,1)S(1)}, u32[]{:S(2)}, u32[]{:S(2)}) %collective-permute-start.11) | collective-permute-done | bytes 131104 | tf_op jit(solution)/shard_map/ppermute | solution.py:355
  32.9 0.7 %add_convert_fusion = bf16[128,512]{1,0:T(8,128)(2,1)} fusion(f32[128,512]{1,0:T(8,128)S(1)} %keep.1, bf16[128,512]{1,0:T(8,128)(2,1)S(1)} %collective-permute-done.11), kind=kLoop, calls=%fused_computation | loop fusion | flops 196608 | bytes 524288 | tf_op jit(solution)/shard_map/convert_element_type | solution.py:359
  (29 shorter events, 0.2 us)
Async XLA Ops:
  0.8 4.8 %copy-start.1 = (bf16[1024,1024]{1,0:T(8,128)(2,1)S(1)}, bf16[1024,1024]{1,0:T(8,128)(2,1)}, u32[]{:S(2)}) copy-start(bf16[1024,1024]{1,0:T(8,128)(2,1)} %table_ref.5) | copy-start | bytes 6291460
  0.8 4.8 %copy-start.5 = (f32[128,8]{0,1:T(8,128)S(1)}, f32[128,8]{0,1:T(8,128)}, u32[]{:S(2)}) copy-start(f32[128,8]{0,1:T(8,128)} %param.18) | copy-start | bytes 12292
  0.9 4.8 %copy-start.6 = (s32[8]{0:T(128)S(1)}, s32[8]{0:T(128)}, u32[]{:S(2)}) copy-start(s32[8]{0:T(128)} %lens_ref.5) | copy-start | bytes 100
  0.9 4.8 %copy-start.7 = (s32[1024]{0:T(1024)S(1)}, s32[1024]{0:T(1024)}, u32[]{:S(2)}) copy-start(s32[1024]{0:T(1024)} %param.13) | copy-start | bytes 12292
  0.9 6.2 %collective-permute-start.2 = (s32[8,128]{1,0:T(8,128)S(1)}, s32[8,128]{1,0:T(8,128)S(1)}, u32[]{:S(2)}, u32[]{:S(2)}) collective-permute-start(s32[8,128]{1,0:T(8,128)S(1)} %payload.1.cand_ref), channel_id=1, source_target_pairs={{0,6},{2,4},{4,2},{6,0},{8,14},{10,12},{12,10},{14,8},{1,7},{3,5},... | collective-permute-start | bytes 12296 | tf_op jit(solution)/shard_map/ppermute | solution.py:276
  4.9 3.6 %collective-permute-start.1 = (s32[8,128]{1,0:T(8,128)S(1)}, s32[8,128]{1,0:T(8,128)S(1)}, u32[]{:S(2)}, u32[]{:S(2)}) collective-permute-start(s32[8,128]{1,0:T(8,128)S(1)} %payload.1.cand_ref), channel_id=1, source_target_pairs={{0,4},{2,6},{4,0},{6,2},{8,12},{10,14},{12,8},{14,10},{1,5},{3,7},... | collective-permute-start | bytes 12296 | tf_op jit(solution)/shard_map/ppermute | solution.py:276
  5.4 3.6 %collective-permute-start = (s32[8,128]{1,0:T(8,128)S(1)}, s32[8,128]{1,0:T(8,128)S(1)}, u32[]{:S(2)}, u32[]{:S(2)}) collective-permute-start(s32[8,128]{1,0:T(8,128)S(1)} %payload.1.cand_ref), channel_id=1, source_target_pairs={{0,2},{2,0},{4,6},{6,4},{8,10},{10,8},{12,14},{14,12},{1,3},{3,1},... | collective-permute-start | bytes 12296 | tf_op jit(solution)/shard_map/ppermute | solution.py:276
  5.6 5.9 %copy-start = (bf16[1024,4,512]{2,1,0:T(4,128)(2,1)S(1)}, bf16[1024,4,512]{2,1,0:T(4,128)(2,1)}, u32[]{:S(2)}) copy-start(bf16[1024,4,512]{2,1,0:T(4,128)(2,1)} %win_ref.3) | copy-start | bytes 12582916
  5.7 5.9 %copy-start.2 = (bf16[1024,512]{1,0:T(8,128)(2,1)S(1)}, bf16[1024,512]{1,0:T(8,128)(2,1)}, u32[]{:S(2)}) copy-start(bf16[1024,512]{1,0:T(8,128)(2,1)} %key_ref.3) | copy-start | bytes 3145732
  5.7 5.9 %copy-start.3 = (bf16[1024,512]{1,0:T(8,128)(2,1)S(1)}, bf16[1024,512]{1,0:T(8,128)(2,1)}, u32[]{:S(2)}) copy-start(bf16[1024,512]{1,0:T(8,128)(2,1)} %value_ref.3) | copy-start | bytes 3145732
  9.0 5.8 %collective-permute-start.3 = (s32[4,8,128]{2,1,0:T(8,128)S(1)}, s32[4,8,128]{2,1,0:T(8,128)S(1)}, u32[]{:S(2)}, u32[]{:S(2)}) collective-permute-start(s32[4,8,128]{2,1,0:T(8,128)S(1)} %pad_add_fusion.cand_ref), channel_id=1, source_target_pairs={{0,8},{2,10},{4,12},{6,14},{8,0},{10,2},{12,4},{14,6},{1,9},{3,11}... | collective-permute-start | bytes 49160 | tf_op jit(solution)/shard_map/ppermute | solution.py:276
  14.8 13.3 %copy-start.4 = (bf16[512,1024]{1,0:T(8,128)(2,1)S(1)}, bf16[512,1024]{1,0:T(8,128)(2,1)}, u32[]{:S(2)}) copy-start(bf16[512,1024]{1,0:T(8,128)(2,1)} %wout_ref.1) | copy-start | bytes 3145732
  17.8 8.3 %collective-permute-start.4 = (bf16[48,512]{1,0:T(8,128)(2,1)S(1)}, bf16[48,512]{1,0:T(8,128)(2,1)S(1)}, u32[]{:S(2)}, u32[]{:S(2)}) collective-permute-start(bf16[48,512]{1,0:T(8,128)(2,1)S(1)} %get-tuple-element.52), channel_id=1, source_target_pairs={{0,8},{2,10},{4,12},{6,14},{8,0},{10,2},{12,4},{14,6},{1,9},{3,11}... | collective-permute-start | bytes 147464 | tf_op jit(solution)/shard_map/ppermute | solution.py:276
  19.2 7.4 %collective-permute-start.5 = (bf16[48,512]{1,0:T(8,128)(2,1)S(1)}, bf16[48,512]{1,0:T(8,128)(2,1)S(1)}, u32[]{:S(2)}, u32[]{:S(2)}) collective-permute-start(bf16[48,512]{1,0:T(8,128)(2,1)S(1)} %get-tuple-element.53), channel_id=1, source_target_pairs={{0,14},{2,12},{4,10},{6,8},{8,6},{10,4},{12,2},{14,0},{1,15},{3,13... | collective-permute-start | bytes 147464 | tf_op jit(solution)/shard_map/ppermute | solution.py:276
  21.7 8.8 %collective-permute-start.6 = (bf16[48,512]{1,0:T(8,128)(2,1)S(1)}, bf16[48,512]{1,0:T(8,128)(2,1)S(1)}, u32[]{:S(2)}, u32[]{:S(2)}) collective-permute-start(bf16[48,512]{1,0:T(8,128)(2,1)S(1)} %get-tuple-element.54), channel_id=1, source_target_pairs={{0,10},{2,8},{4,14},{6,12},{8,2},{10,0},{12,6},{14,4},{1,11},{3,9}... | collective-permute-start | bytes 147464 | tf_op jit(solution)/shard_map/ppermute | solution.py:276
  23.2 7.3 %collective-permute-start.7 = (bf16[48,512]{1,0:T(8,128)(2,1)S(1)}, bf16[48,512]{1,0:T(8,128)(2,1)S(1)}, u32[]{:S(2)}, u32[]{:S(2)}) collective-permute-start(bf16[48,512]{1,0:T(8,128)(2,1)S(1)} %get-tuple-element.55), channel_id=1, source_target_pairs={{0,12},{2,14},{4,8},{6,10},{8,4},{10,6},{12,0},{14,2},{1,13},{3,15... | collective-permute-start | bytes 147464 | tf_op jit(solution)/shard_map/ppermute | solution.py:276
  24.6 6.0 %collective-permute-start.8 = (bf16[48,512]{1,0:T(8,128)(2,1)S(1)}, bf16[48,512]{1,0:T(8,128)(2,1)S(1)}, u32[]{:S(2)}, u32[]{:S(2)}) collective-permute-start(bf16[48,512]{1,0:T(8,128)(2,1)S(1)} %get-tuple-element.56), channel_id=1, source_target_pairs={{0,6},{2,4},{4,2},{6,0},{8,14},{10,12},{12,10},{14,8},{1,7},{3,5},... | collective-permute-start | bytes 147464 | tf_op jit(solution)/shard_map/ppermute | solution.py:276
  26.1 4.4 %collective-permute-start.9 = (bf16[48,512]{1,0:T(8,128)(2,1)S(1)}, bf16[48,512]{1,0:T(8,128)(2,1)S(1)}, u32[]{:S(2)}, u32[]{:S(2)}) collective-permute-start(bf16[48,512]{1,0:T(8,128)(2,1)S(1)} %get-tuple-element.57), channel_id=1, source_target_pairs={{0,4},{2,6},{4,0},{6,2},{8,12},{10,14},{12,8},{14,10},{1,5},{3,7},... | collective-permute-start | bytes 147464 | tf_op jit(solution)/shard_map/ppermute | solution.py:276
  26.6 4.1 %collective-permute-start.10 = (bf16[48,512]{1,0:T(8,128)(2,1)S(1)}, bf16[48,512]{1,0:T(8,128)(2,1)S(1)}, u32[]{:S(2)}, u32[]{:S(2)}) collective-permute-start(bf16[48,512]{1,0:T(8,128)(2,1)S(1)} %get-tuple-element.58), channel_id=1, source_target_pairs={{0,2},{2,0},{4,6},{6,4},{8,10},{10,8},{12,14},{14,12},{1,3},{3,1},... | collective-permute-start | bytes 147464 | tf_op jit(solution)/shard_map/ppermute | solution.py:276
  31.5 1.4 %collective-permute-start.11 = (bf16[128,512]{1,0:T(8,128)(2,1)S(1)}, bf16[128,512]{1,0:T(8,128)(2,1)S(1)}, u32[]{:S(2)}, u32[]{:S(2)}) collective-permute-start(bf16[128,512]{1,0:T(8,128)(2,1)S(1)} %get-tuple-element.62), channel_id=1, source_target_pairs={{0,1},{1,0},{2,3},{3,2},{4,5},{5,4},{6,7},{7,6},{8,9},{9,8},{10,11... | collective-permute-start | bytes 393224 | tf_op jit(solution)/shard_map/ppermute | solution.py:355

commit v6 on v5

--- a/solution.py
+++ b/solution.py
@@ -69,16 +69,15 @@
     return (centred * lax.rsqrt(var + 1e-05)).astype(BF16)
 
 
-def slot_queries(parts, levels, scale, me_ref, lens_ref, cand_ref, table_ref, wq_ref, slot_ref):
+def slot_queries(parts, levels, scale, target_ref, cand_ref, table_ref, wq_ref, slot_ref):
     owners, _, cand = cand_ref.shape
-    first = me_ref[0] * parts * UNIT
     order = ones_where(iota((cand, cand), 0) <= iota((cand, cand), 1))
     slot = iota((MOST, cand), 0).astype(F32) + 1.0
     requests = jnp.concatenate([cand_ref[:, levels, :]] * parts, axis=0)
     line = iota(requests.shape, 0) // owners
     target = jnp.zeros(requests.shape, jnp.int32)
     for p in range(parts):
-        target = jnp.where(line == p, request_at(first + p * UNIT, lens_ref), target)
+        target = jnp.where(line == p, target_ref[p : p + 1, :], target)
     wanted = requests == target
     rank = jnp.where(wanted, dot(ones_where(wanted), order), 0.0)
     for k in range(owners):
@@ -99,7 +98,7 @@
 
 def prepare_kernel(
     levels, heads, parts, me_ref, lens_ref, cand_ref, bucket_ref, bias_ref, table_ref,
-    normed_ref, residual_ref, assign_ref, scale_ref, line_ref, next_ref,
+    normed_ref, residual_ref, assign_ref, scale_ref, line_ref, target_ref, next_ref,
 ):
     _, cand = cand_ref.shape
     eye = ones_where(iota((cand, cand), 0) == iota((cand, cand), 1))
@@ -129,11 +128,16 @@
     for r in range(lens_ref.shape[0]):
         length = jnp.where(request == float(r), lens_ref[r].astype(F32), length)
     scale_ref[...] = jnp.broadcast_to(lax.rsqrt(length), scale_ref.shape)
+    row = iota(target_ref.shape, 0)
+    target = jnp.where(row == target_ref.shape[0] - 1, me_ref[1], 0)
+    for p in range(parts):
+        target = jnp.where(row == p, request_at((me_ref[0] * parts + p) * UNIT, lens_ref), target)
+    target_ref[...] = target
     next_ref[...] = cand_ref[...]
 
 
 def own_kernel(
-    heads, me_ref, sent_ref, bias_ref, normed_ref, win_ref, wout_ref, gate_ref, self_ref, mine_ref, other_ref
+    heads, target_ref, sent_ref, bias_ref, normed_ref, win_ref, wout_ref, gate_ref, self_ref, mine_ref, other_ref
 ):
     cols = win_ref.shape[2]
     head_size = cols // heads
@@ -148,9 +152,11 @@
     self_ref[...] = silu(score) * silu(dot(normed, weights[3]))
     half = wout_ref.shape[1] // 2
     low, high = wout_ref[:, :half], wout_ref[:, half:]
-    second = me_ref[1] == 1
-    mine_ref[...] = jnp.where(second, high, low)
-    other_ref[...] = jnp.where(second, low, high)
+    second = target_ref[target_ref.shape[0] - 1 :, 0:1].astype(F32)
+    to_high = jnp.broadcast_to(second, low.shape).astype(BF16)
+    to_low = jnp.broadcast_to(1.0 - second, low.shape).astype(BF16)
+    mine_ref[...] = high * to_high + low * to_low
+    other_ref[...] = high * to_low + low * to_high
 
 
 def attend(parts, heads, stack, owners, query, line_ref, key_ref, value_ref, store):
@@ -186,35 +192,35 @@
 
 def near_kernel(
     parts, levels, heads, stack, scale,
-    me_ref, lens_ref, cand_ref, table_ref, win_ref, line_ref, key_ref, value_ref, *rest
+    target_ref, cand_ref, table_ref, win_ref, line_ref, key_ref, value_ref, *rest
 ):
     owners = cand_ref.shape[0]
     outs, (wq_ref, slot_ref, result_ref) = rest[:owners], rest[owners:]
     wq_ref[...] = jnp.swapaxes(win_ref[...], 0, 1)[1]
     sums_of(
         parts, levels, heads, stack, scale,
-        me_ref, lens_ref, cand_ref, table_ref, wq_ref, line_ref, key_ref, value_ref, outs, slot_ref, result_ref,
+        target_ref, cand_ref, table_ref, wq_ref, line_ref, key_ref, value_ref, outs, slot_ref, result_ref,
     )
 
 
 def far_kernel(
     parts, levels, heads, stack, scale,
-    me_ref, lens_ref, cand_ref, table_ref, wq_ref, line_ref, key_ref, value_ref, *rest
+    target_ref, cand_ref, table_ref, wq_ref, line_ref, key_ref, value_ref, *rest
 ):
     owners = cand_ref.shape[0]
     outs, (slot_ref, result_ref) = rest[:owners], rest[owners:]
     sums_of(
         parts, levels, heads, stack, scale,
-        me_ref, lens_ref, cand_ref, table_ref, wq_ref, line_ref, key_ref, value_ref, outs, slot_ref, result_ref,
+        target_ref, cand_ref, table_ref, wq_ref, line_ref, key_ref, value_ref, outs, slot_ref, result_ref,
     )
 
 
 def sums_of(
     parts, levels, heads, stack, scale,
-    me_ref, lens_ref, cand_ref, table_ref, wq_ref, line_ref, key_ref, value_ref, outs, slot_ref, result_ref,
+    target_ref, cand_ref, table_ref, wq_ref, line_ref, key_ref, value_ref, outs, slot_ref, result_ref,
 ):
     owners = cand_ref.shape[0]
-    query = slot_queries(parts, levels, scale, me_ref, lens_ref, cand_ref, table_ref, wq_ref, slot_ref)
+    query = slot_queries(parts, levels, scale, target_ref, cand_ref, table_ref, wq_ref, slot_ref)
 
     def store(k, p, at, value):
         result_ref[k, p * MOST : (p + 1) * MOST, at] = value
@@ -293,7 +299,7 @@
     payload = call(
         payload_kernel, "payload", 9_000_000_000, full((ROWS, cand), jnp.int32), [vmem], cost=32 << 20
     )(payload)
-    normed, residual, assign, lengths, line, payload_next = call(
+    normed, residual, assign, lengths, line, target, payload_next = call(
         functools.partial(prepare_kernel, levels, heads, parts),
         "prepare",
         8_000_000_000,
@@ -303,6 +309,7 @@
             full((cand, slots), BF16),
             full((cand, LANES), F32),
             full((heads, hist), F32),
+            full((ROWS, cand), jnp.int32),
             full((ROWS, cand), jnp.int32),
         ],
         [smem] * 2 + [vmem] * 4,
@@ -320,17 +327,17 @@
         "near",
         1_000_000_000,
         [full((block, cols), BF16)] * half + [full((width, cols), BF16)],
-        [smem] * 2 + [vmem] * 6,
+        [vmem] * 7,
         scratch,
-    )(me, hist_lengths, near_cand, code_table, proj_in, line, hist_keys, hist_values)
+    )(target, near_cand, code_table, proj_in, line, hist_keys, hist_values)
     far = call(
         functools.partial(far_kernel, parts, levels, heads, stack, scale),
         "far",
         3_000_000_000,
         [full((block, cols), BF16)] * half,
-        [smem] * 2 + [vmem] * 6,
+        [vmem] * 7,
         scratch,
-    )(me, hist_lengths, far_cand, code_table, wq, line, hist_keys, hist_values)
+    )(target, far_cand, code_table, wq, line, hist_keys, hist_values)
     early = []
     late = [m for m in range(owners) if m not in early]
     sums = list(near) + list(far)
@@ -341,8 +348,8 @@
         "own",
         1_000_000_000,
         [full((cand, cols), F32)] * 2 + [full((cols, width // 2), BF16)] * 2,
-        [smem] + [vmem] * 5,
-    )(me, sent[0], bias, normed, proj_in, proj_out)
+        [vmem] * 6,
+    )(target, sent[0], bias, normed, proj_in, proj_out)
     turns = [4, 7, 5, 6, 3, 2, 1] if owners == 8 else list(range(owners - 1, 0, -1))
     received = [swap(sent[m], m) for m in turns] + [sent[0]]
     mixed, send = call(

time: 33.8 us -> 33 us (0.976)
  Pallas kernels: 11 us -> 9.67 us
  waiting for transfers between devices: 3.1 us -> 3.93 us
    ppermute x11, waiting for transfers between devices: 2 us -> 2.83 us  [swap(): return lax.ppermute(x, 'ctx', [(i, i ^ mask) for i in range(owners)])]
    pallas_call x1, Pallas kernels: 2.92 us -> 2.45 us  [body(): call(functools.partial(far_kernel, parts, levels, heads, stack, scale), '...]
    pallas_call x1, Pallas kernels: 3.24 us -> 2.77 us  [body(): call(functools.partial(near_kernel, parts, levels, heads, stack, scale),...]
    pallas_call x1, Pallas kernels: 2.42 us -> 1.99 us  [body(): call(functools.partial(own_kernel, heads), 'own', 1000000000, [full((cand...]
  transfers between devices with their start and end apart: 12 -> 12, of which waited for: 4 -> 6; matrix products, arithmetic and copies ran while one was open for 0% -> 0% of each run, Pallas kernels for 22% -> 19%
where the time goes in v6:
time: 33 us; the launch traced here: 32.9 us
  starting transfers between devices  17.5 us (53%)
  Pallas kernels  9.67 us (29%)
  waiting for transfers between devices  3.93 us (12%)
  other arithmetic  1.53 us (5%)
    ppermute x11, starting transfers between devices, swap(): return lax.ppermute(x, 'ctx', [(i, i ^ mask) for i in range(owners)])  17.4 us
    ppermute x11, waiting for transfers between devices, swap(): return lax.ppermute(x, 'ctx', [(i, i ^ mask) for i in range(owners)])  2.83 us
    pallas_call x1, Pallas kernels, body(): call(functools.partial(near_kernel, parts, levels, heads, stack, scale),...  2.77 us
    pallas_call x1, Pallas kernels, body(): call(functools.partial(far_kernel, parts, levels, heads, stack, scale), '...  2.45 us
    pallas_call x1, Pallas kernels, body(): call(functools.partial(own_kernel, heads), 'own', 1000000000, [full((cand...  1.99 us
    pallas_call x1, Pallas kernels, body(): call(functools.partial(prepare_kernel, levels, heads, parts), 'prepare',...  1.38 us
    ppermute x1, waiting for transfers between devices, body(): other = lax.ppermute(send, 'head', [(0, 1), (1, 0)])  1.1 us
    pallas_call x1, Pallas kernels, body(): call(functools.partial(mix_kernel, heads, turns), 'mix', 1000000000, [ful...  0.85 us
  transfers between devices with their start and end apart: 12, of which 6 were waited for; matrix products, arithmetic and copies ran while one was open for 0% of the time, Pallas kernels for 19%

profile of v6, /device:TPU:0, one launch (start us, length us, event | category | flops | bytes accessed | tf_op | source)
XLA Modules:
  0.0 32.9 jit_solution(10409870258734685745)
XLA Ops:
  0.1 0.8 %add_add_fusion.cand_ref = s32[8,128]{1,0:T(8,128)S(1)} fusion(s32[1,128]{1,0:T(1,128)} %bitcast.18, s32[4,128]{1,0:T(4,128)} %bitcast.17, s32[8]{0:T(128)S(1)} %pad.6.clone), kind=kLoop, calls=%fused_computation.2 | loop fusion | flops 2048 | bytes 6688 | tf_op jit(solution)/shard_map/concatenate | solution.py:296
  0.9 4.0 %collective-permute-start.2 = (s32[8,128]{1,0:T(8,128)S(1)}, s32[8,128]{1,0:T(8,128)S(1)}, u32[]{:S(2)}, u32[]{:S(2)}) collective-permute-start(s32[8,128]{1,0:T(8,128)S(1)} %payload.1.cand_ref), channel_id=1, source_target_pairs={{0,6},{2,4},{4,2},{6,0},{8,14},{10,12},{12,10},{14,8},{1,7},{3,5},... | collective-permute-start | bytes 12296 | tf_op jit(solution)/shard_map/ppermute | solution.py:282
  4.9 0.4 %collective-permute-start.1 = (s32[8,128]{1,0:T(8,128)S(1)}, s32[8,128]{1,0:T(8,128)S(1)}, u32[]{:S(2)}, u32[]{:S(2)}) collective-permute-start(s32[8,128]{1,0:T(8,128)S(1)} %payload.1.cand_ref), channel_id=1, source_target_pairs={{0,4},{2,6},{4,0},{6,2},{8,12},{10,14},{12,8},{14,10},{1,5},{3,7},... | collective-permute-start | bytes 12296 | tf_op jit(solution)/shard_map/ppermute | solution.py:282
  5.4 0.2 collective-permute-start
  5.7 1.4 %prepare.1 = (bf16[128,1024]{1,0:T(8,128)(2,1)S(1)}, f32[128,512]{1,0:T(8,128)S(1)}, bf16[128,384]{1,0:T(8,128)(2,1)S(1)}, f32[128,128]{1,0:T(8,128)S(1)}, f32[8...) custom-call(s32[2]{0:T(128)S(1)} %pad_add_fusion.1.me_ref, s32[8]{0:T(128)S(1)} %copy-done.7, ...), custom_call_target="tpu_custom_call" | custom-call | flops 8000000000 | bytes 1048576 | tf_op jit(solution)/shard_map/prepare/pallas_call | solution.py:302
  7.1 1.4 %collective-permute-done.1 = s32[8,128]{1,0:T(8,128)S(1)} collective-permute-done((s32[8,128]{1,0:T(8,128)S(1)}, s32[8,128]{1,0:T(8,128)S(1)}, u32[]{:S(2)}, u32[]{:S(2)}) %collective-permute-start.1) | collective-permute-done | bytes 4128 | tf_op jit(solution)/shard_map/ppermute | solution.py:282
  8.5 0.4 %collective-permute-done = s32[8,128]{1,0:T(8,128)S(1)} collective-permute-done((s32[8,128]{1,0:T(8,128)S(1)}, s32[8,128]{1,0:T(8,128)S(1)}, u32[]{:S(2)}, u32[]{:S(2)}) %collective-permute-start) | collective-permute-done | bytes 4128 | tf_op jit(solution)/shard_map/ppermute | solution.py:282
  9.0 2.6 %collective-permute-start.3 = (s32[4,8,128]{2,1,0:T(8,128)S(1)}, s32[4,8,128]{2,1,0:T(8,128)S(1)}, u32[]{:S(2)}, u32[]{:S(2)}) collective-permute-start(s32[4,8,128]{2,1,0:T(8,128)S(1)} %pad_add_fusion.cand_ref), channel_id=1, source_target_pairs={{0,8},{2,10},{4,12},{6,14},{8,0},{10,2},{12,4},{14,6},{1,9},{3,11}... | collective-permute-start | bytes 49160 | tf_op jit(solution)/shard_map/ppermute | solution.py:282
  11.6 2.8 %near.1 = (bf16[48,512]{1,0:T(8,128)(2,1)S(1)}, bf16[48,512]{1,0:T(8,128)(2,1)S(1)}, bf16[48,512]{1,0:T(8,128)(2,1)S(1)}, bf16[48,512]{1,0:T(8,128)(2,1)S(1)}, bf16[1024,512]{1,0:T(8,128)(2,1)S(1)}) custom-call(s32[8,128]{1,0:T(8,128)S(1)} %get-tuple-element.35.target_ref, s32[4,8,128]{2,1,0:T(8,128)S(1)} %pad_add_fusion.cand_ref, ...), custom_call_target="tpu_custom_call" | custom-call | flops 1000000000 | bytes 1048576 | tf_op jit(solution)/shard_map/near/pallas_call | solution.py:325
  14.4 2.4 %far.1 = (bf16[48,512]{1,0:T(8,128)(2,1)S(1)}, bf16[48,512]{1,0:T(8,128)(2,1)S(1)}, bf16[48,512]{1,0:T(8,128)(2,1)S(1)}, bf16[48,512]{1,0:T(8,128)(2,1)S(1)}) custom-call(s32[8,128]{1,0:T(8,128)S(1)} %get-tuple-element.35.target_ref, s32[4,8,128]{2,1,0:T(8,128)S(1)} %collective-permute-done.3.cand_ref, bf16[1024,1024]{1,0:T(8,128)(2,1)S(1)} %copy-done.1, ...), custom_call_target="tpu_custom_call" | custom-call | flops 3000000000 | bytes 1048576 | tf_op jit(solution)/shard_map/far/pallas_call | solution.py:333
  16.8 1.9 %collective-permute-start.4 = (bf16[48,512]{1,0:T(8,128)(2,1)S(1)}, bf16[48,512]{1,0:T(8,128)(2,1)S(1)}, u32[]{:S(2)}, u32[]{:S(2)}) collective-permute-start(bf16[48,512]{1,0:T(8,128)(2,1)S(1)} %get-tuple-element.54), channel_id=1, source_target_pairs={{0,8},{2,10},{4,12},{6,14},{8,0},{10,2},{12,4},{14,6},{1,9},{3,11}... | collective-permute-start | bytes 147464 | tf_op jit(solution)/shard_map/ppermute | solution.py:282
  18.7 2.1 %collective-permute-start.5 = (bf16[48,512]{1,0:T(8,128)(2,1)S(1)}, bf16[48,512]{1,0:T(8,128)(2,1)S(1)}, u32[]{:S(2)}, u32[]{:S(2)}) collective-permute-start(bf16[48,512]{1,0:T(8,128)(2,1)S(1)} %get-tuple-element.55), channel_id=1, source_target_pairs={{0,14},{2,12},{4,10},{6,8},{8,6},{10,4},{12,2},{14,0},{1,15},{3,13... | collective-permute-start | bytes 147464 | tf_op jit(solution)/shard_map/ppermute | solution.py:282
  20.8 1.9 %collective-permute-start.6 = (bf16[48,512]{1,0:T(8,128)(2,1)S(1)}, bf16[48,512]{1,0:T(8,128)(2,1)S(1)}, u32[]{:S(2)}, u32[]{:S(2)}) collective-permute-start(bf16[48,512]{1,0:T(8,128)(2,1)S(1)} %get-tuple-element.56), channel_id=1, source_target_pairs={{0,10},{2,8},{4,14},{6,12},{8,2},{10,0},{12,6},{14,4},{1,11},{3,9}... | collective-permute-start | bytes 147464 | tf_op jit(solution)/shard_map/ppermute | solution.py:282
  22.7 0.9 %collective-permute-start.7 = (bf16[48,512]{1,0:T(8,128)(2,1)S(1)}, bf16[48,512]{1,0:T(8,128)(2,1)S(1)}, u32[]{:S(2)}, u32[]{:S(2)}) collective-permute-start(bf16[48,512]{1,0:T(8,128)(2,1)S(1)} %get-tuple-element.57), channel_id=1, source_target_pairs={{0,12},{2,14},{4,8},{6,10},{8,4},{10,6},{12,0},{14,2},{1,13},{3,15... | collective-permute-start | bytes 147464 | tf_op jit(solution)/shard_map/ppermute | solution.py:282
  23.6 1.5 %collective-permute-start.8 = (bf16[48,512]{1,0:T(8,128)(2,1)S(1)}, bf16[48,512]{1,0:T(8,128)(2,1)S(1)}, u32[]{:S(2)}, u32[]{:S(2)}) collective-permute-start(bf16[48,512]{1,0:T(8,128)(2,1)S(1)} %get-tuple-element.58), channel_id=1, source_target_pairs={{0,6},{2,4},{4,2},{6,0},{8,14},{10,12},{12,10},{14,8},{1,7},{3,5},... | collective-permute-start | bytes 147464 | tf_op jit(solution)/shard_map/ppermute | solution.py:282
  25.2 0.5 %collective-permute-start.9 = (bf16[48,512]{1,0:T(8,128)(2,1)S(1)}, bf16[48,512]{1,0:T(8,128)(2,1)S(1)}, u32[]{:S(2)}, u32[]{:S(2)}) collective-permute-start(bf16[48,512]{1,0:T(8,128)(2,1)S(1)} %get-tuple-element.59), channel_id=1, source_target_pairs={{0,4},{2,6},{4,0},{6,2},{8,12},{10,14},{12,8},{14,10},{1,5},{3,7},... | collective-permute-start | bytes 147464 | tf_op jit(solution)/shard_map/ppermute | solution.py:282
  25.7 0.2 collective-permute-done.5.rest_1_
  25.8 1.3 %collective-permute-start.10 = (bf16[48,512]{1,0:T(8,128)(2,1)S(1)}, bf16[48,512]{1,0:T(8,128)(2,1)S(1)}, u32[]{:S(2)}, u32[]{:S(2)}) collective-permute-start(bf16[48,512]{1,0:T(8,128)(2,1)S(1)} %get-tuple-element.60), channel_id=1, source_target_pairs={{0,2},{2,0},{4,6},{6,4},{8,10},{10,8},{12,14},{14,12},{1,3},{3,1},... | collective-permute-start | bytes 147464 | tf_op jit(solution)/shard_map/ppermute | solution.py:282
  27.1 2.0 %own.1 = (f32[128,512]{1,0:T(8,128)S(1)}, f32[128,512]{1,0:T(8,128)S(1)}, bf16[512,512]{1,0:T(8,128)(2,1)S(1)}, bf16[512,512]{1,0:T(8,128)(2,1)S(1)}) custom-call(s32[8,128]{1,0:T(8,128)S(1)} %get-tuple-element.35.target_ref, bf16[48,512]{1,0:T(8,128)(2,1)S(1)} %get-tuple-element.47.sent_ref.rest_7_, f32[8,128]{1,0:T(8,128)S(1)} %bitcast.12, ...), custom_call_target="tpu_custom_call" | custom-call | flops 1000000000 | bytes 1048576 | tf_op jit(solution)/shard_map/own/pallas_call | solution.py:346
  29.3 0.7 %collective-permute-done.10.rest_6_ = bf16[48,512]{1,0:T(8,128)(2,1)S(1)} collective-permute-done((bf16[48,512]{1,0:T(8,128)(2,1)S(1)}, bf16[48,512]{1,0:T(8,128)(2,1)S(1)}, u32[]{:S(2)}, u32[]{:S(2)}) %collective-permute-start.10) | collective-permute-done | bytes 49184 | tf_op jit(solution)/shard_map/ppermute | solution.py:282
  29.9 0.9 %mix.1 = (bf16[128,512]{1,0:T(8,128)(2,1)S(1)}, bf16[128,512]{1,0:T(8,128)(2,1)S(1)}) custom-call(f32[128,512]{1,0:T(8,128)S(1)} %get-tuple-element.49.gate_ref, f32[128,512]{1,0:T(8,128)S(1)} %get-tuple-element.50.self_ref, bf16[128,384]{1,0:T(8,128)(2,1)S(1)} %get-tuple-element.51.assign_ref, f32[128,128]{1,0:T(8,128)S(1)} %get-tuple-element.52.scale_ref, ...), custom_call_target="tpu_custom_call" | custom-call | flops 1000000000 | bytes 1048576 | tf_op jit(solution)/shard_map/mix/pallas_call | solution.py:355
  30.9 0.2 keep.1
  31.1 1.1 %collective-permute-done.11 = bf16[128,512]{1,0:T(8,128)(2,1)S(1)} collective-permute-done((bf16[128,512]{1,0:T(8,128)(2,1)S(1)}, bf16[128,512]{1,0:T(8,128)(2,1)S(1)}, u32[]{:S(2)}, u32[]{:S(2)}) %collective-permute-start.11) | collective-permute-done | bytes 131104 | tf_op jit(solution)/shard_map/ppermute | solution.py:362
  32.2 0.7 %add_convert_fusion = bf16[128,512]{1,0:T(8,128)(2,1)} fusion(f32[128,512]{1,0:T(8,128)S(1)} %keep.1, bf16[128,512]{1,0:T(8,128)(2,1)S(1)} %collective-permute-done.11), kind=kLoop, calls=%fused_computation | loop fusion | flops 196608 | bytes 524288 | tf_op jit(solution)/shard_map/convert_element_type | solution.py:366
  (29 shorter events, 0.4 us)
Async XLA Ops:
  0.8 4.8 %copy-start.1 = (bf16[1024,1024]{1,0:T(8,128)(2,1)S(1)}, bf16[1024,1024]{1,0:T(8,128)(2,1)}, u32[]{:S(2)}) copy-start(bf16[1024,1024]{1,0:T(8,128)(2,1)} %table_ref.5) | copy-start | bytes 6291460
  0.8 4.8 %copy-start.5 = (f32[128,8]{0,1:T(8,128)S(1)}, f32[128,8]{0,1:T(8,128)}, u32[]{:S(2)}) copy-start(f32[128,8]{0,1:T(8,128)} %param.18) | copy-start | bytes 12292
  0.9 4.8 %copy-start.6 = (s32[1024]{0:T(1024)S(1)}, s32[1024]{0:T(1024)}, u32[]{:S(2)}) copy-start(s32[1024]{0:T(1024)} %param.13) | copy-start | bytes 12292
  0.9 4.8 %copy-start.7 = (s32[8]{0:T(128)S(1)}, s32[8]{0:T(128)}, u32[]{:S(2)}) copy-start(s32[8]{0:T(128)} %lens_ref.1) | copy-start | bytes 100
  0.9 6.2 %collective-permute-start.2 = (s32[8,128]{1,0:T(8,128)S(1)}, s32[8,128]{1,0:T(8,128)S(1)}, u32[]{:S(2)}, u32[]{:S(2)}) collective-permute-start(s32[8,128]{1,0:T(8,128)S(1)} %payload.1.cand_ref), channel_id=1, source_target_pairs={{0,6},{2,4},{4,2},{6,0},{8,14},{10,12},{12,10},{14,8},{1,7},{3,5},... | collective-permute-start | bytes 12296 | tf_op jit(solution)/shard_map/ppermute | solution.py:282
  4.9 3.6 %collective-permute-start.1 = (s32[8,128]{1,0:T(8,128)S(1)}, s32[8,128]{1,0:T(8,128)S(1)}, u32[]{:S(2)}, u32[]{:S(2)}) collective-permute-start(s32[8,128]{1,0:T(8,128)S(1)} %payload.1.cand_ref), channel_id=1, source_target_pairs={{0,4},{2,6},{4,0},{6,2},{8,12},{10,14},{12,8},{14,10},{1,5},{3,7},... | collective-permute-start | bytes 12296 | tf_op jit(solution)/shard_map/ppermute | solution.py:282
  5.4 3.6 %collective-permute-start = (s32[8,128]{1,0:T(8,128)S(1)}, s32[8,128]{1,0:T(8,128)S(1)}, u32[]{:S(2)}, u32[]{:S(2)}) collective-permute-start(s32[8,128]{1,0:T(8,128)S(1)} %payload.1.cand_ref), channel_id=1, source_target_pairs={{0,2},{2,0},{4,6},{6,4},{8,10},{10,8},{12,14},{14,12},{1,3},{3,1},... | collective-permute-start | bytes 12296 | tf_op jit(solution)/shard_map/ppermute | solution.py:282
  5.6 5.9 %copy-start = (bf16[1024,4,512]{2,1,0:T(4,128)(2,1)S(1)}, bf16[1024,4,512]{2,1,0:T(4,128)(2,1)}, u32[]{:S(2)}) copy-start(bf16[1024,4,512]{2,1,0:T(4,128)(2,1)} %win_ref.3) | copy-start | bytes 12582916
  5.7 5.9 %copy-start.3 = (bf16[1024,512]{1,0:T(8,128)(2,1)S(1)}, bf16[1024,512]{1,0:T(8,128)(2,1)}, u32[]{:S(2)}) copy-start(bf16[1024,512]{1,0:T(8,128)(2,1)} %key_ref.3) | copy-start | bytes 3145732
  5.7 5.9 %copy-start.4 = (bf16[1024,512]{1,0:T(8,128)(2,1)S(1)}, bf16[1024,512]{1,0:T(8,128)(2,1)}, u32[]{:S(2)}) copy-start(bf16[1024,512]{1,0:T(8,128)(2,1)} %value_ref.3) | copy-start | bytes 3145732
  9.0 5.4 %collective-permute-start.3 = (s32[4,8,128]{2,1,0:T(8,128)S(1)}, s32[4,8,128]{2,1,0:T(8,128)S(1)}, u32[]{:S(2)}, u32[]{:S(2)}) collective-permute-start(s32[4,8,128]{2,1,0:T(8,128)S(1)} %pad_add_fusion.cand_ref), channel_id=1, source_target_pairs={{0,8},{2,10},{4,12},{6,14},{8,0},{10,2},{12,4},{14,6},{1,9},{3,11}... | collective-permute-start | bytes 49160 | tf_op jit(solution)/shard_map/ppermute | solution.py:282
  14.4 12.8 %copy-start.2 = (bf16[512,1024]{1,0:T(8,128)(2,1)S(1)}, bf16[512,1024]{1,0:T(8,128)(2,1)}, u32[]{:S(2)}) copy-start(bf16[512,1024]{1,0:T(8,128)(2,1)} %wout_ref.1) | copy-start | bytes 3145732
  16.8 8.3 %collective-permute-start.4 = (bf16[48,512]{1,0:T(8,128)(2,1)S(1)}, bf16[48,512]{1,0:T(8,128)(2,1)S(1)}, u32[]{:S(2)}, u32[]{:S(2)}) collective-permute-start(bf16[48,512]{1,0:T(8,128)(2,1)S(1)} %get-tuple-element.54), channel_id=1, source_target_pairs={{0,8},{2,10},{4,12},{6,14},{8,0},{10,2},{12,4},{14,6},{1,9},{3,11}... | collective-permute-start | bytes 147464 | tf_op jit(solution)/shard_map/ppermute | solution.py:282
  18.7 7.1 %collective-permute-start.5 = (bf16[48,512]{1,0:T(8,128)(2,1)S(1)}, bf16[48,512]{1,0:T(8,128)(2,1)S(1)}, u32[]{:S(2)}, u32[]{:S(2)}) collective-permute-start(bf16[48,512]{1,0:T(8,128)(2,1)S(1)} %get-tuple-element.55), channel_id=1, source_target_pairs={{0,14},{2,12},{4,10},{6,8},{8,6},{10,4},{12,2},{14,0},{1,15},{3,13... | collective-permute-start | bytes 147464 | tf_op jit(solution)/shard_map/ppermute | solution.py:282
  20.8 8.4 %collective-permute-start.6 = (bf16[48,512]{1,0:T(8,128)(2,1)S(1)}, bf16[48,512]{1,0:T(8,128)(2,1)S(1)}, u32[]{:S(2)}, u32[]{:S(2)}) collective-permute-start(bf16[48,512]{1,0:T(8,128)(2,1)S(1)} %get-tuple-element.56), channel_id=1, source_target_pairs={{0,10},{2,8},{4,14},{6,12},{8,2},{10,0},{12,6},{14,4},{1,11},{3,9}... | collective-permute-start | bytes 147464 | tf_op jit(solution)/shard_map/ppermute | solution.py:282
  22.7 6.4 %collective-permute-start.7 = (bf16[48,512]{1,0:T(8,128)(2,1)S(1)}, bf16[48,512]{1,0:T(8,128)(2,1)S(1)}, u32[]{:S(2)}, u32[]{:S(2)}) collective-permute-start(bf16[48,512]{1,0:T(8,128)(2,1)S(1)} %get-tuple-element.57), channel_id=1, source_target_pairs={{0,12},{2,14},{4,8},{6,10},{8,4},{10,6},{12,0},{14,2},{1,13},{3,15... | collective-permute-start | bytes 147464 | tf_op jit(solution)/shard_map/ppermute | solution.py:282
  23.6 5.5 %collective-permute-start.8 = (bf16[48,512]{1,0:T(8,128)(2,1)S(1)}, bf16[48,512]{1,0:T(8,128)(2,1)S(1)}, u32[]{:S(2)}, u32[]{:S(2)}) collective-permute-start(bf16[48,512]{1,0:T(8,128)(2,1)S(1)} %get-tuple-element.58), channel_id=1, source_target_pairs={{0,6},{2,4},{4,2},{6,0},{8,14},{10,12},{12,10},{14,8},{1,7},{3,5},... | collective-permute-start | bytes 147464 | tf_op jit(solution)/shard_map/ppermute | solution.py:282
  25.2 4.1 %collective-permute-start.9 = (bf16[48,512]{1,0:T(8,128)(2,1)S(1)}, bf16[48,512]{1,0:T(8,128)(2,1)S(1)}, u32[]{:S(2)}, u32[]{:S(2)}) collective-permute-start(bf16[48,512]{1,0:T(8,128)(2,1)S(1)} %get-tuple-element.59), channel_id=1, source_target_pairs={{0,4},{2,6},{4,0},{6,2},{8,12},{10,14},{12,8},{14,10},{1,5},{3,7},... | collective-permute-start | bytes 147464 | tf_op jit(solution)/shard_map/ppermute | solution.py:282
  25.8 4.1 %collective-permute-start.10 = (bf16[48,512]{1,0:T(8,128)(2,1)S(1)}, bf16[48,512]{1,0:T(8,128)(2,1)S(1)}, u32[]{:S(2)}, u32[]{:S(2)}) collective-permute-start(bf16[48,512]{1,0:T(8,128)(2,1)S(1)} %get-tuple-element.60), channel_id=1, source_target_pairs={{0,2},{2,0},{4,6},{6,4},{8,10},{10,8},{12,14},{14,12},{1,3},{3,1},... | collective-permute-start | bytes 147464 | tf_op jit(solution)/shard_map/ppermute | solution.py:282
  30.8 1.4 %collective-permute-start.11 = (bf16[128,512]{1,0:T(8,128)(2,1)S(1)}, bf16[128,512]{1,0:T(8,128)(2,1)S(1)}, u32[]{:S(2)}, u32[]{:S(2)}) collective-permute-start(bf16[128,512]{1,0:T(8,128)(2,1)S(1)} %get-tuple-element.64), channel_id=1, source_target_pairs={{0,1},{1,0},{2,3},{3,2},{4,5},{5,4},{6,7},{7,6},{8,9},{9,8},{10,11... | collective-permute-start | bytes 393224 | tf_op jit(solution)/shard_map/ppermute | solution.py:362

commit v7 on v6

--- a/solution.py
+++ b/solution.py
@@ -338,11 +338,7 @@
         [vmem] * 7,
         scratch,
     )(target, far_cand, code_table, wq, line, hist_keys, hist_values)
-    early = []
-    late = [m for m in range(owners) if m not in early]
-    sums = list(near) + list(far)
-    tied = lax.optimization_barrier(tuple(sums[m] for m in late))
-    sent = [tied[late.index(m)] if m in late else sums[m] for m in range(owners)]
+    sent = list(lax.optimization_barrier(tuple(near) + tuple(far)))
     gate, self_term, wout_mine, wout_other = call(
         functools.partial(own_kernel, heads),
         "own",
@@ -350,7 +346,7 @@
         [full((cand, cols), F32)] * 2 + [full((cols, width // 2), BF16)] * 2,
         [vmem] * 6,
     )(target, sent[0], bias, normed, proj_in, proj_out)
-    turns = [4, 7, 5, 6, 3, 2, 1] if owners == 8 else list(range(owners - 1, 0, -1))
+    turns = [4, 6, 5, 7, 3, 2, 1] if owners == 8 else list(range(owners - 1, 0, -1))
     received = [swap(sent[m], m) for m in turns] + [sent[0]]
     mixed, send = call(
         functools.partial(mix_kernel, heads, turns),

time: 33 us -> 32.8 us (level)
  waiting for transfers between devices: 3.93 us -> 3.55 us
    ppermute x11, waiting for transfers between devices: 2.83 us -> 2.45 us  [swap(): return lax.ppermute(x, 'ctx', [(i, i ^ mask) for i in range(owners)])]
  transfers between devices with their start and end apart: 12 -> 12, of which waited for: 6 -> 5; matrix products, arithmetic and copies ran while one was open for 0% -> 0% of each run, Pallas kernels for 19% -> 19%
where the time goes in v7:
time: 32.8 us; the launch traced here: 32.7 us
  starting transfers between devices  17.7 us (54%)
  Pallas kernels  9.67 us (29%)
  waiting for transfers between devices  3.55 us (11%)
  other arithmetic  1.53 us (5%)
    ppermute x11, starting transfers between devices, swap(): return lax.ppermute(x, 'ctx', [(i, i ^ mask) for i in range(owners)])  17.6 us
    pallas_call x1, Pallas kernels, body(): call(functools.partial(near_kernel, parts, levels, heads, stack, scale),...  2.77 us
    ppermute x11, waiting for transfers between devices, swap(): return lax.ppermute(x, 'ctx', [(i, i ^ mask) for i in range(owners)])  2.45 us
    pallas_call x1, Pallas kernels, body(): call(functools.partial(far_kernel, parts, levels, heads, stack, scale), '...  2.45 us
    pallas_call x1, Pallas kernels, body(): call(functools.partial(own_kernel, heads), 'own', 1000000000, [full((cand...  1.99 us
    pallas_call x1, Pallas kernels, body(): call(functools.partial(prepare_kernel, levels, heads, parts), 'prepare',...  1.38 us
    ppermute x1, waiting for transfers between devices, body(): other = lax.ppermute(send, 'head', [(0, 1), (1, 0)])  1.09 us
    pallas_call x1, Pallas kernels, body(): call(functools.partial(mix_kernel, heads, turns), 'mix', 1000000000, [ful...  0.85 us
  transfers between devices with their start and end apart: 12, of which 5 were waited for; matrix products, arithmetic and copies ran while one was open for 0% of the time, Pallas kernels for 19%

profile of v7, /device:TPU:0, one launch (start us, length us, event | category | flops | bytes accessed | tf_op | source)
XLA Modules:
  0.0 32.7 jit_solution(411707150248173899)
XLA Ops:
  0.1 0.8 %add_add_fusion.cand_ref = s32[8,128]{1,0:T(8,128)S(1)} fusion(s32[1,128]{1,0:T(1,128)} %bitcast.18, s32[4,128]{1,0:T(4,128)} %bitcast.17, s32[8]{0:T(128)S(1)} %pad.6.clone), kind=kLoop, calls=%fused_computation.2 | loop fusion | flops 2048 | bytes 6688 | tf_op jit(solution)/shard_map/concatenate | solution.py:296
  0.9 4.0 %collective-permute-start.2 = (s32[8,128]{1,0:T(8,128)S(1)}, s32[8,128]{1,0:T(8,128)S(1)}, u32[]{:S(2)}, u32[]{:S(2)}) collective-permute-start(s32[8,128]{1,0:T(8,128)S(1)} %payload.1.cand_ref), channel_id=1, source_target_pairs={{0,6},{2,4},{4,2},{6,0},{8,14},{10,12},{12,10},{14,8},{1,7},{3,5},... | collective-permute-start | bytes 12296 | tf_op jit(solution)/shard_map/ppermute | solution.py:282
  4.9 0.4 %collective-permute-start.1 = (s32[8,128]{1,0:T(8,128)S(1)}, s32[8,128]{1,0:T(8,128)S(1)}, u32[]{:S(2)}, u32[]{:S(2)}) collective-permute-start(s32[8,128]{1,0:T(8,128)S(1)} %payload.1.cand_ref), channel_id=1, source_target_pairs={{0,4},{2,6},{4,0},{6,2},{8,12},{10,14},{12,8},{14,10},{1,5},{3,7},... | collective-permute-start | bytes 12296 | tf_op jit(solution)/shard_map/ppermute | solution.py:282
  5.4 0.2 collective-permute-start
  5.7 1.4 %prepare.1 = (bf16[128,1024]{1,0:T(8,128)(2,1)S(1)}, f32[128,512]{1,0:T(8,128)S(1)}, bf16[128,384]{1,0:T(8,128)(2,1)S(1)}, f32[128,128]{1,0:T(8,128)S(1)}, f32[8...) custom-call(s32[2]{0:T(128)S(1)} %pad_add_fusion.1.me_ref, s32[8]{0:T(128)S(1)} %copy-done.7, ...), custom_call_target="tpu_custom_call" | custom-call | flops 8000000000 | bytes 1048576 | tf_op jit(solution)/shard_map/prepare/pallas_call | solution.py:302
  7.1 1.4 %collective-permute-done.1 = s32[8,128]{1,0:T(8,128)S(1)} collective-permute-done((s32[8,128]{1,0:T(8,128)S(1)}, s32[8,128]{1,0:T(8,128)S(1)}, u32[]{:S(2)}, u32[]{:S(2)}) %collective-permute-start.1) | collective-permute-done | bytes 4128 | tf_op jit(solution)/shard_map/ppermute | solution.py:282
  8.5 0.4 %collective-permute-done = s32[8,128]{1,0:T(8,128)S(1)} collective-permute-done((s32[8,128]{1,0:T(8,128)S(1)}, s32[8,128]{1,0:T(8,128)S(1)}, u32[]{:S(2)}, u32[]{:S(2)}) %collective-permute-start) | collective-permute-done | bytes 4128 | tf_op jit(solution)/shard_map/ppermute | solution.py:282
  9.0 2.6 %collective-permute-start.3 = (s32[4,8,128]{2,1,0:T(8,128)S(1)}, s32[4,8,128]{2,1,0:T(8,128)S(1)}, u32[]{:S(2)}, u32[]{:S(2)}) collective-permute-start(s32[4,8,128]{2,1,0:T(8,128)S(1)} %pad_add_fusion.cand_ref), channel_id=1, source_target_pairs={{0,8},{2,10},{4,12},{6,14},{8,0},{10,2},{12,4},{14,6},{1,9},{3,11}... | collective-permute-start | bytes 49160 | tf_op jit(solution)/shard_map/ppermute | solution.py:282
  11.6 2.8 %near.1 = (bf16[48,512]{1,0:T(8,128)(2,1)S(1)}, bf16[48,512]{1,0:T(8,128)(2,1)S(1)}, bf16[48,512]{1,0:T(8,128)(2,1)S(1)}, bf16[48,512]{1,0:T(8,128)(2,1)S(1)}, bf16[1024,512]{1,0:T(8,128)(2,1)S(1)}) custom-call(s32[8,128]{1,0:T(8,128)S(1)} %get-tuple-element.35.target_ref, s32[4,8,128]{2,1,0:T(8,128)S(1)} %pad_add_fusion.cand_ref, ...), custom_call_target="tpu_custom_call" | custom-call | flops 1000000000 | bytes 1048576 | tf_op jit(solution)/shard_map/near/pallas_call | solution.py:325
  14.4 2.4 %far.1 = (bf16[48,512]{1,0:T(8,128)(2,1)S(1)}, bf16[48,512]{1,0:T(8,128)(2,1)S(1)}, bf16[48,512]{1,0:T(8,128)(2,1)S(1)}, bf16[48,512]{1,0:T(8,128)(2,1)S(1)}) custom-call(s32[8,128]{1,0:T(8,128)S(1)} %get-tuple-element.35.target_ref, s32[4,8,128]{2,1,0:T(8,128)S(1)} %collective-permute-done.3.cand_ref, bf16[1024,1024]{1,0:T(8,128)(2,1)S(1)} %copy-done.1, ...), custom_call_target="tpu_custom_call" | custom-call | flops 3000000000 | bytes 1048576 | tf_op jit(solution)/shard_map/far/pallas_call | solution.py:333
  16.8 1.9 %collective-permute-start.4 = (bf16[48,512]{1,0:T(8,128)(2,1)S(1)}, bf16[48,512]{1,0:T(8,128)(2,1)S(1)}, u32[]{:S(2)}, u32[]{:S(2)}) collective-permute-start(bf16[48,512]{1,0:T(8,128)(2,1)S(1)} %get-tuple-element.54), channel_id=1, source_target_pairs={{0,8},{2,10},{4,12},{6,14},{8,0},{10,2},{12,4},{14,6},{1,9},{3,11}... | collective-permute-start | bytes 147464 | tf_op jit(solution)/shard_map/ppermute | solution.py:282
  18.7 2.1 %collective-permute-start.5 = (bf16[48,512]{1,0:T(8,128)(2,1)S(1)}, bf16[48,512]{1,0:T(8,128)(2,1)S(1)}, u32[]{:S(2)}, u32[]{:S(2)}) collective-permute-start(bf16[48,512]{1,0:T(8,128)(2,1)S(1)} %get-tuple-element.55), channel_id=1, source_target_pairs={{0,12},{2,14},{4,8},{6,10},{8,4},{10,6},{12,0},{14,2},{1,13},{3,15... | collective-permute-start | bytes 147464 | tf_op jit(solution)/shard_map/ppermute | solution.py:282
  20.8 0.9 %collective-permute-start.6 = (bf16[48,512]{1,0:T(8,128)(2,1)S(1)}, bf16[48,512]{1,0:T(8,128)(2,1)S(1)}, u32[]{:S(2)}, u32[]{:S(2)}) collective-permute-start(bf16[48,512]{1,0:T(8,128)(2,1)S(1)} %get-tuple-element.56), channel_id=1, source_target_pairs={{0,10},{2,8},{4,14},{6,12},{8,2},{10,0},{12,6},{14,4},{1,11},{3,9}... | collective-permute-start | bytes 147464 | tf_op jit(solution)/shard_map/ppermute | solution.py:282
  21.8 1.9 %collective-permute-start.7 = (bf16[48,512]{1,0:T(8,128)(2,1)S(1)}, bf16[48,512]{1,0:T(8,128)(2,1)S(1)}, u32[]{:S(2)}, u32[]{:S(2)}) collective-permute-start(bf16[48,512]{1,0:T(8,128)(2,1)S(1)} %get-tuple-element.57), channel_id=1, source_target_pairs={{0,14},{2,12},{4,10},{6,8},{8,6},{10,4},{12,2},{14,0},{1,15},{3,13... | collective-permute-start | bytes 147464 | tf_op jit(solution)/shard_map/ppermute | solution.py:282
  23.6 1.5 %collective-permute-start.8 = (bf16[48,512]{1,0:T(8,128)(2,1)S(1)}, bf16[48,512]{1,0:T(8,128)(2,1)S(1)}, u32[]{:S(2)}, u32[]{:S(2)}) collective-permute-start(bf16[48,512]{1,0:T(8,128)(2,1)S(1)} %get-tuple-element.58), channel_id=1, source_target_pairs={{0,6},{2,4},{4,2},{6,0},{8,14},{10,12},{12,10},{14,8},{1,7},{3,5},... | collective-permute-start | bytes 147464 | tf_op jit(solution)/shard_map/ppermute | solution.py:282
  25.2 0.4 %collective-permute-start.9 = (bf16[48,512]{1,0:T(8,128)(2,1)S(1)}, bf16[48,512]{1,0:T(8,128)(2,1)S(1)}, u32[]{:S(2)}, u32[]{:S(2)}) collective-permute-start(bf16[48,512]{1,0:T(8,128)(2,1)S(1)} %get-tuple-element.59), channel_id=1, source_target_pairs={{0,4},{2,6},{4,0},{6,2},{8,12},{10,14},{12,8},{14,10},{1,5},{3,7},... | collective-permute-start | bytes 147464 | tf_op jit(solution)/shard_map/ppermute | solution.py:282
  25.6 1.5 %collective-permute-start.10 = (bf16[48,512]{1,0:T(8,128)(2,1)S(1)}, bf16[48,512]{1,0:T(8,128)(2,1)S(1)}, u32[]{:S(2)}, u32[]{:S(2)}) collective-permute-start(bf16[48,512]{1,0:T(8,128)(2,1)S(1)} %get-tuple-element.60), channel_id=1, source_target_pairs={{0,2},{2,0},{4,6},{6,4},{8,10},{10,8},{12,14},{14,12},{1,3},{3,1},... | collective-permute-start | bytes 147464 | tf_op jit(solution)/shard_map/ppermute | solution.py:282
  27.1 2.0 %own.1 = (f32[128,512]{1,0:T(8,128)S(1)}, f32[128,512]{1,0:T(8,128)S(1)}, bf16[512,512]{1,0:T(8,128)(2,1)S(1)}, bf16[512,512]{1,0:T(8,128)(2,1)S(1)}) custom-call(s32[8,128]{1,0:T(8,128)S(1)} %get-tuple-element.35.target_ref, bf16[48,512]{1,0:T(8,128)(2,1)S(1)} %get-tuple-element.47.sent_ref.rest_7_, f32[8,128]{1,0:T(8,128)S(1)} %bitcast.12, ...), custom_call_target="tpu_custom_call" | custom-call | flops 1000000000 | bytes 1048576 | tf_op jit(solution)/shard_map/own/pallas_call | solution.py:342
  29.2 0.1 collective-permute-done.9.rest_5_
  29.3 0.5 %collective-permute-done.10.rest_6_ = bf16[48,512]{1,0:T(8,128)(2,1)S(1)} collective-permute-done((bf16[48,512]{1,0:T(8,128)(2,1)S(1)}, bf16[48,512]{1,0:T(8,128)(2,1)S(1)}, u32[]{:S(2)}, u32[]{:S(2)}) %collective-permute-start.10) | collective-permute-done | bytes 49184 | tf_op jit(solution)/shard_map/ppermute | solution.py:282
  29.7 0.8 %mix.1 = (bf16[128,512]{1,0:T(8,128)(2,1)S(1)}, bf16[128,512]{1,0:T(8,128)(2,1)S(1)}) custom-call(f32[128,512]{1,0:T(8,128)S(1)} %get-tuple-element.49.gate_ref, f32[128,512]{1,0:T(8,128)S(1)} %get-tuple-element.50.self_ref, bf16[128,384]{1,0:T(8,128)(2,1)S(1)} %get-tuple-element.51.assign_ref, f32[128,128]{1,0:T(8,128)S(1)} %get-tuple-element.52.scale_ref, ...), custom_call_target="tpu_custom_call" | custom-call | flops 1000000000 | bytes 1048576 | tf_op jit(solution)/shard_map/mix/pallas_call | solution.py:351
  30.7 0.2 keep.1
  30.9 1.1 %collective-permute-done.11 = bf16[128,512]{1,0:T(8,128)(2,1)S(1)} collective-permute-done((bf16[128,512]{1,0:T(8,128)(2,1)S(1)}, bf16[128,512]{1,0:T(8,128)(2,1)S(1)}, u32[]{:S(2)}, u32[]{:S(2)}) %collective-permute-start.11) | collective-permute-done | bytes 131104 | tf_op jit(solution)/shard_map/ppermute | solution.py:358
  32.0 0.7 %add_convert_fusion = bf16[128,512]{1,0:T(8,128)(2,1)} fusion(f32[128,512]{1,0:T(8,128)S(1)} %keep.1, bf16[128,512]{1,0:T(8,128)(2,1)S(1)} %collective-permute-done.11), kind=kLoop, calls=%fused_computation | loop fusion | flops 196608 | bytes 524288 | tf_op jit(solution)/shard_map/convert_element_type | solution.py:362
  (29 shorter events, 0.3 us)
Async XLA Ops:
  0.8 4.8 %copy-start.1 = (bf16[1024,1024]{1,0:T(8,128)(2,1)S(1)}, bf16[1024,1024]{1,0:T(8,128)(2,1)}, u32[]{:S(2)}) copy-start(bf16[1024,1024]{1,0:T(8,128)(2,1)} %table_ref.5) | copy-start | bytes 6291460
  0.8 4.8 %copy-start.5 = (f32[128,8]{0,1:T(8,128)S(1)}, f32[128,8]{0,1:T(8,128)}, u32[]{:S(2)}) copy-start(f32[128,8]{0,1:T(8,128)} %param.18) | copy-start | bytes 12292
  0.9 4.8 %copy-start.6 = (s32[1024]{0:T(1024)S(1)}, s32[1024]{0:T(1024)}, u32[]{:S(2)}) copy-start(s32[1024]{0:T(1024)} %param.13) | copy-start | bytes 12292
  0.9 4.8 %copy-start.7 = (s32[8]{0:T(128)S(1)}, s32[8]{0:T(128)}, u32[]{:S(2)}) copy-start(s32[8]{0:T(128)} %lens_ref.1) | copy-start | bytes 100
  0.9 6.2 %collective-permute-start.2 = (s32[8,128]{1,0:T(8,128)S(1)}, s32[8,128]{1,0:T(8,128)S(1)}, u32[]{:S(2)}, u32[]{:S(2)}) collective-permute-start(s32[8,128]{1,0:T(8,128)S(1)} %payload.1.cand_ref), channel_id=1, source_target_pairs={{0,6},{2,4},{4,2},{6,0},{8,14},{10,12},{12,10},{14,8},{1,7},{3,5},... | collective-permute-start | bytes 12296 | tf_op jit(solution)/shard_map/ppermute | solution.py:282
  4.9 3.6 %collective-permute-start.1 = (s32[8,128]{1,0:T(8,128)S(1)}, s32[8,128]{1,0:T(8,128)S(1)}, u32[]{:S(2)}, u32[]{:S(2)}) collective-permute-start(s32[8,128]{1,0:T(8,128)S(1)} %payload.1.cand_ref), channel_id=1, source_target_pairs={{0,4},{2,6},{4,0},{6,2},{8,12},{10,14},{12,8},{14,10},{1,5},{3,7},... | collective-permute-start | bytes 12296 | tf_op jit(solution)/shard_map/ppermute | solution.py:282
  5.4 3.6 %collective-permute-start = (s32[8,128]{1,0:T(8,128)S(1)}, s32[8,128]{1,0:T(8,128)S(1)}, u32[]{:S(2)}, u32[]{:S(2)}) collective-permute-start(s32[8,128]{1,0:T(8,128)S(1)} %payload.1.cand_ref), channel_id=1, source_target_pairs={{0,2},{2,0},{4,6},{6,4},{8,10},{10,8},{12,14},{14,12},{1,3},{3,1},... | collective-permute-start | bytes 12296 | tf_op jit(solution)/shard_map/ppermute | solution.py:282
  5.6 5.9 %copy-start = (bf16[1024,4,512]{2,1,0:T(4,128)(2,1)S(1)}, bf16[1024,4,512]{2,1,0:T(4,128)(2,1)}, u32[]{:S(2)}) copy-start(bf16[1024,4,512]{2,1,0:T(4,128)(2,1)} %win_ref.3) | copy-start | bytes 12582916
  5.7 5.9 %copy-start.3 = (bf16[1024,512]{1,0:T(8,128)(2,1)S(1)}, bf16[1024,512]{1,0:T(8,128)(2,1)}, u32[]{:S(2)}) copy-start(bf16[1024,512]{1,0:T(8,128)(2,1)} %key_ref.3) | copy-start | bytes 3145732
  5.7 5.9 %copy-start.4 = (bf16[1024,512]{1,0:T(8,128)(2,1)S(1)}, bf16[1024,512]{1,0:T(8,128)(2,1)}, u32[]{:S(2)}) copy-start(bf16[1024,512]{1,0:T(8,128)(2,1)} %value_ref.3) | copy-start | bytes 3145732
  9.0 5.4 %collective-permute-start.3 = (s32[4,8,128]{2,1,0:T(8,128)S(1)}, s32[4,8,128]{2,1,0:T(8,128)S(1)}, u32[]{:S(2)}, u32[]{:S(2)}) collective-permute-start(s32[4,8,128]{2,1,0:T(8,128)S(1)} %pad_add_fusion.cand_ref), channel_id=1, source_target_pairs={{0,8},{2,10},{4,12},{6,14},{8,0},{10,2},{12,4},{14,6},{1,9},{3,11}... | collective-permute-start | bytes 49160 | tf_op jit(solution)/shard_map/ppermute | solution.py:282
  14.4 12.8 %copy-start.2 = (bf16[512,1024]{1,0:T(8,128)(2,1)S(1)}, bf16[512,1024]{1,0:T(8,128)(2,1)}, u32[]{:S(2)}) copy-start(bf16[512,1024]{1,0:T(8,128)(2,1)} %wout_ref.1) | copy-start | bytes 3145732
  16.8 8.3 %collective-permute-start.4 = (bf16[48,512]{1,0:T(8,128)(2,1)S(1)}, bf16[48,512]{1,0:T(8,128)(2,1)S(1)}, u32[]{:S(2)}, u32[]{:S(2)}) collective-permute-start(bf16[48,512]{1,0:T(8,128)(2,1)S(1)} %get-tuple-element.54), channel_id=1, source_target_pairs={{0,8},{2,10},{4,12},{6,14},{8,0},{10,2},{12,4},{14,6},{1,9},{3,11}... | collective-permute-start | bytes 147464 | tf_op jit(solution)/shard_map/ppermute | solution.py:282
  18.7 6.9 %collective-permute-start.5 = (bf16[48,512]{1,0:T(8,128)(2,1)S(1)}, bf16[48,512]{1,0:T(8,128)(2,1)S(1)}, u32[]{:S(2)}, u32[]{:S(2)}) collective-permute-start(bf16[48,512]{1,0:T(8,128)(2,1)S(1)} %get-tuple-element.55), channel_id=1, source_target_pairs={{0,12},{2,14},{4,8},{6,10},{8,4},{10,6},{12,0},{14,2},{1,13},{3,15... | collective-permute-start | bytes 147464 | tf_op jit(solution)/shard_map/ppermute | solution.py:282
  20.8 8.3 %collective-permute-start.6 = (bf16[48,512]{1,0:T(8,128)(2,1)S(1)}, bf16[48,512]{1,0:T(8,128)(2,1)S(1)}, u32[]{:S(2)}, u32[]{:S(2)}) collective-permute-start(bf16[48,512]{1,0:T(8,128)(2,1)S(1)} %get-tuple-element.56), channel_id=1, source_target_pairs={{0,10},{2,8},{4,14},{6,12},{8,2},{10,0},{12,6},{14,4},{1,11},{3,9}... | collective-permute-start | bytes 147464 | tf_op jit(solution)/shard_map/ppermute | solution.py:282
  21.8 7.4 %collective-permute-start.7 = (bf16[48,512]{1,0:T(8,128)(2,1)S(1)}, bf16[48,512]{1,0:T(8,128)(2,1)S(1)}, u32[]{:S(2)}, u32[]{:S(2)}) collective-permute-start(bf16[48,512]{1,0:T(8,128)(2,1)S(1)} %get-tuple-element.57), channel_id=1, source_target_pairs={{0,14},{2,12},{4,10},{6,8},{8,6},{10,4},{12,2},{14,0},{1,15},{3,13... | collective-permute-start | bytes 147464 | tf_op jit(solution)/shard_map/ppermute | solution.py:282
  23.6 5.5 %collective-permute-start.8 = (bf16[48,512]{1,0:T(8,128)(2,1)S(1)}, bf16[48,512]{1,0:T(8,128)(2,1)S(1)}, u32[]{:S(2)}, u32[]{:S(2)}) collective-permute-start(bf16[48,512]{1,0:T(8,128)(2,1)S(1)} %get-tuple-element.58), channel_id=1, source_target_pairs={{0,6},{2,4},{4,2},{6,0},{8,14},{10,12},{12,10},{14,8},{1,7},{3,5},... | collective-permute-start | bytes 147464 | tf_op jit(solution)/shard_map/ppermute | solution.py:282
  25.2 4.1 %collective-permute-start.9 = (bf16[48,512]{1,0:T(8,128)(2,1)S(1)}, bf16[48,512]{1,0:T(8,128)(2,1)S(1)}, u32[]{:S(2)}, u32[]{:S(2)}) collective-permute-start(bf16[48,512]{1,0:T(8,128)(2,1)S(1)} %get-tuple-element.59), channel_id=1, source_target_pairs={{0,4},{2,6},{4,0},{6,2},{8,12},{10,14},{12,8},{14,10},{1,5},{3,7},... | collective-permute-start | bytes 147464 | tf_op jit(solution)/shard_map/ppermute | solution.py:282
  25.6 4.1 %collective-permute-start.10 = (bf16[48,512]{1,0:T(8,128)(2,1)S(1)}, bf16[48,512]{1,0:T(8,128)(2,1)S(1)}, u32[]{:S(2)}, u32[]{:S(2)}) collective-permute-start(bf16[48,512]{1,0:T(8,128)(2,1)S(1)} %get-tuple-element.60), channel_id=1, source_target_pairs={{0,2},{2,0},{4,6},{6,4},{8,10},{10,8},{12,14},{14,12},{1,3},{3,1},... | collective-permute-start | bytes 147464 | tf_op jit(solution)/shard_map/ppermute | solution.py:282
  30.6 1.4 %collective-permute-start.11 = (bf16[128,512]{1,0:T(8,128)(2,1)S(1)}, bf16[128,512]{1,0:T(8,128)(2,1)S(1)}, u32[]{:S(2)}, u32[]{:S(2)}) collective-permute-start(bf16[128,512]{1,0:T(8,128)(2,1)S(1)} %get-tuple-element.64), channel_id=1, source_target_pairs={{0,1},{1,0},{2,3},{3,2},{4,5},{5,4},{6,7},{7,6},{8,9},{9,8},{10,11... | collective-permute-start | bytes 393224 | tf_op jit(solution)/shard_map/ppermute | solution.py:358

commit v8 on v7

--- a/solution.py
+++ b/solution.py
@@ -35,13 +35,14 @@
     return jnp.where(mask, 1.0, 0.0).astype(BF16)
 
 
-def head_sums(x, head_size):
+def head_sums(x, head_size, split=True):
     rows, cols = x.shape
     tall = jnp.concatenate([x[:, at : at + LANES] for at in range(0, cols, LANES)], axis=0)
     same = ones_where(iota((LANES, LANES), 0) // head_size == iota((LANES, LANES), 1) // head_size)
     high = tall.astype(BF16)
-    low = (tall - high.astype(F32)).astype(BF16)
-    sums = dot(high, same) + dot(low, same)
+    sums = dot(high, same)
+    if split:
+        sums = sums + dot((tall - high.astype(F32)).astype(BF16), same)
     return jnp.concatenate([sums[at : at + rows] for at in range(0, sums.shape[0], rows)], axis=1)
 
 
@@ -237,7 +238,7 @@
     history = dot(assign_ref[...], jnp.concatenate([r[...] for r in received], axis=0))
     attended = history * scale_ref[:, 0:1] + self_ref[...]
     centred = attended - head_sums(attended, head_size) * (1.0 / head_size)
-    var = head_sums(centred * centred, head_size) * (1.0 / head_size)
+    var = head_sums(centred * centred, head_size, split=False) * (1.0 / head_size)
     mixed = (centred * lax.rsqrt(var + 1e-05) * gate_ref[...]).astype(BF16)
     mixed_ref[...] = mixed
     send_ref[...] = dot(mixed, wout_ref[...]).astype(BF16)

time: 32.8 us -> 32.7 us (level)
  transfers between devices with their start and end apart: 12 -> 12, of which waited for: 5 -> 5; matrix products, arithmetic and copies ran while one was open for 0% -> 0% of each run, Pallas kernels for 19% -> 20%
where the time goes in v8:
time: 32.7 us; the launch traced here: 32.6 us
  starting transfers between devices  17.6 us (54%)
  Pallas kernels  9.58 us (29%)
  waiting for transfers between devices  3.55 us (11%)
  other arithmetic  1.53 us (5%)
    ppermute x11, starting transfers between devices, swap(): return lax.ppermute(x, 'ctx', [(i, i ^ mask) for i in range(owners)])  17.6 us
    pallas_call x1, Pallas kernels, body(): call(functools.partial(near_kernel, parts, levels, heads, stack, scale),...  2.77 us
    ppermute x11, waiting for transfers between devices, swap(): return lax.ppermute(x, 'ctx', [(i, i ^ mask) for i in range(owners)])  2.45 us
    pallas_call x1, Pallas kernels, body(): call(functools.partial(far_kernel, parts, levels, heads, stack, scale), '...  2.45 us
    pallas_call x1, Pallas kernels, body(): call(functools.partial(own_kernel, heads), 'own', 1000000000, [full((cand...  1.99 us
    pallas_call x1, Pallas kernels, body(): call(functools.partial(prepare_kernel, levels, heads, parts), 'prepare',...  1.38 us
    ppermute x1, waiting for transfers between devices, body(): other = lax.ppermute(send, 'head', [(0, 1), (1, 0)])  1.1 us
    concatenate x1, other arithmetic, body(): jnp.concatenate([sem_tokens.T, cand_request.T, jnp.zeros((ROWS - levels -...  0.77 us
  transfers between devices with their start and end apart: 12, of which 5 were waited for; matrix products, arithmetic and copies ran while one was open for 0% of the time, Pallas kernels for 20%

profile of v8, /device:TPU:0, one launch (start us, length us, event | category | flops | bytes accessed | tf_op | source)
XLA Modules:
  0.0 32.6 jit_solution(7501903572423693868)
XLA Ops:
  0.1 0.8 %add_add_fusion.cand_ref = s32[8,128]{1,0:T(8,128)S(1)} fusion(s32[1,128]{1,0:T(1,128)} %bitcast.18, s32[4,128]{1,0:T(4,128)} %bitcast.17, s32[8]{0:T(128)S(1)} %pad.6.clone), kind=kLoop, calls=%fused_computation.2 | loop fusion | flops 2048 | bytes 6688 | tf_op jit(solution)/shard_map/concatenate | solution.py:297
  0.9 4.0 %collective-permute-start.2 = (s32[8,128]{1,0:T(8,128)S(1)}, s32[8,128]{1,0:T(8,128)S(1)}, u32[]{:S(2)}, u32[]{:S(2)}) collective-permute-start(s32[8,128]{1,0:T(8,128)S(1)} %payload.1.cand_ref), channel_id=1, source_target_pairs={{0,6},{2,4},{4,2},{6,0},{8,14},{10,12},{12,10},{14,8},{1,7},{3,5},... | collective-permute-start | bytes 12296 | tf_op jit(solution)/shard_map/ppermute | solution.py:283
  4.9 0.4 %collective-permute-start.1 = (s32[8,128]{1,0:T(8,128)S(1)}, s32[8,128]{1,0:T(8,128)S(1)}, u32[]{:S(2)}, u32[]{:S(2)}) collective-permute-start(s32[8,128]{1,0:T(8,128)S(1)} %payload.1.cand_ref), channel_id=1, source_target_pairs={{0,4},{2,6},{4,0},{6,2},{8,12},{10,14},{12,8},{14,10},{1,5},{3,7},... | collective-permute-start | bytes 12296 | tf_op jit(solution)/shard_map/ppermute | solution.py:283
  5.4 0.2 collective-permute-start
  5.7 1.4 %prepare.1 = (bf16[128,1024]{1,0:T(8,128)(2,1)S(1)}, f32[128,512]{1,0:T(8,128)S(1)}, bf16[128,384]{1,0:T(8,128)(2,1)S(1)}, f32[128,128]{1,0:T(8,128)S(1)}, f32[8...) custom-call(s32[2]{0:T(128)S(1)} %pad_add_fusion.1.me_ref, s32[8]{0:T(128)S(1)} %copy-done.7, ...), custom_call_target="tpu_custom_call" | custom-call | flops 8000000000 | bytes 1048576 | tf_op jit(solution)/shard_map/prepare/pallas_call | solution.py:303
  7.1 1.4 %collective-permute-done.1 = s32[8,128]{1,0:T(8,128)S(1)} collective-permute-done((s32[8,128]{1,0:T(8,128)S(1)}, s32[8,128]{1,0:T(8,128)S(1)}, u32[]{:S(2)}, u32[]{:S(2)}) %collective-permute-start.1) | collective-permute-done | bytes 4128 | tf_op jit(solution)/shard_map/ppermute | solution.py:283
  8.5 0.4 %collective-permute-done = s32[8,128]{1,0:T(8,128)S(1)} collective-permute-done((s32[8,128]{1,0:T(8,128)S(1)}, s32[8,128]{1,0:T(8,128)S(1)}, u32[]{:S(2)}, u32[]{:S(2)}) %collective-permute-start) | collective-permute-done | bytes 4128 | tf_op jit(solution)/shard_map/ppermute | solution.py:283
  9.0 2.6 %collective-permute-start.3 = (s32[4,8,128]{2,1,0:T(8,128)S(1)}, s32[4,8,128]{2,1,0:T(8,128)S(1)}, u32[]{:S(2)}, u32[]{:S(2)}) collective-permute-start(s32[4,8,128]{2,1,0:T(8,128)S(1)} %pad_add_fusion.cand_ref), channel_id=1, source_target_pairs={{0,8},{2,10},{4,12},{6,14},{8,0},{10,2},{12,4},{14,6},{1,9},{3,11}... | collective-permute-start | bytes 49160 | tf_op jit(solution)/shard_map/ppermute | solution.py:283
  11.6 2.8 %near.1 = (bf16[48,512]{1,0:T(8,128)(2,1)S(1)}, bf16[48,512]{1,0:T(8,128)(2,1)S(1)}, bf16[48,512]{1,0:T(8,128)(2,1)S(1)}, bf16[48,512]{1,0:T(8,128)(2,1)S(1)}, bf16[1024,512]{1,0:T(8,128)(2,1)S(1)}) custom-call(s32[8,128]{1,0:T(8,128)S(1)} %get-tuple-element.35.target_ref, s32[4,8,128]{2,1,0:T(8,128)S(1)} %pad_add_fusion.cand_ref, ...), custom_call_target="tpu_custom_call" | custom-call | flops 1000000000 | bytes 1048576 | tf_op jit(solution)/shard_map/near/pallas_call | solution.py:326
  14.4 2.4 %far.1 = (bf16[48,512]{1,0:T(8,128)(2,1)S(1)}, bf16[48,512]{1,0:T(8,128)(2,1)S(1)}, bf16[48,512]{1,0:T(8,128)(2,1)S(1)}, bf16[48,512]{1,0:T(8,128)(2,1)S(1)}) custom-call(s32[8,128]{1,0:T(8,128)S(1)} %get-tuple-element.35.target_ref, s32[4,8,128]{2,1,0:T(8,128)S(1)} %collective-permute-done.3.cand_ref, bf16[1024,1024]{1,0:T(8,128)(2,1)S(1)} %copy-done.1, ...), custom_call_target="tpu_custom_call" | custom-call | flops 3000000000 | bytes 1048576 | tf_op jit(solution)/shard_map/far/pallas_call | solution.py:334
  16.8 1.9 %collective-permute-start.4 = (bf16[48,512]{1,0:T(8,128)(2,1)S(1)}, bf16[48,512]{1,0:T(8,128)(2,1)S(1)}, u32[]{:S(2)}, u32[]{:S(2)}) collective-permute-start(bf16[48,512]{1,0:T(8,128)(2,1)S(1)} %get-tuple-element.54), channel_id=1, source_target_pairs={{0,8},{2,10},{4,12},{6,14},{8,0},{10,2},{12,4},{14,6},{1,9},{3,11}... | collective-permute-start | bytes 147464 | tf_op jit(solution)/shard_map/ppermute | solution.py:283
  18.7 2.1 %collective-permute-start.5 = (bf16[48,512]{1,0:T(8,128)(2,1)S(1)}, bf16[48,512]{1,0:T(8,128)(2,1)S(1)}, u32[]{:S(2)}, u32[]{:S(2)}) collective-permute-start(bf16[48,512]{1,0:T(8,128)(2,1)S(1)} %get-tuple-element.55), channel_id=1, source_target_pairs={{0,12},{2,14},{4,8},{6,10},{8,4},{10,6},{12,0},{14,2},{1,13},{3,15... | collective-permute-start | bytes 147464 | tf_op jit(solution)/shard_map/ppermute | solution.py:283
  20.8 0.9 %collective-permute-start.6 = (bf16[48,512]{1,0:T(8,128)(2,1)S(1)}, bf16[48,512]{1,0:T(8,128)(2,1)S(1)}, u32[]{:S(2)}, u32[]{:S(2)}) collective-permute-start(bf16[48,512]{1,0:T(8,128)(2,1)S(1)} %get-tuple-element.56), channel_id=1, source_target_pairs={{0,10},{2,8},{4,14},{6,12},{8,2},{10,0},{12,6},{14,4},{1,11},{3,9}... | collective-permute-start | bytes 147464 | tf_op jit(solution)/shard_map/ppermute | solution.py:283
  21.8 1.9 %collective-permute-start.7 = (bf16[48,512]{1,0:T(8,128)(2,1)S(1)}, bf16[48,512]{1,0:T(8,128)(2,1)S(1)}, u32[]{:S(2)}, u32[]{:S(2)}) collective-permute-start(bf16[48,512]{1,0:T(8,128)(2,1)S(1)} %get-tuple-element.57), channel_id=1, source_target_pairs={{0,14},{2,12},{4,10},{6,8},{8,6},{10,4},{12,2},{14,0},{1,15},{3,13... | collective-permute-start | bytes 147464 | tf_op jit(solution)/shard_map/ppermute | solution.py:283
  23.6 1.5 %collective-permute-start.8 = (bf16[48,512]{1,0:T(8,128)(2,1)S(1)}, bf16[48,512]{1,0:T(8,128)(2,1)S(1)}, u32[]{:S(2)}, u32[]{:S(2)}) collective-permute-start(bf16[48,512]{1,0:T(8,128)(2,1)S(1)} %get-tuple-element.58), channel_id=1, source_target_pairs={{0,6},{2,4},{4,2},{6,0},{8,14},{10,12},{12,10},{14,8},{1,7},{3,5},... | collective-permute-start | bytes 147464 | tf_op jit(solution)/shard_map/ppermute | solution.py:283
  25.2 0.4 %collective-permute-start.9 = (bf16[48,512]{1,0:T(8,128)(2,1)S(1)}, bf16[48,512]{1,0:T(8,128)(2,1)S(1)}, u32[]{:S(2)}, u32[]{:S(2)}) collective-permute-start(bf16[48,512]{1,0:T(8,128)(2,1)S(1)} %get-tuple-element.59), channel_id=1, source_target_pairs={{0,4},{2,6},{4,0},{6,2},{8,12},{10,14},{12,8},{14,10},{1,5},{3,7},... | collective-permute-start | bytes 147464 | tf_op jit(solution)/shard_map/ppermute | solution.py:283
  25.6 1.5 %collective-permute-start.10 = (bf16[48,512]{1,0:T(8,128)(2,1)S(1)}, bf16[48,512]{1,0:T(8,128)(2,1)S(1)}, u32[]{:S(2)}, u32[]{:S(2)}) collective-permute-start(bf16[48,512]{1,0:T(8,128)(2,1)S(1)} %get-tuple-element.60), channel_id=1, source_target_pairs={{0,2},{2,0},{4,6},{6,4},{8,10},{10,8},{12,14},{14,12},{1,3},{3,1},... | collective-permute-start | bytes 147464 | tf_op jit(solution)/shard_map/ppermute | solution.py:283
  27.1 2.0 %own.1 = (f32[128,512]{1,0:T(8,128)S(1)}, f32[128,512]{1,0:T(8,128)S(1)}, bf16[512,512]{1,0:T(8,128)(2,1)S(1)}, bf16[512,512]{1,0:T(8,128)(2,1)S(1)}) custom-call(s32[8,128]{1,0:T(8,128)S(1)} %get-tuple-element.35.target_ref, bf16[48,512]{1,0:T(8,128)(2,1)S(1)} %get-tuple-element.47.sent_ref.rest_7_, f32[8,128]{1,0:T(8,128)S(1)} %bitcast.12, ...), custom_call_target="tpu_custom_call" | custom-call | flops 1000000000 | bytes 1048576 | tf_op jit(solution)/shard_map/own/pallas_call | solution.py:343
  29.2 0.1 collective-permute-done.9.rest_5_
  29.3 0.5 %collective-permute-done.10.rest_6_ = bf16[48,512]{1,0:T(8,128)(2,1)S(1)} collective-permute-done((bf16[48,512]{1,0:T(8,128)(2,1)S(1)}, bf16[48,512]{1,0:T(8,128)(2,1)S(1)}, u32[]{:S(2)}, u32[]{:S(2)}) %collective-permute-start.10) | collective-permute-done | bytes 49184 | tf_op jit(solution)/shard_map/ppermute | solution.py:283
  29.7 0.8 %mix.1 = (bf16[128,512]{1,0:T(8,128)(2,1)S(1)}, bf16[128,512]{1,0:T(8,128)(2,1)S(1)}) custom-call(f32[128,512]{1,0:T(8,128)S(1)} %get-tuple-element.49.gate_ref, f32[128,512]{1,0:T(8,128)S(1)} %get-tuple-element.50.self_ref, bf16[128,384]{1,0:T(8,128)(2,1)S(1)} %get-tuple-element.51.assign_ref, f32[128,128]{1,0:T(8,128)S(1)} %get-tuple-element.52.scale_ref, ...), custom_call_target="tpu_custom_call" | custom-call | flops 1000000000 | bytes 1048576 | tf_op jit(solution)/shard_map/mix/pallas_call | solution.py:352
  30.6 0.2 keep.1
  30.8 1.1 %collective-permute-done.11 = bf16[128,512]{1,0:T(8,128)(2,1)S(1)} collective-permute-done((bf16[128,512]{1,0:T(8,128)(2,1)S(1)}, bf16[128,512]{1,0:T(8,128)(2,1)S(1)}, u32[]{:S(2)}, u32[]{:S(2)}) %collective-permute-start.11) | collective-permute-done | bytes 131104 | tf_op jit(solution)/shard_map/ppermute | solution.py:359
  31.9 0.7 %add_convert_fusion = bf16[128,512]{1,0:T(8,128)(2,1)} fusion(f32[128,512]{1,0:T(8,128)S(1)} %keep.1, bf16[128,512]{1,0:T(8,128)(2,1)S(1)} %collective-permute-done.11), kind=kLoop, calls=%fused_computation | loop fusion | flops 196608 | bytes 524288 | tf_op jit(solution)/shard_map/convert_element_type | solution.py:363
  (29 shorter events, 0.3 us)
Async XLA Ops:
  0.8 4.8 %copy-start.1 = (bf16[1024,1024]{1,0:T(8,128)(2,1)S(1)}, bf16[1024,1024]{1,0:T(8,128)(2,1)}, u32[]{:S(2)}) copy-start(bf16[1024,1024]{1,0:T(8,128)(2,1)} %table_ref.5) | copy-start | bytes 6291460
  0.8 4.8 %copy-start.5 = (f32[128,8]{0,1:T(8,128)S(1)}, f32[128,8]{0,1:T(8,128)}, u32[]{:S(2)}) copy-start(f32[128,8]{0,1:T(8,128)} %param.18) | copy-start | bytes 12292
  0.9 4.8 %copy-start.6 = (s32[1024]{0:T(1024)S(1)}, s32[1024]{0:T(1024)}, u32[]{:S(2)}) copy-start(s32[1024]{0:T(1024)} %param.13) | copy-start | bytes 12292
  0.9 4.8 %copy-start.7 = (s32[8]{0:T(128)S(1)}, s32[8]{0:T(128)}, u32[]{:S(2)}) copy-start(s32[8]{0:T(128)} %lens_ref.1) | copy-start | bytes 100
  0.9 6.2 %collective-permute-start.2 = (s32[8,128]{1,0:T(8,128)S(1)}, s32[8,128]{1,0:T(8,128)S(1)}, u32[]{:S(2)}, u32[]{:S(2)}) collective-permute-start(s32[8,128]{1,0:T(8,128)S(1)} %payload.1.cand_ref), channel_id=1, source_target_pairs={{0,6},{2,4},{4,2},{6,0},{8,14},{10,12},{12,10},{14,8},{1,7},{3,5},... | collective-permute-start | bytes 12296 | tf_op jit(solution)/shard_map/ppermute | solution.py:283
  4.9 3.6 %collective-permute-start.1 = (s32[8,128]{1,0:T(8,128)S(1)}, s32[8,128]{1,0:T(8,128)S(1)}, u32[]{:S(2)}, u32[]{:S(2)}) collective-permute-start(s32[8,128]{1,0:T(8,128)S(1)} %payload.1.cand_ref), channel_id=1, source_target_pairs={{0,4},{2,6},{4,0},{6,2},{8,12},{10,14},{12,8},{14,10},{1,5},{3,7},... | collective-permute-start | bytes 12296 | tf_op jit(solution)/shard_map/ppermute | solution.py:283
  5.4 3.6 %collective-permute-start = (s32[8,128]{1,0:T(8,128)S(1)}, s32[8,128]{1,0:T(8,128)S(1)}, u32[]{:S(2)}, u32[]{:S(2)}) collective-permute-start(s32[8,128]{1,0:T(8,128)S(1)} %payload.1.cand_ref), channel_id=1, source_target_pairs={{0,2},{2,0},{4,6},{6,4},{8,10},{10,8},{12,14},{14,12},{1,3},{3,1},... | collective-permute-start | bytes 12296 | tf_op jit(solution)/shard_map/ppermute | solution.py:283
  5.6 5.9 %copy-start = (bf16[1024,4,512]{2,1,0:T(4,128)(2,1)S(1)}, bf16[1024,4,512]{2,1,0:T(4,128)(2,1)}, u32[]{:S(2)}) copy-start(bf16[1024,4,512]{2,1,0:T(4,128)(2,1)} %win_ref.3) | copy-start | bytes 12582916
  5.7 5.9 %copy-start.3 = (bf16[1024,512]{1,0:T(8,128)(2,1)S(1)}, bf16[1024,512]{1,0:T(8,128)(2,1)}, u32[]{:S(2)}) copy-start(bf16[1024,512]{1,0:T(8,128)(2,1)} %key_ref.3) | copy-start | bytes 3145732
  5.7 5.9 %copy-start.4 = (bf16[1024,512]{1,0:T(8,128)(2,1)S(1)}, bf16[1024,512]{1,0:T(8,128)(2,1)}, u32[]{:S(2)}) copy-start(bf16[1024,512]{1,0:T(8,128)(2,1)} %value_ref.3) | copy-start | bytes 3145732
  9.0 5.4 %collective-permute-start.3 = (s32[4,8,128]{2,1,0:T(8,128)S(1)}, s32[4,8,128]{2,1,0:T(8,128)S(1)}, u32[]{:S(2)}, u32[]{:S(2)}) collective-permute-start(s32[4,8,128]{2,1,0:T(8,128)S(1)} %pad_add_fusion.cand_ref), channel_id=1, source_target_pairs={{0,8},{2,10},{4,12},{6,14},{8,0},{10,2},{12,4},{14,6},{1,9},{3,11}... | collective-permute-start | bytes 49160 | tf_op jit(solution)/shard_map/ppermute | solution.py:283
  14.4 12.8 %copy-start.2 = (bf16[512,1024]{1,0:T(8,128)(2,1)S(1)}, bf16[512,1024]{1,0:T(8,128)(2,1)}, u32[]{:S(2)}) copy-start(bf16[512,1024]{1,0:T(8,128)(2,1)} %wout_ref.1) | copy-start | bytes 3145732
  16.8 8.3 %collective-permute-start.4 = (bf16[48,512]{1,0:T(8,128)(2,1)S(1)}, bf16[48,512]{1,0:T(8,128)(2,1)S(1)}, u32[]{:S(2)}, u32[]{:S(2)}) collective-permute-start(bf16[48,512]{1,0:T(8,128)(2,1)S(1)} %get-tuple-element.54), channel_id=1, source_target_pairs={{0,8},{2,10},{4,12},{6,14},{8,0},{10,2},{12,4},{14,6},{1,9},{3,11}... | collective-permute-start | bytes 147464 | tf_op jit(solution)/shard_map/ppermute | solution.py:283
  18.7 6.9 %collective-permute-start.5 = (bf16[48,512]{1,0:T(8,128)(2,1)S(1)}, bf16[48,512]{1,0:T(8,128)(2,1)S(1)}, u32[]{:S(2)}, u32[]{:S(2)}) collective-permute-start(bf16[48,512]{1,0:T(8,128)(2,1)S(1)} %get-tuple-element.55), channel_id=1, source_target_pairs={{0,12},{2,14},{4,8},{6,10},{8,4},{10,6},{12,0},{14,2},{1,13},{3,15... | collective-permute-start | bytes 147464 | tf_op jit(solution)/shard_map/ppermute | solution.py:283
  20.8 8.3 %collective-permute-start.6 = (bf16[48,512]{1,0:T(8,128)(2,1)S(1)}, bf16[48,512]{1,0:T(8,128)(2,1)S(1)}, u32[]{:S(2)}, u32[]{:S(2)}) collective-permute-start(bf16[48,512]{1,0:T(8,128)(2,1)S(1)} %get-tuple-element.56), channel_id=1, source_target_pairs={{0,10},{2,8},{4,14},{6,12},{8,2},{10,0},{12,6},{14,4},{1,11},{3,9}... | collective-permute-start | bytes 147464 | tf_op jit(solution)/shard_map/ppermute | solution.py:283
  21.8 7.4 %collective-permute-start.7 = (bf16[48,512]{1,0:T(8,128)(2,1)S(1)}, bf16[48,512]{1,0:T(8,128)(2,1)S(1)}, u32[]{:S(2)}, u32[]{:S(2)}) collective-permute-start(bf16[48,512]{1,0:T(8,128)(2,1)S(1)} %get-tuple-element.57), channel_id=1, source_target_pairs={{0,14},{2,12},{4,10},{6,8},{8,6},{10,4},{12,2},{14,0},{1,15},{3,13... | collective-permute-start | bytes 147464 | tf_op jit(solution)/shard_map/ppermute | solution.py:283
  23.6 5.5 %collective-permute-start.8 = (bf16[48,512]{1,0:T(8,128)(2,1)S(1)}, bf16[48,512]{1,0:T(8,128)(2,1)S(1)}, u32[]{:S(2)}, u32[]{:S(2)}) collective-permute-start(bf16[48,512]{1,0:T(8,128)(2,1)S(1)} %get-tuple-element.58), channel_id=1, source_target_pairs={{0,6},{2,4},{4,2},{6,0},{8,14},{10,12},{12,10},{14,8},{1,7},{3,5},... | collective-permute-start | bytes 147464 | tf_op jit(solution)/shard_map/ppermute | solution.py:283
  25.2 4.1 %collective-permute-start.9 = (bf16[48,512]{1,0:T(8,128)(2,1)S(1)}, bf16[48,512]{1,0:T(8,128)(2,1)S(1)}, u32[]{:S(2)}, u32[]{:S(2)}) collective-permute-start(bf16[48,512]{1,0:T(8,128)(2,1)S(1)} %get-tuple-element.59), channel_id=1, source_target_pairs={{0,4},{2,6},{4,0},{6,2},{8,12},{10,14},{12,8},{14,10},{1,5},{3,7},... | collective-permute-start | bytes 147464 | tf_op jit(solution)/shard_map/ppermute | solution.py:283
  25.6 4.1 %collective-permute-start.10 = (bf16[48,512]{1,0:T(8,128)(2,1)S(1)}, bf16[48,512]{1,0:T(8,128)(2,1)S(1)}, u32[]{:S(2)}, u32[]{:S(2)}) collective-permute-start(bf16[48,512]{1,0:T(8,128)(2,1)S(1)} %get-tuple-element.60), channel_id=1, source_target_pairs={{0,2},{2,0},{4,6},{6,4},{8,10},{10,8},{12,14},{14,12},{1,3},{3,1},... | collective-permute-start | bytes 147464 | tf_op jit(solution)/shard_map/ppermute | solution.py:283
  30.5 1.4 %collective-permute-start.11 = (bf16[128,512]{1,0:T(8,128)(2,1)S(1)}, bf16[128,512]{1,0:T(8,128)(2,1)S(1)}, u32[]{:S(2)}, u32[]{:S(2)}) collective-permute-start(bf16[128,512]{1,0:T(8,128)(2,1)S(1)} %get-tuple-element.64), channel_id=1, source_target_pairs={{0,1},{1,0},{2,3},{3,2},{4,5},{5,4},{6,7},{7,6},{8,9},{9,8},{10,11... | collective-permute-start | bytes 393224 | tf_op jit(solution)/shard_map/ppermute | solution.py:359
